TPU v7x, 256 devices: a whole 4x4x8 slice. The times are simulated.
256 devices in a mesh: kz: 16 (over z, x_lo), en: 16 (over x_hi, y, core).
Axes of the slice: x: 4 (x_hi: 2, x_lo: 2; x = x_hi * 2 + x_lo), y: 4, z: 8, core: 2. Of those that a mesh axis runs over, the one named last changes fastest.
Arguments:
- green_real: bfloat16 [16, 384, 128, 128], P('kz', 'en'), may hold values from -6 to 6
- green_imag: bfloat16 [16, 384, 128, 128], P('kz', 'en'), may hold values from -6 to 6
- coupling: bfloat16 [2, 4, 16, 128, 128], P(None, None, 'kz'), may hold values from -0.5 to 0.5
- strengths: float32 [2, 4, 8], replicated, may hold values from 0.1 to 1
- offsets: int32 [2, 8], replicated, may hold values from -4 to 4, as said below
Outputs:
- dressed_real: bfloat16 [16, 384, 128, 128], P('kz', 'en')
- dressed_imag: bfloat16 [16, 384, 128, 128], P('kz', 'en')
Inputs may be any that keep to these rules, and one draw needn't show every extreme that they name: Each row of offsets holds each of -4 to -1 and 1 to 4 exactly once.
All inputs are finite; a program needn't handle non-finite values.
Results may differ from a plain program's by a relative error of at most 0.007.
Values may be sent and summed in bfloat16 or wider, within the bound.
No kernel may reach another device: no remote copies, remote signals or barrier semaphores. Data moves between devices by JAX's collectives and lax.ppermute only.
A program may use at most 128 MiB of HBM per device.

v0:
```python
import jax
import jax.numpy as jnp
from jax import lax
from jax.sharding import PartitionSpec as P

REACH = 4
HOPS = 2
BRANCHES = 4


def shifted(block, axis, distance):
    devices = range(lax.axis_size(axis))
    route = [((i - distance) % len(devices), i) for i in devices]
    return lax.ppermute(block, axis, route)


def with_halo(cells, sides, width):
    for axis, dim in sides:
        count = lax.axis_size(axis)
        ends = count - 1
        head = lax.slice_in_dim(cells, 0, width, axis=dim)
        tail = lax.slice_in_dim(cells, cells.shape[dim] - width, cells.shape[dim], axis=dim)
        cells = jnp.concatenate(
            [
                lax.ppermute(tail, axis, [(i, (i + 1) % count) for i in range(ends)]),
                cells,
                lax.ppermute(head, axis, [((i + 1) % count, i) for i in range(ends)]),
            ],
            axis=dim,
        )
    return cells


def mixing(strengths, offsets):
    levels = jnp.arange(-REACH, REACH + 1)
    match_table = (offsets[:, None, :, None] == levels[None, None, None, :]).astype(jnp.float32)
    return jnp.sum(strengths[:, :, :, None] * match_table, axis=2)


def matmul_batch(first_term, second_term):
    return jnp.einsum("eab,ebc->eac", first_term, second_term, preferred_element_type=jnp.float32)


def shards(green_real, green_imag, coupling, strengths, offsets):
    energies = green_real.shape[1]
    orbitals = green_real.shape[2]
    stacked = jnp.stack([green_real[0], green_imag[0]])
    near_block = shifted(stacked, "kz", 1)
    far_block = shifted(near_block, "kz", 1)
    edged_pair = with_halo(jnp.stack([near_block, far_block]), (("en", 2),), REACH)
    extended = [edged_pair[0], edged_pair[1]]
    weights_table = mixing(strengths, offsets)
    self_energy = jnp.zeros((2, energies, orbitals, orbitals), jnp.float32)
    for hop_index in range(HOPS):
        edged_block = extended[hop_index]
        for branch_index in range(BRANCHES):
            summed_block = jnp.zeros((2, energies, orbitals, orbitals), jnp.float32)
            for step_index in range(2 * REACH + 1):
                energy_shift = step_index - REACH
                if energy_shift == 0:
                    continue
                window = edged_block[:, REACH - energy_shift : REACH - energy_shift + energies]
                summed_block = summed_block + weights_table[
                    hop_index, branch_index, step_index
                ] * window.astype(jnp.float32)
            summed_block = summed_block.astype(jnp.bfloat16)
            matrix = coupling[hop_index, branch_index, 0]
            left_prod = jnp.einsum(
                "ab,xebc->xeac", matrix, summed_block, preferred_element_type=jnp.float32
            ).astype(jnp.bfloat16)
            self_energy = self_energy + jnp.einsum(
                "xeab,cb->xeac", left_prod, matrix, preferred_element_type=jnp.float32
            )
    self_energy = self_energy.astype(jnp.bfloat16)
    real_part = green_real[0]
    imag_part = green_imag[0]
    self_real = self_energy[0]
    self_imag = self_energy[1]
    prod_real = (matmul_batch(real_part, self_real) - matmul_batch(imag_part, self_imag)).astype(
        jnp.bfloat16
    )
    prod_imag = (matmul_batch(real_part, self_imag) + matmul_batch(imag_part, self_real)).astype(
        jnp.bfloat16
    )
    back_real = matmul_batch(prod_real, real_part) - matmul_batch(prod_imag, imag_part)
    back_imag = matmul_batch(prod_real, imag_part) + matmul_batch(prod_imag, real_part)
    dressed_real = (real_part.astype(jnp.float32) + back_real / orbitals).astype(jnp.bfloat16)
    dressed_imag = (imag_part.astype(jnp.float32) + back_imag / orbitals).astype(jnp.bfloat16)
    return (dressed_real[None], dressed_imag[None])


def solution(mesh):
    in_specs = (
        P("kz", "en", None, None),
        P("kz", "en", None, None),
        P(None, None, "kz", None, None),
        P(),
        P(),
    )
    out_specs = (P("kz", "en", None, None), P("kz", "en", None, None))
    return jax.shard_map(shards, mesh=mesh, in_specs=in_specs, out_specs=out_specs, check_vma=False)
```

profile of v0, /device:TPU:4, one launch (start us, length us, event | category | flops | bytes accessed | tf_op | source)
XLA Modules:
  0.0 208.1 jit_solution(16680610046193617033)
XLA Ops:
  0.6 1.5 pad_maximum_fusion.1
  2.2 1.3 collective-permute-start
  3.5 39.7 %collective-permute-done = bf16[2,24,128,128]{3,2,1,0:T(8,128)(2,1)S(1)} collective-permute-done((bf16[2,24,128,128]{3,2,1,0:T(8,128)(2,1)S(1)}, bf16[2,24,128,128]{3,2,1,0:T(8,128)(2,1)S(1)}, u32[]{:S(2)}, u32[]{:S(2)}) %collective-permute-start) | collective-permute-done | bytes 1572896 | tf_op jit(solution)/shard_map/ppermute | solution.py:14
  43.2 37.6 %collective-permute-done.1 = bf16[2,24,128,128]{3,2,1,0:T(8,128)(2,1)S(1)} collective-permute-done((bf16[2,24,128,128]{3,2,1,0:T(8,128)(2,1)S(1)}, bf16[2,24,128,128]{3,2,1,0:T(8,128)(2,1)S(1)}, u32[]{:S(2)}, u32[]{:S(2)}) %collective-permute-start.1) | collective-permute-done | bytes 1572896 | tf_op jit(solution)/shard_map/ppermute | solution.py:14
  80.9 1.9 collective-permute-start.2
  82.9 7.3 %collective-permute-start.3 = (bf16[2,2,4,128,128]{4,3,2,1,0:T(8,128)(2,1)S(1)}, bf16[2,2,4,128,128]{4,3,2,1,0:T(8,128)(2,1)S(1)}, u32[]{:S(2)}, u32[]{:S(2)}) collective-permute-start(bf16[2,2,4,128,128]{4,3,2,1,0:T(8,128)(2,1)S(1)} %get-tuple-element.5), channel_id=1, source_target_pairs={{1,0},{2,1},{3,2},{4,3},{5,4},{6,5},{7,6},{8,7},{9,8},{10,9},{11,1... | collective-permute-start | bytes 1572872 | tf_op jit(solution)/shard_map/ppermute | solution.py:27
  90.9 0.7 fusion.306
  91.6 0.7 fusion.305
  92.3 0.7 fusion.304
  93.1 2.0 collective-permute-done.2
  95.0 1.8 collective-permute-done.3
  97.5 1.8 slice_bitcast_fusion.1
  99.2 13.8 %fusion.77 = f32[2,24,128,128]{3,2,1,0:T(8,128)} fusion(f32[]{:T(128)} %bitcast.11, f32[]{:T(128)} %bitcast.10, f32[]{:T(128)} %bitcast.9, f32[]{:T(128)} %bitcast.8, f32[]{:T(128)} %bitcast.7, f32[]{:T(128)} %bitcast.6, f32[]{:T(128)} %bitcast.5, f32[]{:T(128)} %bitcast.1, bf16[2,32,128,128]{3,2,1,0:T(8,128)(2,1)} %get-tuple-element.2, ...), kind=kOutput, calls=%fused_computation.154 | convolution fusion | flops 422313984 | bytes 15798272 | tf_op jit(solution)/shard_map/xeab,cb->xeac/dot_general | solution.py:71
  113.0 13.7 %fusion.71 = f32[2,24,128,128]{3,2,1,0:T(8,128)} fusion(f32[]{:T(128)} %bitcast.47, f32[]{:T(128)} %bitcast.46, f32[]{:T(128)} %bitcast.45, f32[]{:T(128)} %bitcast.44, f32[]{:T(128)} %bitcast.43, f32[]{:T(128)} %bitcast.42, f32[]{:T(128)} %bitcast.41, f32[]{:T(128)} %bitcast.40, bf16[2,32,128,128]{3,2,1,0:T(8,128)(2,1)} %get-tuple-element.2, ...), kind=kOutput, calls=%fused_computation.148 | convolution fusion | flops 422313984 | bytes 15798272 | tf_op jit(solution)/shard_map/xeab,cb->xeac/dot_general | solution.py:71
  126.7 13.8 %fusion.73 = f32[2,24,128,128]{3,2,1,0:T(8,128)} fusion(f32[]{:T(128)} %bitcast.35, f32[]{:T(128)} %bitcast.34, f32[]{:T(128)} %bitcast.33, f32[]{:T(128)} %bitcast.32, f32[]{:T(128)} %bitcast.31, f32[]{:T(128)} %bitcast.30, f32[]{:T(128)} %bitcast.29, f32[]{:T(128)} %bitcast.28, bf16[2,32,128,128]{3,2,1,0:T(8,128)(2,1)} %get-tuple-element.2, ...), kind=kOutput, calls=%fused_computation.150 | convolution fusion | flops 422313984 | bytes 15798272 | tf_op jit(solution)/shard_map/xeab,cb->xeac/dot_general | solution.py:71
  140.5 13.9 %fusion.75 = f32[2,24,128,128]{3,2,1,0:T(8,128)} fusion(f32[]{:T(128)} %bitcast.23, f32[]{:T(128)} %bitcast.22, f32[]{:T(128)} %bitcast.21, f32[]{:T(128)} %bitcast.20, f32[]{:T(128)} %bitcast.19, f32[]{:T(128)} %bitcast.18, f32[]{:T(128)} %bitcast.17, f32[]{:T(128)} %bitcast.16, bf16[2,32,128,128]{3,2,1,0:T(8,128)(2,1)} %get-tuple-element.2, ...), kind=kOutput, calls=%fused_computation.152 | convolution fusion | flops 422313984 | bytes 15798272 | tf_op jit(solution)/shard_map/xeab,cb->xeac/dot_general | solution.py:71
  154.4 9.2 %fusion.69 = f32[2,24,128,128]{3,2,1,0:T(8,128)} fusion(f32[]{:T(128)} %bitcast.60, f32[]{:T(128)} %bitcast.59, f32[]{:T(128)} %bitcast.58, f32[]{:T(128)} %bitcast.57, f32[]{:T(128)} %bitcast.56, f32[]{:T(128)} %bitcast.55, f32[]{:T(128)} %bitcast.54, f32[]{:T(128)} %bitcast.52, bf16[2,32,128,128]{3,2,1,0:T(8,128)(2,1)S(1)} %get-tuple-element.3, ...), kind=kOutput, calls=%fused_computation.146 | convolution fusion | flops 422313984 | bytes 15794208 | tf_op jit(solution)/shard_map/xeab,cb->xeac/dot_general | solution.py:71
  163.6 9.3 %fusion.65 = f32[2,24,128,128]{3,2,1,0:T(8,128)} fusion(f32[]{:T(128)} %bitcast.84, f32[]{:T(128)} %bitcast.83, f32[]{:T(128)} %bitcast.82, f32[]{:T(128)} %bitcast.81, f32[]{:T(128)} %bitcast.80, f32[]{:T(128)} %bitcast.79, f32[]{:T(128)} %bitcast.78, f32[]{:T(128)} %bitcast.77, bf16[2,32,128,128]{3,2,1,0:T(8,128)(2,1)S(1)} %get-tuple-element.3, ...), kind=kOutput, calls=%fused_computation.142 | convolution fusion | flops 422313984 | bytes 15794208 | tf_op jit(solution)/shard_map/xeab,cb->xeac/dot_general | solution.py:71
  172.9 9.5 %fusion.67 = f32[2,24,128,128]{3,2,1,0:T(8,128)} fusion(f32[]{:T(128)} %bitcast.72, f32[]{:T(128)} %bitcast.71, f32[]{:T(128)} %bitcast.70, f32[]{:T(128)} %bitcast.69, f32[]{:T(128)} %bitcast.68, f32[]{:T(128)} %bitcast.67, f32[]{:T(128)} %bitcast.66, f32[]{:T(128)} %bitcast.65, bf16[2,32,128,128]{3,2,1,0:T(8,128)(2,1)S(1)} %get-tuple-element.3, ...), kind=kOutput, calls=%fused_computation.144 | convolution fusion | flops 422313984 | bytes 15794208 | tf_op jit(solution)/shard_map/xeab,cb->xeac/dot_general | solution.py:71
  182.4 19.1 %add_convert_fusion = bf16[2,24,128,128]{3,2,1,0:T(8,128)(2,1)S(1)} fusion(f32[2,24,128,128]{3,2,1,0:T(8,128)} %fusion.65, f32[2,24,128,128]{3,2,1,0:T(8,128)} %fusion.67, f32[2,24,128,128]{3,2,1,0:T(8,128)} %fusion.69, f32[2,24,128,128]{3,2,1,0:T(8,128)} %fusion.71, f32[2,24,128,128]{3,2,1,0:T(8,128)} %fusion.73, f32[2,24,128,128]{3,2,1,0:T(8,128)} %fusion.77, ...), kind=kOutput, calls=%fused_computation.129 | convolution fusion | flops 428605440 | bytes 36245504 | tf_op jit(solution)/shard_map/xeab,cb->xeac/dot_general | solution.py:71
  203.0 0.7 subtract_convert_fusion
  204.5 0.7 add_convert_fusion.3
  205.3 1.4 fusion.131
  206.7 1.4 fusion.130
  (23 shorter events, 3.9 us)
Async XLA Ops:
  0.6 42.5 %copy-start.5 = (s32[2,8]{1,0:T(2,128)S(1)}, s32[2,8]{1,0:T(2,128)}, u32[]{:S(2)}) copy-start(s32[2,8]{1,0:T(2,128)} %param.9) | copy-start | bytes 196
  0.6 89.5 %copy-start.4 = (f32[2,4,8]{2,1,0:T(4,128)S(1)}, f32[2,4,8]{2,1,0:T(4,128)}, u32[]{:S(2)}) copy-start(f32[2,4,8]{2,1,0:T(4,128)} %param.8) | copy-start | bytes 772
  2.2 41.0 %collective-permute-start = (bf16[2,24,128,128]{3,2,1,0:T(8,128)(2,1)S(1)}, bf16[2,24,128,128]{3,2,1,0:T(8,128)(2,1)S(1)}, u32[]{:S(2)}, u32[]{:S(2)}) collective-permute-start(bf16[2,24,128,128]{3,2,1,0:T(8,128)(2,1)S(1)} %pad_maximum_fusion.1), channel_id=1, source_target_pairs={{240,0},{0,16},{16,32},{32,48},{48,64},{64,80},{80,96},{96,112},{1... | collective-permute-start | bytes 4718600 | tf_op jit(solution)/shard_map/ppermute | solution.py:14
  43.1 37.7 %collective-permute-start.1 = (bf16[2,24,128,128]{3,2,1,0:T(8,128)(2,1)S(1)}, bf16[2,24,128,128]{3,2,1,0:T(8,128)(2,1)S(1)}, u32[]{:S(2)}, u32[]{:S(2)}) collective-permute-start(bf16[2,24,128,128]{3,2,1,0:T(8,128)(2,1)S(1)} %collective-permute-done), channel_id=1, source_target_pairs={{240,0},{0,16},{16,32},{32,48},{48,64},{64,80},{80,96},{96,112},{1... | collective-permute-start | bytes 4718600 | tf_op jit(solution)/shard_map/ppermute | solution.py:14
  80.9 14.1 %collective-permute-start.2 = (bf16[2,2,4,128,128]{4,3,2,1,0:T(8,128)(2,1)S(1)}, bf16[2,2,4,128,128]{4,3,2,1,0:T(8,128)(2,1)S(1)}, u32[]{:S(2)}, u32[]{:S(2)}) collective-permute-start(bf16[2,2,4,128,128]{4,3,2,1,0:T(8,128)(2,1)S(1)} %get-tuple-element.4), channel_id=1, source_target_pairs={{0,1},{1,2},{2,3},{3,4},{4,5},{5,6},{6,7},{7,8},{8,9},{9,10},{10,1... | collective-permute-start | bytes 1572872 | tf_op jit(solution)/shard_map/ppermute | solution.py:25
  82.9 13.9 %collective-permute-start.3 = (bf16[2,2,4,128,128]{4,3,2,1,0:T(8,128)(2,1)S(1)}, bf16[2,2,4,128,128]{4,3,2,1,0:T(8,128)(2,1)S(1)}, u32[]{:S(2)}, u32[]{:S(2)}) collective-permute-start(bf16[2,2,4,128,128]{4,3,2,1,0:T(8,128)(2,1)S(1)} %get-tuple-element.5), channel_id=1, source_target_pairs={{1,0},{2,1},{3,2},{4,3},{5,4},{6,5},{7,6},{8,7},{9,8},{10,9},{11,1... | collective-permute-start | bytes 1572872 | tf_op jit(solution)/shard_map/ppermute | solution.py:27
  97.5 1.8 copy-start.3
  99.2 73.7 %copy-start.2 = (bf16[2,32,128,128]{3,2,1,0:T(8,128)(2,1)}, bf16[2,32,128,128]{3,2,1,0:T(8,128)(2,1)S(1)}, u32[]{:S(2)}) copy-start(bf16[2,32,128,128]{3,2,1,0:T(8,128)(2,1)S(1)} %get-tuple-element.3) | copy-start | bytes 6291460
  182.4 19.1 %copy-start = (bf16[1,24,128,128]{3,2,1,0:T(8,128)(2,1)S(1)}, bf16[1,24,128,128]{3,2,1,0:T(8,128)(2,1)}, u32[]{:S(2)}) copy-start(bf16[1,24,128,128]{3,2,1,0:T(8,128)(2,1)} %param.5) | copy-start | bytes 2359300
  201.5 1.4 copy-start.1
where the time goes:
time: 212 us; the launch traced here: 208 us
  matrix products  109 us (51%)
  waiting for transfers between devices  81 us (38%)
  starting transfers between devices  10.5 us (5%)
  local copies, waits for them, and re-layouts  4.62 us (2%)
  other arithmetic  2.44 us (1%)
    dot_general x8, matrix products, shards(): jnp.einsum('xeab,cb->xeac', left_prod, matrix, preferred_element_type=jnp...  102 us
    ppermute x2, waiting for transfers between devices, shifted(): return lax.ppermute(block, axis, route)  77.3 us
    ppermute x1, starting transfers between devices, with_halo(): lax.ppermute(head, axis, [((i + 1) % count, i) for i in range(ends)])  7.26 us
    dot_general x8, matrix products, matmul_batch(): jnp.einsum('eab,ebc->eac', first_term, second_term, preferred_element_typ...  6.51 us
  transfers between devices with their start and end apart: 4, of which 4 were waited for; matrix products, arithmetic and copies ran while one was open for 1% of the time, Pallas kernels for 0%

commit v1 on v0

v1 whole, which is shorter than its diff:
```python
import functools

import jax
import jax.numpy as jnp
from jax import lax
from jax.experimental import pallas as pl
from jax.experimental.pallas import tpu as pltpu
from jax.sharding import PartitionSpec as P

REACH = 4
HOPS = 2
BRANCHES = 4
WINDOW = 2 * REACH
VMEM_LIMIT = 40 * 2**20

F32 = jnp.float32
BF16 = jnp.bfloat16
dot = functools.partial(jnp.dot, preferred_element_type=F32)
WHOLE = pl.BlockSpec(memory_space=pltpu.VMEM)
SCALARS = pl.BlockSpec(memory_space=pltpu.SMEM)
UNTOUCHED = pl.BlockSpec(memory_space=pl.ANY)


def prepare_kernel(offsets_ref, strengths_ref, coupling_ref, weights_ref, joined_ref):
    no = coupling_ref.shape[-1]
    for s in range(HOPS):
        for n in range(BRANCHES):
            matrix = coupling_ref[s, n, 0]
            joined_ref[s, :, n * no : (n + 1) * no] = matrix
            turned = matrix.astype(F32).T
            for i in range(WINDOW):
                w = offsets_ref[s, i]
                j = jnp.where(w > 0, REACH - w, REACH - 1 - w)
                rows = pl.ds(pl.multiple_of(j * no, no), no)
                weights_ref[s, rows, n * no : (n + 1) * no] = (strengths_ref[s, n, i] * turned).astype(BF16)


def prepare(coupling, strengths, offsets):
    no = coupling.shape[-1]
    return pl.pallas_call(
        prepare_kernel,
        out_shape=(
            jax.ShapeDtypeStruct((HOPS, WINDOW * no, BRANCHES * no), BF16),
            jax.ShapeDtypeStruct((HOPS, no, BRANCHES * no), BF16),
        ),
        in_specs=[SCALARS, SCALARS, WHOLE],
        out_specs=(WHOLE, WHOLE),
        compiler_params=pltpu.CompilerParams(vmem_limit_bytes=VMEM_LIMIT),
        cost_estimate=pl.CostEstimate(flops=10**6, bytes_accessed=3 * 10**6, transcendentals=0),
        name="prepare",
    )(offsets, strengths, coupling)


def hop_terms(s, tiles, first, weights_ref, joined_ref):
    no = joined_ref.shape[1]
    energy = lambda t: tiles[first + t // REACH][t % REACH]
    rows = []
    for i in range(REACH):
        rows.append(jnp.concatenate([energy(i + j + (j >= REACH)) for j in range(WINDOW)], axis=1))
    right = dot(jnp.concatenate(rows, axis=0), weights_ref[s]).astype(BF16)
    terms = []
    for i in range(REACH):
        stacked = []
        for n in range(BRANCHES):
            block = right[i * 2 * no : (i + 1) * 2 * no, n * no : (n + 1) * no]
            stacked.append(jnp.concatenate([block[:no], block[no:]], axis=1))
        terms.append(dot(joined_ref[s], jnp.concatenate(stacked, axis=0)))
    return terms


def far_kernel(count, *refs):
    tiles, (weights_ref, joined_ref, out_ref) = refs[: count + 2], refs[count + 2 :]
    for c in range(count):
        for i, term in enumerate(hop_terms(1, tiles, c, weights_ref, joined_ref)):
            out_ref[c * REACH + i] = term


def far_part(tiles, weights, joined):
    count = len(tiles) - 2
    no = joined.shape[1]
    return pl.pallas_call(
        functools.partial(far_kernel, count),
        out_shape=jax.ShapeDtypeStruct((count * REACH, no, 2 * no), F32),
        in_specs=[WHOLE] * (count + 4),
        out_specs=WHOLE,
        compiler_params=pltpu.CompilerParams(vmem_limit_bytes=VMEM_LIMIT),
        cost_estimate=pl.CostEstimate(flops=count * 2 * 10**9, bytes_accessed=2 * 10**6, transcendentals=0),
        name="far_part",
    )(*tiles, weights, joined)


def crossed(real, imag):
    return jnp.concatenate(
        [jnp.concatenate([real, imag], axis=1), jnp.concatenate([-imag, real], axis=1)], axis=0
    )


def near_kernel(count, *refs):
    tiles, refs = refs[: count + 2], refs[count + 2 :]
    weights_ref, joined_ref, real_ref, imag_ref = refs[:4]
    parts, refs = refs[4 : 4 + count], refs[4 + count :]
    out_real_ref, out_imag_ref = refs[-2:]
    no = joined_ref.shape[1]
    for c in range(count):
        for i, term in enumerate(hop_terms(0, tiles, c, weights_ref, joined_ref)):
            e = c * REACH + i
            sigma = (term + parts[c][i]).astype(BF16)
            real, imag = real_ref[0, e], imag_ref[0, e]
            prod = dot(jnp.concatenate([real, imag], axis=1), crossed(sigma[:, :no], sigma[:, no:])).astype(BF16)
            back = dot(prod, crossed(real, imag)) / no
            out_real_ref[0, e] = (real.astype(F32) + back[:, :no]).astype(BF16)
            out_imag_ref[0, e] = (imag.astype(F32) + back[:, no:]).astype(BF16)


def near_part(tiles, weights, joined, green, parts, start, so_far):
    count = len(tiles) - 2
    no = joined.shape[1]
    size = count * REACH
    own = pl.BlockSpec((1, size, no, no), lambda g: (0, start // size, 0, 0))
    shape = jax.ShapeDtypeStruct(green[0].shape, BF16)
    inputs = [*tiles, weights, joined, *green, *parts]
    in_specs = [WHOLE] * (count + 4) + [own] * 2 + [WHOLE] * count
    aliases = {}
    if so_far is not None:
        aliases = {len(inputs): 0, len(inputs) + 1: 1}
        inputs += so_far
        in_specs += [UNTOUCHED] * 2
    return pl.pallas_call(
        functools.partial(near_kernel, count),
        grid=(1,),
        out_shape=(shape, shape),
        in_specs=in_specs,
        out_specs=(own, own),
        input_output_aliases=aliases,
        compiler_params=pltpu.CompilerParams(vmem_limit_bytes=VMEM_LIMIT),
        cost_estimate=pl.CostEstimate(flops=count * 25 * 10**8, bytes_accessed=4 * 10**6, transcendentals=0),
        name="near_part",
    )(*inputs)


def shards(green_real, green_imag, coupling, strengths, offsets):
    energies = green_real.shape[1]
    momenta = lax.axis_size("kz")
    lanes = lax.axis_size("en")
    chunks = energies // REACH
    two_on = [(i, (i + 2) % momenta) for i in range(momenta)]
    swap = [(i, i ^ 1) for i in range(momenta)]
    up = [(i, i + 1) for i in range(lanes - 1)]
    down = [(i + 1, i) for i in range(lanes - 1)]
    even = lax.axis_index("kz") % 2 == 0

    def own_chunk(c):
        cut = slice(c * REACH, (c + 1) * REACH)
        return jnp.concatenate([green_real[0, cut], green_imag[0, cut]], axis=1)

    order = [0, chunks - 1] + list(range(1, chunks - 1))
    own, far, near = {}, {}, {}
    for c in order:
        own[c] = own_chunk(c)
        far[c] = lax.ppermute(own[c], "kz", two_on)
    weights, joined = prepare(coupling, strengths, offsets)
    for c in order:
        near[c] = lax.ppermute(jnp.where(even, own[c], far[c]), "kz", swap)
    last = chunks - 1
    below = lax.ppermute(jnp.stack([near[last], far[last]]), "en", up)
    above = lax.ppermute(jnp.stack([near[0], far[0]]), "en", down)
    near[-1], far[-1] = below[0], below[1]
    near[chunks], far[chunks] = above[0], above[1]

    out = None
    green = (green_real, green_imag)
    groups = [[c] for c in range(chunks // 2)] + [list(range(chunks // 2, chunks))]
    for group in groups:
        around = range(group[0] - 1, group[-1] + 2)
        parts = [far_part([far[n] for n in (c - 1, c, c + 1)], weights, joined) for c in group]
        out = near_part([near[n] for n in around], weights, joined, green, parts, group[0] * REACH, out)
    return tuple(out)


def solution(mesh):
    in_specs = (
        P("kz", "en", None, None),
        P("kz", "en", None, None),
        P(None, None, "kz", None, None),
        P(),
        P(),
    )
    out_specs = (P("kz", "en", None, None), P("kz", "en", None, None))
    return jax.shard_map(shards, mesh=mesh, in_specs=in_specs, out_specs=out_specs, check_vma=False)
```

time: 212 us -> 88.5 us (0.42)
  the two profiles are of different devices: /device:TPU:4 before, /device:TPU:25 now
where the time goes in v1:
time: 88.5 us; the launch traced here: 88.3 us
  waiting for transfers between devices  34 us (38%)
  Pallas kernels  24.6 us (28%)
  starting transfers between devices  23 us (26%)
  other arithmetic  4.14 us (5%)
  local copies, waits for them, and re-layouts  1.65 us (2%)
  between operations  0.91 us (1%)
    ppermute x6, waiting for transfers between devices, shards(): far[c] = lax.ppermute(own[c], 'kz', two_on)  18.3 us
    pallas_call x4, Pallas kernels, near_part(): pl.pallas_call(functools.partial(near_kernel, count), grid=(1,), out_shap...  14.8 us
    ppermute x6, starting transfers between devices, shards(): far[c] = lax.ppermute(own[c], 'kz', two_on)  9.31 us
    ppermute x1, waiting for transfers between devices, shards(): above = lax.ppermute(jnp.stack([near[0], far[0]]), 'en', down)  8.64 us
    pallas_call x6, Pallas kernels, far_part(): pl.pallas_call(functools.partial(far_kernel, count), out_shape=jax.ShapeD...  8.58 us
    ppermute x1, waiting for transfers between devices, shards(): below = lax.ppermute(jnp.stack([near[last], far[last]]), 'en', up)  7.05 us
    ppermute x6, starting transfers between devices, shards(): near[c] = lax.ppermute(jnp.where(even, own[c], far[c]), 'kz', swap)  6.33 us
    ppermute x1, starting transfers between devices, shards(): below = lax.ppermute(jnp.stack([near[last], far[last]]), 'en', up)  5.41 us
  transfers between devices with their start and end apart: 14, of which 7 were waited for; matrix products, arithmetic and copies ran while one was open for 4% of the time, Pallas kernels for 20%

profile of v1, /device:TPU:25, one launch (start us, length us, event | category | flops | bytes accessed | tf_op | source)
XLA Modules:
  0.0 88.3 jit_solution(4063535526980471987)
XLA Ops:
  0.6 1.6 %slice_bitcast_fusion.4 = (bf16[4,128,128]{2,1,0:T(8,128)(2,1)S(1)}, bf16[4,128,128]{2,1,0:T(8,128)(2,1)S(1)}, bf16[4,128,128]{2,1,0:T(8,128)(2,1)S(1)}, bf16[4,...) fusion(bf16[1,24,128,128]{3,2,1,0:T(8,128)(2,1)} %refs_8_.1, ...), kind=kLoop, calls=%fused_computation.18 | loop fusion | bytes 3145728 | tf_op jit(solution)/shard_map/squeeze | solution.py:154
  2.9 1.6 %collective-permute-start.6 = (bf16[4,256,128]{2,1,0:T(8,128)(2,1)}, bf16[4,256,128]{2,1,0:T(8,128)(2,1)S(1)}, u32[]{:S(2)}, u32[]{:S(2)}) collective-permute-start(bf16[4,256,128]{2,1,0:T(8,128)(2,1)} %pad_maximum_fusion.5), channel_id=1, source_target_pairs={{0,32},{16,48},{32,64},{48,80},{64,96},{80,112},{96,128},{112,144}... | collective-permute-start | bytes 786440 | tf_op jit(solution)/shard_map/ppermute | solution.py:160
  5.3 1.6 %collective-permute-start.11 = (bf16[4,256,128]{2,1,0:T(8,128)(2,1)}, bf16[4,256,128]{2,1,0:T(8,128)(2,1)S(1)}, u32[]{:S(2)}, u32[]{:S(2)}) collective-permute-start(bf16[4,256,128]{2,1,0:T(8,128)(2,1)} %pad_maximum_fusion.7), channel_id=1, source_target_pairs={{0,32},{16,48},{32,64},{48,80},{64,96},{80,112},{96,128},{112,144}... | collective-permute-start | bytes 786440 | tf_op jit(solution)/shard_map/ppermute | solution.py:160
  7.6 1.6 %collective-permute-start.8 = (bf16[4,256,128]{2,1,0:T(8,128)(2,1)}, bf16[4,256,128]{2,1,0:T(8,128)(2,1)S(1)}, u32[]{:S(2)}, u32[]{:S(2)}) collective-permute-start(bf16[4,256,128]{2,1,0:T(8,128)(2,1)} %pad_maximum_fusion.6), channel_id=1, source_target_pairs={{0,32},{16,48},{32,64},{48,80},{64,96},{80,112},{96,128},{112,144}... | collective-permute-start | bytes 786440 | tf_op jit(solution)/shard_map/ppermute | solution.py:160
  10.0 2.8 %collective-permute-start = (bf16[4,256,128]{2,1,0:T(8,128)(2,1)}, bf16[4,256,128]{2,1,0:T(8,128)(2,1)S(1)}, u32[]{:S(2)}, u32[]{:S(2)}) collective-permute-start(bf16[4,256,128]{2,1,0:T(8,128)(2,1)} %pad_maximum_fusion.2), channel_id=1, source_target_pairs={{0,32},{16,48},{32,64},{48,80},{64,96},{80,112},{96,128},{112,144}... | collective-permute-start | bytes 786440 | tf_op jit(solution)/shard_map/ppermute | solution.py:160
  16.5 3.9 %collective-permute-done.11.refs_0_.refs_1_.refs_2_ = bf16[4,256,128]{2,1,0:T(8,128)(2,1)S(1)} collective-permute-done((bf16[4,256,128]{2,1,0:T(8,128)(2,1)}, bf16[4,256,128]{2,1,0:T(8,128)(2,1)S(1)}, u32[]{:S(2)}, u32[]{:S(2)}) %collective-permute-start.11) | collective-permute-done | bytes 262176 | tf_op jit(solution)/shard_map/ppermute | solution.py:160
  21.7 4.3 %collective-permute-done.8.refs_0_.refs_1_ = bf16[4,256,128]{2,1,0:T(8,128)(2,1)S(1)} collective-permute-done((bf16[4,256,128]{2,1,0:T(8,128)(2,1)}, bf16[4,256,128]{2,1,0:T(8,128)(2,1)S(1)}, u32[]{:S(2)}, u32[]{:S(2)}) %collective-permute-start.8) | collective-permute-done | bytes 262176 | tf_op jit(solution)/shard_map/ppermute | solution.py:160
  27.3 4.3 %collective-permute-done.refs_0_.refs_1_.refs_2_ = bf16[4,256,128]{2,1,0:T(8,128)(2,1)S(1)} collective-permute-done((bf16[4,256,128]{2,1,0:T(8,128)(2,1)}, bf16[4,256,128]{2,1,0:T(8,128)(2,1)S(1)}, u32[]{:S(2)}, u32[]{:S(2)}) %collective-permute-start) | collective-permute-done | bytes 262176 | tf_op jit(solution)/shard_map/ppermute | solution.py:160
  32.9 4.3 %collective-permute-done.2.refs_1_.refs_0_.refs_2_ = bf16[4,256,128]{2,1,0:T(8,128)(2,1)S(1)} collective-permute-done((bf16[4,256,128]{2,1,0:T(8,128)(2,1)}, bf16[4,256,128]{2,1,0:T(8,128)(2,1)S(1)}, u32[]{:S(2)}, u32[]{:S(2)}) %collective-permute-start.2) | collective-permute-done | bytes 262176 | tf_op jit(solution)/shard_map/ppermute | solution.py:160
  38.5 1.4 %far_part.10.refs_7_ = f32[4,128,256]{2,1,0:T(8,128)S(1)} custom-call(bf16[4,256,128]{2,1,0:T(8,128)(2,1)S(1)} %collective-permute-done.8.refs_0_.refs_1_, bf16[4,256,128]{2,1,0:T(8,128)(2,1)S(1)} %collective-permute-done.11.refs_0_.refs_1_.refs_2_, bf16[4,256,128]{2,1,0:T(8,128)(2,1)S(1)} %collective-permute-done.refs_0_.refs_1_.refs_2_, ...), custom_call_target="tpu_custom_call" | custom-call | flops 2000000000 | bytes 2000000 | tf_op jit(solution)/shard_map/far_part/pallas_call | solution.py:81
  40.0 1.4 %far_part.9.refs_7_ = f32[4,128,256]{2,1,0:T(8,128)S(1)} custom-call(bf16[4,256,128]{2,1,0:T(8,128)(2,1)S(1)} %collective-permute-done.11.refs_0_.refs_1_.refs_2_, bf16[4,256,128]{2,1,0:T(8,128)(2,1)S(1)} %collective-permute-done.refs_0_.refs_1_.refs_2_, bf16[4,256,128]{2,1,0:T(8,128)(2,1)S(1)} %collective-permute-done.2.refs_1_.refs_0_.refs_2_, ...), custom_call_target="tpu_custom_call" | custom-call | flops 2000000000 | bytes 2000000 | tf_op jit(solution)/shard_map/far_part/pallas_call | solution.py:81
  41.4 1.4 %collective-permute-done.4.refs_2_.refs_1_.refs_0_ = bf16[4,256,128]{2,1,0:T(8,128)(2,1)S(1)} collective-permute-done((bf16[4,256,128]{2,1,0:T(8,128)(2,1)S(1)}, bf16[4,256,128]{2,1,0:T(8,128)(2,1)S(1)}, u32[]{:S(2)}, u32[]{:S(2)}) %collective-permute-start.4) | collective-permute-done | bytes 262176 | tf_op jit(solution)/shard_map/ppermute | solution.py:160
  44.1 1.4 %far_part.7.refs_10_ = f32[4,128,256]{2,1,0:T(8,128)S(1)} custom-call(bf16[4,256,128]{2,1,0:T(8,128)(2,1)S(1)} %collective-permute-done.2.refs_1_.refs_0_.refs_2_, bf16[4,256,128]{2,1,0:T(8,128)(2,1)S(1)} %collective-permute-done.4.refs_2_.refs_1_.refs_0_, bf16[4,256,128]{2,1,0:T(8,128)(2,1)S(1)} %collective-permute-done.6.refs_2_.refs_1_, ...), custom_call_target="tpu_custom_call" | custom-call | flops 2000000000 | bytes 2000000 | tf_op jit(solution)/shard_map/far_part/pallas_call | solution.py:81
  45.6 5.4 %collective-permute-start.13 = (bf16[2,4,256,128]{3,2,1,0:T(8,128)(2,1)S(1)}, bf16[2,4,256,128]{3,2,1,0:T(8,128)(2,1)S(1)}, u32[]{:S(2)}, u32[]{:S(2)}) collective-permute-start(bf16[2,4,256,128]{3,2,1,0:T(8,128)(2,1)S(1)} %pad_maximum_fusion.1), channel_id=1, source_target_pairs={{0,1},{1,2},{2,3},{3,4},{4,5},{5,6},{6,7},{7,8},{8,9},{9,10},{10,1... | collective-permute-start | bytes 1572872 | tf_op jit(solution)/shard_map/ppermute | solution.py:165
  51.0 1.4 %far_part.6.refs_9_ = f32[4,128,256]{2,1,0:T(8,128)S(1)} custom-call(bf16[4,256,128]{2,1,0:T(8,128)(2,1)S(1)} %collective-permute-done.refs_0_.refs_1_.refs_2_, bf16[4,256,128]{2,1,0:T(8,128)(2,1)S(1)} %collective-permute-done.2.refs_1_.refs_0_.refs_2_, bf16[4,256,128]{2,1,0:T(8,128)(2,1)S(1)} %collective-permute-done.4.refs_2_.refs_1_.refs_0_, ...), custom_call_target="tpu_custom_call" | custom-call | flops 2000000000 | bytes 2000000 | tf_op jit(solution)/shard_map/far_part/pallas_call | solution.py:81
  52.9 7.0 %collective-permute-done.13 = bf16[2,4,256,128]{3,2,1,0:T(8,128)(2,1)S(1)} collective-permute-done((bf16[2,4,256,128]{3,2,1,0:T(8,128)(2,1)S(1)}, bf16[2,4,256,128]{3,2,1,0:T(8,128)(2,1)S(1)}, u32[]{:S(2)}, u32[]{:S(2)}) %collective-permute-start.13) | collective-permute-done | bytes 524320 | tf_op jit(solution)/shard_map/ppermute | solution.py:165
  59.9 1.9 %collective-permute-start.10 = (bf16[2,4,256,128]{3,2,1,0:T(8,128)(2,1)S(1)}, bf16[2,4,256,128]{3,2,1,0:T(8,128)(2,1)S(1)}, u32[]{:S(2)}, u32[]{:S(2)}) collective-permute-start(bf16[2,4,256,128]{3,2,1,0:T(8,128)(2,1)S(1)} %pad_maximum_fusion), channel_id=1, source_target_pairs={{1,0},{2,1},{3,2},{4,3},{5,4},{6,5},{7,6},{8,7},{9,8},{10,9},{11,1... | collective-permute-start | bytes 1572872 | tf_op jit(solution)/shard_map/ppermute | solution.py:166
  61.9 1.4 %far_part.11.refs_7_ = f32[4,128,256]{2,1,0:T(8,128)S(1)} custom-call(bf16[4,256,128]{2,1,0:T(8,128)(2,1)S(1)} %get-tuple-element.30.refs_0_, bf16[4,256,128]{2,1,0:T(8,128)(2,1)S(1)} %collective-permute-done.8.refs_0_.refs_1_, bf16[4,256,128]{2,1,0:T(8,128)(2,1)S(1)} %collective-permute-done.11.refs_0_.refs_1_.refs_2_, ...), custom_call_target="tpu_custom_call" | custom-call | flops 2000000000 | bytes 2000000 | tf_op jit(solution)/shard_map/far_part/pallas_call | solution.py:81
  63.3 2.8 %near_part.4 = (bf16[1,24,128,128]{3,2,1,0:T(8,128)(2,1)}, bf16[1,24,128,128]{3,2,1,0:T(8,128)(2,1)}) custom-call(bf16[4,256,128]{2,1,0:T(8,128)(2,1)S(1)} %get-tuple-element.31.refs_0_, bf16[4,256,128]{2,1,0:T(8,128)(2,1)S(1)} %collective-permute-done.9.refs_1_.refs_0_, bf16[4,256,128]{2,1,0:T(8,128)(2,1)S(1)} %collective-permute-done.12.refs_2_.refs_1_.refs_0_, ...), custom_call_target="tpu_custom_call" | custom-call | flops 2500000000 | bytes 4000000 | tf_op jit(solution)/shard_map/near_part/pallas_call | solution.py:128
  66.1 8.6 %collective-permute-done.10 = bf16[2,4,256,128]{3,2,1,0:T(8,128)(2,1)S(1)} collective-permute-done((bf16[2,4,256,128]{3,2,1,0:T(8,128)(2,1)S(1)}, bf16[2,4,256,128]{3,2,1,0:T(8,128)(2,1)S(1)}, u32[]{:S(2)}, u32[]{:S(2)}) %collective-permute-start.10) | collective-permute-done | bytes 524320 | tf_op jit(solution)/shard_map/ppermute | solution.py:166
  74.8 2.8 %near_part.5 = (bf16[1,24,128,128]{3,2,1,0:T(8,128)(2,1)}, bf16[1,24,128,128]{3,2,1,0:T(8,128)(2,1)}) custom-call(bf16[4,256,128]{2,1,0:T(8,128)(2,1)S(1)} %collective-permute-done.9.refs_1_.refs_0_, bf16[4,256,128]{2,1,0:T(8,128)(2,1)S(1)} %collective-permute-done.12.refs_2_.refs_1_.refs_0_, ...), custom_call_target="tpu_custom_call", output_to_operand_aliasing={{0}: (8, {}), {1}: (9, {})} | custom-call | flops 2500000000 | bytes 4000000 | tf_op jit(solution)/shard_map/near_part/pallas_call | solution.py:128
  77.6 1.4 %far_part.8.refs_11_ = f32[4,128,256]{2,1,0:T(8,128)S(1)} custom-call(bf16[4,256,128]{2,1,0:T(8,128)(2,1)S(1)} %collective-permute-done.4.refs_2_.refs_1_.refs_0_, bf16[4,256,128]{2,1,0:T(8,128)(2,1)S(1)} %collective-permute-done.6.refs_2_.refs_1_, bf16[4,256,128]{2,1,0:T(8,128)(2,1)S(1)} %get-tuple-element.32.refs_2_, ...), custom_call_target="tpu_custom_call" | custom-call | flops 2000000000 | bytes 2000000 | tf_op jit(solution)/shard_map/far_part/pallas_call | solution.py:81
  79.0 2.8 %near_part.6 = (bf16[1,24,128,128]{3,2,1,0:T(8,128)(2,1)}, bf16[1,24,128,128]{3,2,1,0:T(8,128)(2,1)}) custom-call(bf16[4,256,128]{2,1,0:T(8,128)(2,1)S(1)} %collective-permute-done.12.refs_2_.refs_1_.refs_0_, bf16[4,256,128]{2,1,0:T(8,128)(2,1)S(1)} %collective-permute-done.1.refs_2_.refs_1_.refs_0_, ...), custom_call_target="tpu_custom_call", output_to_operand_aliasing={{0}: (8, {}), {1}: (9, {})} | custom-call | flops 2500000000 | bytes 4000000 | tf_op jit(solution)/shard_map/near_part/pallas_call | solution.py:128
  81.8 6.5 %near_part.7 = (bf16[1,24,128,128]{3,2,1,0:T(8,128)(2,1)}, bf16[1,24,128,128]{3,2,1,0:T(8,128)(2,1)}) custom-call(bf16[4,256,128]{2,1,0:T(8,128)(2,1)S(1)} %collective-permute-done.1.refs_2_.refs_1_.refs_0_, bf16[4,256,128]{2,1,0:T(8,128)(2,1)S(1)} %collective-permute-done.3.refs_2_.refs_1_, ...), custom_call_target="tpu_custom_call", output_to_operand_aliasing={{0}: (12, {}), {1}: (13, {})} | custom-call | flops 7500000256 | bytes 4000000 | tf_op jit(solution)/shard_map/near_part/pallas_call | solution.py:128
  (42 shorter events, 13.4 us)
Async XLA Ops:
  2.2 12.2 %copy-start.2 = (bf16[2,4,1,128,128]{4,3,2,1,0:T(8,128)(2,1)S(1)}, bf16[2,4,1,128,128]{4,3,2,1,0:T(8,128)(2,1)}, u32[]{:S(2)}) copy-start(bf16[2,4,1,128,128]{4,3,2,1,0:T(8,128)(2,1)} %coupling_ref.1) | copy-start | bytes 786436
  2.2 12.2 %copy-start.3 = (f32[2,4,8]{2,1,0:T(4,128)S(1)}, f32[2,4,8]{2,1,0:T(4,128)}, u32[]{:S(2)}) copy-start(f32[2,4,8]{2,1,0:T(4,128)} %strengths_ref.1) | copy-start | bytes 772
  2.2 12.2 %copy-start.4 = (s32[2,8]{1,0:T(2,128)S(1)}, s32[2,8]{1,0:T(2,128)}, u32[]{:S(2)}) copy-start(s32[2,8]{1,0:T(2,128)} %offsets_ref.1) | copy-start | bytes 196
  2.9 12.7 %collective-permute-start.6 = (bf16[4,256,128]{2,1,0:T(8,128)(2,1)}, bf16[4,256,128]{2,1,0:T(8,128)(2,1)S(1)}, u32[]{:S(2)}, u32[]{:S(2)}) collective-permute-start(bf16[4,256,128]{2,1,0:T(8,128)(2,1)} %pad_maximum_fusion.5), channel_id=1, source_target_pairs={{0,32},{16,48},{32,64},{48,80},{64,96},{80,112},{96,128},{112,144}... | collective-permute-start | bytes 786440 | tf_op jit(solution)/shard_map/ppermute | solution.py:160
  5.3 15.1 %collective-permute-start.11 = (bf16[4,256,128]{2,1,0:T(8,128)(2,1)}, bf16[4,256,128]{2,1,0:T(8,128)(2,1)S(1)}, u32[]{:S(2)}, u32[]{:S(2)}) collective-permute-start(bf16[4,256,128]{2,1,0:T(8,128)(2,1)} %pad_maximum_fusion.7), channel_id=1, source_target_pairs={{0,32},{16,48},{32,64},{48,80},{64,96},{80,112},{96,128},{112,144}... | collective-permute-start | bytes 786440 | tf_op jit(solution)/shard_map/ppermute | solution.py:160
  7.6 18.3 %collective-permute-start.8 = (bf16[4,256,128]{2,1,0:T(8,128)(2,1)}, bf16[4,256,128]{2,1,0:T(8,128)(2,1)S(1)}, u32[]{:S(2)}, u32[]{:S(2)}) collective-permute-start(bf16[4,256,128]{2,1,0:T(8,128)(2,1)} %pad_maximum_fusion.6), channel_id=1, source_target_pairs={{0,32},{16,48},{32,64},{48,80},{64,96},{80,112},{96,128},{112,144}... | collective-permute-start | bytes 786440 | tf_op jit(solution)/shard_map/ppermute | solution.py:160
  10.0 21.6 %collective-permute-start = (bf16[4,256,128]{2,1,0:T(8,128)(2,1)}, bf16[4,256,128]{2,1,0:T(8,128)(2,1)S(1)}, u32[]{:S(2)}, u32[]{:S(2)}) collective-permute-start(bf16[4,256,128]{2,1,0:T(8,128)(2,1)} %pad_maximum_fusion.2), channel_id=1, source_target_pairs={{0,32},{16,48},{32,64},{48,80},{64,96},{80,112},{96,128},{112,144}... | collective-permute-start | bytes 786440 | tf_op jit(solution)/shard_map/ppermute | solution.py:160
  13.6 23.7 %collective-permute-start.2 = (bf16[4,256,128]{2,1,0:T(8,128)(2,1)}, bf16[4,256,128]{2,1,0:T(8,128)(2,1)S(1)}, u32[]{:S(2)}, u32[]{:S(2)}) collective-permute-start(bf16[4,256,128]{2,1,0:T(8,128)(2,1)} %pad_maximum_fusion.3), channel_id=1, source_target_pairs={{0,32},{16,48},{32,64},{48,80},{64,96},{80,112},{96,128},{112,144}... | collective-permute-start | bytes 786440 | tf_op jit(solution)/shard_map/ppermute | solution.py:160
  15.6 27.2 %collective-permute-start.4 = (bf16[4,256,128]{2,1,0:T(8,128)(2,1)S(1)}, bf16[4,256,128]{2,1,0:T(8,128)(2,1)S(1)}, u32[]{:S(2)}, u32[]{:S(2)}) collective-permute-start(bf16[4,256,128]{2,1,0:T(8,128)(2,1)S(1)} %pad_maximum_fusion.4), channel_id=1, source_target_pairs={{0,32},{16,48},{32,64},{48,80},{64,96},{80,112},{96,128},{112,144}... | collective-permute-start | bytes 786440 | tf_op jit(solution)/shard_map/ppermute | solution.py:160
  20.4 25.1 %collective-permute-start.7 = (bf16[4,256,128]{2,1,0:T(8,128)(2,1)S(1)}, bf16[4,256,128]{2,1,0:T(8,128)(2,1)S(1)}, u32[]{:S(2)}, u32[]{:S(2)}) collective-permute-start(bf16[4,256,128]{2,1,0:T(8,128)(2,1)S(1)} %broadcast_select_fusion.2), channel_id=1, source_target_pairs={{0,16},{16,0},{32,48},{48,32},{64,80},{80,64},{96,112},{112,96},{1... | collective-permute-start | bytes 786440 | tf_op jit(solution)/shard_map/ppermute | solution.py:163
  26.0 37.3 %collective-permute-start.12 = (bf16[4,256,128]{2,1,0:T(8,128)(2,1)S(1)}, bf16[4,256,128]{2,1,0:T(8,128)(2,1)S(1)}, u32[]{:S(2)}, u32[]{:S(2)}) collective-permute-start(bf16[4,256,128]{2,1,0:T(8,128)(2,1)S(1)} %broadcast_select_fusion), channel_id=1, source_target_pairs={{0,16},{16,0},{32,48},{48,32},{64,80},{80,64},{96,112},{112,96},{1... | collective-permute-start | bytes 786440 | tf_op jit(solution)/shard_map/ppermute | solution.py:163
  31.6 20.9 %collective-permute-start.9 = (bf16[4,256,128]{2,1,0:T(8,128)(2,1)S(1)}, bf16[4,256,128]{2,1,0:T(8,128)(2,1)S(1)}, u32[]{:S(2)}, u32[]{:S(2)}) collective-permute-start(bf16[4,256,128]{2,1,0:T(8,128)(2,1)S(1)} %broadcast_select_fusion.1), channel_id=1, source_target_pairs={{0,16},{16,0},{32,48},{48,32},{64,80},{80,64},{96,112},{112,96},{1... | collective-permute-start | bytes 786440 | tf_op jit(solution)/shard_map/ppermute | solution.py:163
  37.2 37.6 %collective-permute-start.1 = (bf16[4,256,128]{2,1,0:T(8,128)(2,1)S(1)}, bf16[4,256,128]{2,1,0:T(8,128)(2,1)S(1)}, u32[]{:S(2)}, u32[]{:S(2)}) collective-permute-start(bf16[4,256,128]{2,1,0:T(8,128)(2,1)S(1)} %broadcast_select_fusion.5), channel_id=1, source_target_pairs={{0,16},{16,0},{32,48},{48,32},{64,80},{80,64},{96,112},{112,96},{1... | collective-permute-start | bytes 786440 | tf_op jit(solution)/shard_map/ppermute | solution.py:163
  42.8 36.1 %collective-permute-start.3 = (bf16[4,256,128]{2,1,0:T(8,128)(2,1)S(1)}, bf16[4,256,128]{2,1,0:T(8,128)(2,1)S(1)}, u32[]{:S(2)}, u32[]{:S(2)}) collective-permute-start(bf16[4,256,128]{2,1,0:T(8,128)(2,1)S(1)} %broadcast_select_fusion.4), channel_id=1, source_target_pairs={{0,16},{16,0},{32,48},{48,32},{64,80},{80,64},{96,112},{112,96},{1... | collective-permute-start | bytes 786440 | tf_op jit(solution)/shard_map/ppermute | solution.py:163
  45.6 14.3 %collective-permute-start.13 = (bf16[2,4,256,128]{3,2,1,0:T(8,128)(2,1)S(1)}, bf16[2,4,256,128]{3,2,1,0:T(8,128)(2,1)S(1)}, u32[]{:S(2)}, u32[]{:S(2)}) collective-permute-start(bf16[2,4,256,128]{3,2,1,0:T(8,128)(2,1)S(1)} %pad_maximum_fusion.1), channel_id=1, source_target_pairs={{0,1},{1,2},{2,3},{3,4},{4,5},{5,6},{6,7},{7,8},{8,9},{9,10},{10,1... | collective-permute-start | bytes 1572872 | tf_op jit(solution)/shard_map/ppermute | solution.py:165
  52.5 29.3 %collective-permute-start.5 = (bf16[4,256,128]{2,1,0:T(8,128)(2,1)S(1)}, bf16[4,256,128]{2,1,0:T(8,128)(2,1)S(1)}, u32[]{:S(2)}, u32[]{:S(2)}) collective-permute-start(bf16[4,256,128]{2,1,0:T(8,128)(2,1)S(1)} %broadcast_select_fusion.3), channel_id=1, source_target_pairs={{0,16},{16,0},{32,48},{48,32},{64,80},{80,64},{96,112},{112,96},{1... | collective-permute-start | bytes 786440 | tf_op jit(solution)/shard_map/ppermute | solution.py:163
  59.9 14.8 %collective-permute-start.10 = (bf16[2,4,256,128]{3,2,1,0:T(8,128)(2,1)S(1)}, bf16[2,4,256,128]{3,2,1,0:T(8,128)(2,1)S(1)}, u32[]{:S(2)}, u32[]{:S(2)}) collective-permute-start(bf16[2,4,256,128]{3,2,1,0:T(8,128)(2,1)S(1)} %pad_maximum_fusion), channel_id=1, source_target_pairs={{1,0},{2,1},{3,2},{4,3},{5,4},{6,5},{7,6},{8,7},{9,8},{10,9},{11,1... | collective-permute-start | bytes 1572872 | tf_op jit(solution)/shard_map/ppermute | solution.py:166
  61.9 1.5 %copy-start = (bf16[1,24,128,128]{3,2,1,0:T(8,128)(2,1)S(1)}, bf16[1,24,128,128]{3,2,1,0:T(8,128)(2,1)}, u32[]{:S(2)}) copy-start(bf16[1,24,128,128]{3,2,1,0:T(8,128)(2,1)} %refs_8_.1) | copy-start | bytes 2359300
  61.9 1.5 %copy-start.1 = (bf16[1,24,128,128]{3,2,1,0:T(8,128)(2,1)S(1)}, bf16[1,24,128,128]{3,2,1,0:T(8,128)(2,1)}, u32[]{:S(2)}) copy-start(bf16[1,24,128,128]{3,2,1,0:T(8,128)(2,1)} %refs_7_.1) | copy-start | bytes 2359300

commit v2 on v1

v2 whole, which is shorter than its diff:
```python
import functools

import jax
import jax.numpy as jnp
from jax import lax
from jax.experimental import pallas as pl
from jax.experimental.pallas import tpu as pltpu
from jax.sharding import PartitionSpec as P

REACH = 4
HOPS = 2
BRANCHES = 4
WINDOW = 2 * REACH
AHEAD = 2
VMEM_LIMIT = 40 * 2**20

F32 = jnp.float32
BF16 = jnp.bfloat16
dot = functools.partial(jnp.dot, preferred_element_type=F32)
WHOLE = pl.BlockSpec(memory_space=pltpu.VMEM)
SCALARS = pl.BlockSpec(memory_space=pltpu.SMEM)
UNTOUCHED = pl.BlockSpec(memory_space=pl.ANY)
FREE = pl.CostEstimate(flops=0, bytes_accessed=10**6, transcendentals=0)


def prepare_kernel(offsets_ref, strengths_ref, coupling_ref, *outs):
    no = coupling_ref.shape[-1]
    for s in range(HOPS):
        weights_ref, joined_ref = outs[2 * s : 2 * s + 2]
        for n in range(BRANCHES):
            matrix = coupling_ref[s, n, 0]
            joined_ref[:, n * no : (n + 1) * no] = matrix
            turned = matrix.astype(F32).T
            for i in range(WINDOW):
                w = offsets_ref[s, i]
                j = jnp.where(w > 0, REACH - w, REACH - 1 - w)
                rows = pl.ds(pl.multiple_of(j * no, no), no)
                weights_ref[rows, n * no : (n + 1) * no] = (strengths_ref[s, n, i] * turned).astype(BF16)


def prepare(coupling, strengths, offsets):
    no = coupling.shape[-1]
    outs = pl.pallas_call(
        prepare_kernel,
        out_shape=[
            jax.ShapeDtypeStruct((WINDOW * no, BRANCHES * no), BF16),
            jax.ShapeDtypeStruct((no, BRANCHES * no), BF16),
        ]
        * HOPS,
        in_specs=[SCALARS, SCALARS, WHOLE],
        out_specs=[WHOLE] * (2 * HOPS),
        compiler_params=pltpu.CompilerParams(vmem_limit_bytes=VMEM_LIMIT),
        cost_estimate=FREE,
        name="prepare",
    )(offsets, strengths, coupling)
    return outs[:2], outs[2:]


def hop_terms(odd_ref, tiles, first, weights_ref, joined_ref):
    no = joined_ref.shape[0]

    def energy(t):
        tile = tiles[first + t // REACH]
        if isinstance(tile, tuple):
            return jnp.where(odd_ref[0] > 0, tile[0][t % REACH], tile[1][t % REACH])
        return tile[t % REACH]

    rows = []
    for i in range(REACH):
        rows.append(jnp.concatenate([energy(i + j + (j >= REACH)) for j in range(WINDOW)], axis=1))
    right = dot(jnp.concatenate(rows, axis=0), weights_ref[...]).astype(BF16)
    terms = []
    for i in range(REACH):
        stacked = []
        for n in range(BRANCHES):
            block = right[i * 2 * no : (i + 1) * 2 * no, n * no : (n + 1) * no]
            stacked.append(jnp.concatenate([block[:no], block[no:]], axis=1))
        terms.append(dot(joined_ref[...], jnp.concatenate(stacked, axis=0)))
    return terms


def regroup(layout, refs):
    refs = iter(refs)
    return [(next(refs), next(refs)) if pair else next(refs) for pair in layout]


def flat(tiles):
    layout = tuple(isinstance(tile, tuple) for tile in tiles)
    return layout, [x for tile in tiles for x in (tile if isinstance(tile, tuple) else (tile,))]


def far_kernel(layout, odd_ref, *refs):
    width = len(layout) + sum(layout)
    tiles, (weights_ref, joined_ref, *outs) = regroup(layout, refs[:width]), refs[width:]
    count = len(layout) - 2
    for c in range(count):
        for i, term in enumerate(hop_terms(odd_ref, tiles, c, weights_ref, joined_ref)):
            outs[c][i] = term


def far_part(odd, tiles, weights, joined):
    count = len(tiles) - 2
    layout, tiles = flat(tiles)
    no = joined.shape[0]
    return pl.pallas_call(
        functools.partial(far_kernel, layout),
        out_shape=[jax.ShapeDtypeStruct((REACH, no, 2 * no), F32)] * count,
        in_specs=[SCALARS] + [WHOLE] * (len(tiles) + 2),
        out_specs=[WHOLE] * count,
        compiler_params=pltpu.CompilerParams(vmem_limit_bytes=VMEM_LIMIT),
        cost_estimate=FREE,
        name="far_part",
    )(odd, *tiles, weights, joined)


def crossed(real, imag):
    return jnp.concatenate(
        [jnp.concatenate([real, imag], axis=1), jnp.concatenate([-imag, real], axis=1)], axis=0
    )


def near_kernel(layouts, odd_ref, *refs):
    count = len(layouts[1])
    width, own_width = (len(layout) + sum(layout) for layout in layouts)
    tiles, refs = regroup(layouts[0], refs[:width]), refs[width:]
    owns, refs = regroup(layouts[1], refs[:own_width]), refs[own_width:]
    weights_ref, joined_ref = refs[:2]
    parts = refs[2 : 2 + count]
    out_real_ref, out_imag_ref = refs[-2:]
    no = joined_ref.shape[0]
    for c in range(count):

        @pl.when(pl.program_id(0) == c)
        def _():
            terms = hop_terms(odd_ref, tiles, c, weights_ref, joined_ref)
            sigmas = [(term + parts[c][i]).astype(BF16) for i, term in enumerate(terms)]
            greens = []
            for i in range(REACH):
                own = owns[c]
                green = jnp.where(odd_ref[0] > 0, own[0][i], own[1][i]) if isinstance(own, tuple) else own[i]
                greens.append((green[:no], green[no:]))
            prods = [
                dot(jnp.concatenate(pair, axis=1), crossed(sigma[:, :no], sigma[:, no:])).astype(BF16)
                for pair, sigma in zip(greens, sigmas)
            ]
            backs = [dot(prod, crossed(*pair)) / no for pair, prod in zip(greens, prods)]
            for i, ((real, imag), back) in enumerate(zip(greens, backs)):
                out_real_ref[0, i] = (real.astype(F32) + back[:, :no]).astype(BF16)
                out_imag_ref[0, i] = (imag.astype(F32) + back[:, no:]).astype(BF16)


def near_part(odd, tiles, weights, joined, owns, parts, start, shape, so_far):
    count = len(owns)
    layout, tiles = flat(tiles)
    own_layout, owns = flat(owns)
    no = joined.shape[0]
    block = pl.BlockSpec((1, REACH, no, no), lambda g: (0, start + g, 0, 0))
    shape = jax.ShapeDtypeStruct(shape, BF16)
    inputs = [odd, *tiles, *owns, weights, joined, *parts]
    in_specs = [SCALARS] + [WHOLE] * (len(inputs) - 1)
    aliases = {}
    if so_far is not None:
        aliases = {len(inputs): 0, len(inputs) + 1: 1}
        inputs += so_far
        in_specs += [UNTOUCHED] * 2
    return pl.pallas_call(
        functools.partial(near_kernel, (layout, own_layout)),
        grid=(count,),
        out_shape=(shape, shape),
        in_specs=in_specs,
        out_specs=(block, block),
        input_output_aliases=aliases,
        compiler_params=pltpu.CompilerParams(vmem_limit_bytes=VMEM_LIMIT),
        cost_estimate=FREE,
        name="near_part",
    )(*inputs)


def tied(x, *deps):
    return lax.optimization_barrier((x, *deps))[0] if deps else x


def shards(green_real, green_imag, coupling, strengths, offsets):
    chunks = green_real.shape[1] // REACH
    momenta, lanes = lax.axis_size("kz"), lax.axis_size("en")
    both = ("kz", "en")
    even = lax.axis_index("kz") % 2 == 0
    lane = lax.axis_index("en")
    odd_lane = lane % 2 == 1
    middle = lanes // 2
    at_middle = (lane == middle - 1) | (lane == middle)
    two_on = [(i, (i + 2) % momenta) for i in range(momenta)]
    swap = [(i, i ^ 1) for i in range(momenta)]
    outer = [p for m in range(1, lanes - 1, 2) for p in ((m, m + 1), (m + 1, m))]
    inner = [(i, i ^ 1) for i in range(lanes)]
    outer_turned = [
        (k * lanes + i, (k ^ 1 if {i, j} == {middle - 1, middle} else k) * lanes + j)
        for k in range(momenta)
        for i, j in outer
    ]

    def by_lane(odd, other):
        return jnp.where(odd_lane, odd, other)

    last = chunks - 1
    def cut(c, real, imag):
        energies = slice(c * REACH, (c + 1) * REACH)
        return jnp.concatenate([real[0, energies], imag[0, energies]], axis=1)

    green = (green_real, green_imag)
    own = [by_lane(cut(last, *green), cut(0, *green))]
    far, near = [lax.ppermute(own[0], "kz", two_on)], []
    green = lax.optimization_barrier((*green, own[0]))[:2]
    own.append(by_lane(cut(0, *green), cut(last, *green)))
    own += [cut(c, *green) for c in range(1, last)]
    for i in range(1, chunks):
        if i >= AHEAD:
            own[i] = tied(own[i], far[i - AHEAD])
        far.append(lax.ppermute(own[i], "kz", two_on))
    near_side, far_side = prepare(coupling, strengths, offsets)

    def arranged(sent, outer_halo, inner_halo):
        below, first = (inner_halo, outer_halo), (sent[1], sent[0])
        top, above = (sent[0], sent[1]), (outer_halo, inner_halo)
        return [below, first, *sent[2:], top, above]

    shape = green_real.shape
    odd = odd_lane.astype(jnp.int32).reshape(1)
    out, done = None, (far_side[0],)
    parts, halos, source = {}, {}, []
    far_work = {2: [0], 3: [1], 4: [2], 5: [3, 4, 5]}
    near_work = {4: [0], 5: [1]}
    rest = [2, 3, 4, 5]

    def grouped(sent, side, group):
        sent = sent + [sent[-1]] * (chunks - len(sent))
        return arranged(sent, halos[side, "outer"], halos[side, "inner"])[group[0] : group[-1] + 3]

    def after(tiles, done):
        tiles[-1] = tuple(tied(x, *done) for x in tiles[-1]) if isinstance(tiles[-1], tuple) else tied(tiles[-1], *done)
        return tiles

    for i in range(chunks):
        if i >= 2:
            done += (near[i - 2],)
        if i == 4:
            done += (halos["near", "outer"],)
        far[i] = tied(far[i], *done)
        source.append(jnp.where(even, own[i], far[i]))
        gate = [source[i]]
        if i == 0:
            halos["far", "outer"] = lax.ppermute(far[0], "en", outer)
        near.append(lax.ppermute(source[i], "kz", swap))
        if i == 1:
            halos["far", "inner"] = lax.ppermute(far[1], "en", inner)
        if i == 2:
            edge = tied(jnp.where(at_middle, source[0], near[0]), source[i])
            halos["near", "outer"] = lax.ppermute(edge, both, outer_turned)
            gate.append(edge)
        if i == 3:
            edge = tied(near[1], source[i])
            halos["near", "inner"] = lax.ppermute(edge, "en", inner)
            gate.append(edge)
        done = tuple(gate)
        if i in far_work:
            group = far_work[i]
            part = far_part(odd, after(grouped(far, "far", group), done), *far_side)
            for n, c in enumerate(group):
                parts[c] = part[n]
            done = (part[-1],)
        for c in near_work.get(i, []):
            owns = arranged(own, own[0], own[0])[c + 1 : c + 2]
            tiles = grouped(near, "near", [c])
            tiles[2] = tied(tiles[2], *done)
            out = near_part(odd, tiles, *near_side, owns, [parts[c]], c, shape, out)
            done = (out[0],)
    owns = arranged(own, own[0], own[0])[rest[0] + 1 : rest[-1] + 2]
    out = near_part(
        odd, grouped(near, "near", rest), *near_side, owns, [parts[c] for c in rest], rest[0], shape, out
    )
    return tuple(out)


def solution(mesh):
    in_specs = (
        P("kz", "en", None, None),
        P("kz", "en", None, None),
        P(None, None, "kz", None, None),
        P(),
        P(),
    )
    out_specs = (P("kz", "en", None, None), P("kz", "en", None, None))
    return jax.shard_map(shards, mesh=mesh, in_specs=in_specs, out_specs=out_specs, check_vma=False)
```

time: 88.5 us -> 67.8 us (0.77)
  the two profiles are of different devices: /device:TPU:25 before, /device:TPU:4 now
where the time goes in v2:
time: 67.8 us; the launch traced here: 67.4 us
  Pallas kernels  25.1 us (37%)
  starting transfers between devices  23.8 us (35%)
  other arithmetic  7.5 us (11%)
  waiting for transfers between devices  5.55 us (8%)
  local copies, waits for them, and re-layouts  4.54 us (7%)
  between operations  0.9 us (1%)
    pallas_call x3, Pallas kernels, near_part(): pl.pallas_call(functools.partial(near_kernel, (layout, own_layout)), grid...  15.6 us
    pallas_call x4, Pallas kernels, far_part(): pl.pallas_call(functools.partial(far_kernel, layout), out_shape=[jax.Shap...  8.24 us
    ppermute x5, starting transfers between devices, shards(): far.append(lax.ppermute(own[i], 'kz', two_on))  7.79 us
    ppermute x6, starting transfers between devices, shards(): near.append(lax.ppermute(source[i], 'kz', swap))  6.87 us
    ppermute x1, starting transfers between devices, shards(): halos['near', 'outer'] = lax.ppermute(edge, both, outer_turned)  3.93 us
    ppermute x1, starting transfers between devices, shards(): halos['far', 'outer'] = lax.ppermute(far[0], 'en', outer)  3.09 us
    concatenate x4, other arithmetic, cut(): return jnp.concatenate([real[0, energies], imag[0, energies]], axis=1)  2.87 us
    select_n x6, other arithmetic, shards(): source.append(jnp.where(even, own[i], far[i]))  2.81 us
  transfers between devices with their start and end apart: 16, of which 4 were waited for; matrix products, arithmetic and copies ran while one was open for 13% of the time, Pallas kernels for 24%

profile of v2, /device:TPU:4, one launch (start us, length us, event | category | flops | bytes accessed | tf_op | source)
XLA Modules:
  0.0 67.4 jit_solution(7165886054126116980)
XLA Ops:
  0.7 1.2 %slice_bitcast_fusion.12 = (bf16[4,128,128]{2,1,0:T(8,128)(2,1)S(1)}, bf16[4,128,128]{2,1,0:T(8,128)(2,1)S(1)}, bf16[4,128,128]{2,1,0:T(8,128)(2,1)S(1)}, bf16[4,128,128]{2,1,0:T(8,128)(2,1)S(1)}) fusion(bf16[1,24,128,128]{3,2,1,0:T(8,128)(2,1)} %param.6, bf16[1,24,128,128]{3,2,1,0:T(8,128)(2,1)} %param.5), kind=kLoop, calls=%fused_computation.25 | loop fusion | bytes 1048576 | tf_op jit(solution)/shard_map/squeeze | solution.py:208
  2.0 2.0 %collective-permute-start = (bf16[4,256,128]{2,1,0:T(8,128)(2,1)S(1)}, bf16[4,256,128]{2,1,0:T(8,128)(2,1)S(1)}, u32[]{:S(2)}, u32[]{:S(2)}) collective-permute-start(bf16[4,256,128]{2,1,0:T(8,128)(2,1)S(1)} %maximum_select_fusion.refs_6_.refs_11_), channel_id=1, source_target_pairs={{0,32},{16,48},{32,64},{48,80},{64,96},{80,112},{96,128},{112,144}... | collective-permute-start | bytes 786440 | tf_op jit(solution)/shard_map/ppermute | solution.py:212
  6.2 1.9 %collective-permute-start.2 = (bf16[4,256,128]{2,1,0:T(8,128)(2,1)}, bf16[4,256,128]{2,1,0:T(8,128)(2,1)S(1)}, u32[]{:S(2)}, u32[]{:S(2)}) collective-permute-start(bf16[4,256,128]{2,1,0:T(8,128)(2,1)} %maximum_select_fusion.1.refs_5_.refs_12_), channel_id=1, source_target_pairs={{0,32},{16,48},{32,64},{48,80},{64,96},{80,112},{96,128},{112,144}... | collective-permute-start | bytes 786440 | tf_op jit(solution)/shard_map/ppermute | solution.py:219
  9.6 1.2 %prepare.1 = (bf16[1024,512]{1,0:T(8,128)(2,1)S(1)}, bf16[128,512]{1,0:T(8,128)(2,1)S(1)}, bf16[1024,512]{1,0:T(8,128)(2,1)S(1)}, bf16[128,512]{1,0:T(8,128)(2,1)S(1)}) custom-call(s32[2,8]{1,0:T(2,128)S(1)} %copy-done.7, f32[2,4,8]{2,1,0:T(4,128)S(1)} %copy-done.6, bf16[2,4,1,128,128]{4,3,2,1,0:T(8,128)(2,1)S(1)} %copy-done.5), custom_call_target="tpu_custom_call" | custom-call | bytes 1000000 | tf_op jit(solution)/shard_map/prepare/pallas_call | solution.py:43
  12.6 2.4 %collective-permute-done.refs_3_.refs_1_ = bf16[4,256,128]{2,1,0:T(8,128)(2,1)S(1)} collective-permute-done((bf16[4,256,128]{2,1,0:T(8,128)(2,1)S(1)}, bf16[4,256,128]{2,1,0:T(8,128)(2,1)S(1)}, u32[]{:S(2)}, u32[]{:S(2)}) %collective-permute-start) | collective-permute-done | bytes 262176 | tf_op jit(solution)/shard_map/ppermute | solution.py:212
  15.8 1.2 %collective-permute-start.3 = (bf16[4,256,128]{2,1,0:T(8,128)(2,1)}, bf16[4,256,128]{2,1,0:T(8,128)(2,1)S(1)}, u32[]{:S(2)}, u32[]{:S(2)}) collective-permute-start(bf16[4,256,128]{2,1,0:T(8,128)(2,1)} %broadcast_select_fusion.6), channel_id=1, source_target_pairs={{0,16},{16,0},{32,48},{48,32},{64,80},{80,64},{96,112},{112,96},{1... | collective-permute-start | bytes 786440 | tf_op jit(solution)/shard_map/ppermute | solution.py:253
  17.7 3.1 %collective-permute-start.7 = (bf16[4,256,128]{2,1,0:T(8,128)(2,1)S(1)}, bf16[4,256,128]{2,1,0:T(8,128)(2,1)S(1)}, u32[]{:S(2)}, u32[]{:S(2)}) collective-permute-start(bf16[4,256,128]{2,1,0:T(8,128)(2,1)S(1)} %collective-permute-done.refs_3_.refs_1_), channel_id=1, source_target_pairs={{1,2},{2,1},{3,4},{4,3},{5,6},{6,5},{7,8},{8,7},{9,10},{10,9},{11,... | collective-permute-start | bytes 786440 | tf_op jit(solution)/shard_map/ppermute | solution.py:252
  20.8 3.2 %collective-permute-start.5 = (bf16[4,256,128]{2,1,0:T(8,128)(2,1)}, bf16[4,256,128]{2,1,0:T(8,128)(2,1)S(1)}, u32[]{:S(2)}, u32[]{:S(2)}) collective-permute-start(bf16[4,256,128]{2,1,0:T(8,128)(2,1)} %pad_maximum_fusion.1.refs_8_), channel_id=1, source_target_pairs={{0,32},{16,48},{32,64},{48,80},{64,96},{80,112},{96,128},{112,144}... | collective-permute-start | bytes 786440 | tf_op jit(solution)/shard_map/ppermute | solution.py:219
  24.0 1.0 %broadcast_select_fusion.5 = bf16[4,256,128]{2,1,0:T(8,128)(2,1)S(1)} fusion(bf16[4,256,128]{2,1,0:T(8,128)(2,1)} %maximum_select_fusion.1.refs_5_.refs_12_, bf16[4,256,128]{2,1,0:T(8,128)(2,1)S(1)} %collective-permute-done.2.refs_2_.refs_0_.refs_4_, pred[]{:T(512)S(6)} %eq.16), kind=kLoop, calls=%fused_computation.11 | loop fusion | flops 131072 | bytes 786433 | tf_op jit(solution)/shard_map/jit(_where)/select_n | solution.py:249
  25.4 1.2 %collective-permute-start.8 = (bf16[4,256,128]{2,1,0:T(8,128)(2,1)S(1)}, bf16[4,256,128]{2,1,0:T(8,128)(2,1)S(1)}, u32[]{:S(2)}, u32[]{:S(2)}) collective-permute-start(bf16[4,256,128]{2,1,0:T(8,128)(2,1)S(1)} %broadcast_select_fusion.5), channel_id=1, source_target_pairs={{0,16},{16,0},{32,48},{48,32},{64,80},{80,64},{96,112},{112,96},{1... | collective-permute-start | bytes 786440 | tf_op jit(solution)/shard_map/ppermute | solution.py:253
  26.6 1.0 %broadcast_select_fusion.4 = bf16[4,256,128]{2,1,0:T(8,128)(2,1)S(1)} fusion(bf16[4,256,128]{2,1,0:T(8,128)(2,1)} %pad_maximum_fusion.refs_4_, bf16[4,256,128]{2,1,0:T(8,128)(2,1)S(1)} %collective-permute-done.1.refs_4_.refs_2_.refs_0_, pred[]{:T(512)S(6)} %eq.16), kind=kLoop, calls=%fused_computation.10 | loop fusion | flops 131072 | bytes 786433 | tf_op jit(solution)/shard_map/jit(_where)/select_n | solution.py:249
  27.6 1.0 %broadcast_select_fusion = bf16[4,256,128]{2,1,0:T(8,128)(2,1)S(1)} fusion(bf16[4,256,128]{2,1,0:T(8,128)(2,1)} %broadcast_select_fusion.6, bf16[4,256,128]{2,1,0:T(8,128)(2,1)S(1)} %collective-permute-done.3.refs_3_.refs_1_.refs_4_, pred[]{:T(512)S(6)} %or.3), kind=kLoop, calls=%fused_computation.6 | loop fusion | flops 131072 | bytes 786433 | tf_op jit(solution)/shard_map/jit(_where)/select_n | solution.py:257
  28.6 3.9 %collective-permute-start.11 = (bf16[4,256,128]{2,1,0:T(8,128)(2,1)S(1)}, bf16[4,256,128]{2,1,0:T(8,128)(2,1)S(1)}, u32[]{:S(2)}, u32[]{:S(2)}) collective-permute-start(bf16[4,256,128]{2,1,0:T(8,128)(2,1)S(1)} %broadcast_select_fusion), channel_id=1, source_target_pairs={{1,2},{2,1},{3,4},{4,3},{5,6},{6,5},{7,24},{8,23},{9,10},{10,9},{1... | collective-permute-start | bytes 786440 | tf_op jit(solution)/shard_map/ppermute | solution.py:258
  32.6 2.0 %collective-permute-start.4 = (bf16[4,256,128]{2,1,0:T(8,128)(2,1)S(1)}, bf16[4,256,128]{2,1,0:T(8,128)(2,1)S(1)}, u32[]{:S(2)}, u32[]{:S(2)}) collective-permute-start(bf16[4,256,128]{2,1,0:T(8,128)(2,1)S(1)} %broadcast_select_fusion.4), channel_id=1, source_target_pairs={{0,16},{16,0},{32,48},{48,32},{64,80},{80,64},{96,112},{112,96},{1... | collective-permute-start | bytes 786440 | tf_op jit(solution)/shard_map/ppermute | solution.py:253
  34.6 1.4 %far_part.4.refs_9_ = f32[4,128,256]{2,1,0:T(8,128)S(1)} custom-call(s32[1]{0:T(128)} %bitcast.odd_ref, bf16[4,256,128]{2,1,0:T(8,128)(2,1)S(1)} %collective-permute-done.6.refs_0_.refs_6_, bf16[4,256,128]{2,1,0:T(8,128)(2,1)S(1)} %collective-permute-done.7.refs_1_.refs_5_, bf16[4,256,128]{2,1,0:T(8,128)(2,1)S(1)} %collective-permute-done.2.refs_2_.refs_0_.refs_4_, ...), custom_call_target="tpu_custom_call" | custom-call | bytes 1000000 | tf_op jit(solution)/shard_map/far_part/pallas_call | solution.py:105
  37.0 2.7 %collective-permute-start.13 = (bf16[4,256,128]{2,1,0:T(8,128)(2,1)S(1)}, bf16[4,256,128]{2,1,0:T(8,128)(2,1)S(1)}, u32[]{:S(2)}, u32[]{:S(2)}) collective-permute-start(bf16[4,256,128]{2,1,0:T(8,128)(2,1)S(1)} %copy-done), channel_id=1, source_target_pairs={{0,32},{16,48},{32,64},{48,80},{64,96},{80,112},{96,128},{112,144}... | collective-permute-start | bytes 786440 | tf_op jit(solution)/shard_map/ppermute | solution.py:219
  39.8 1.4 %far_part.5.refs_7_ = f32[4,128,256]{2,1,0:T(8,128)S(1)} custom-call(s32[1]{0:T(128)} %bitcast.odd_ref, bf16[4,256,128]{2,1,0:T(8,128)(2,1)S(1)} %collective-permute-done.2.refs_2_.refs_0_.refs_4_, bf16[4,256,128]{2,1,0:T(8,128)(2,1)S(1)} %collective-permute-done.refs_3_.refs_1_, bf16[4,256,128]{2,1,0:T(8,128)(2,1)S(1)} %collective-permute-done.1.refs_4_.refs_2_.refs_0_, ...), custom_call_target="tpu_custom_call" | custom-call | bytes 1000000 | tf_op jit(solution)/shard_map/far_part/pallas_call | solution.py:105
  41.3 2.2 %collective-permute-start.12 = (bf16[4,256,128]{2,1,0:T(8,128)(2,1)S(1)}, bf16[4,256,128]{2,1,0:T(8,128)(2,1)S(1)}, u32[]{:S(2)}, u32[]{:S(2)}) collective-permute-start(bf16[4,256,128]{2,1,0:T(8,128)(2,1)S(1)} %broadcast_select_fusion.2), channel_id=1, source_target_pairs={{0,16},{16,0},{32,48},{48,32},{64,80},{80,64},{96,112},{112,96},{1... | collective-permute-start | bytes 786440 | tf_op jit(solution)/shard_map/ppermute | solution.py:253
  43.5 1.4 %far_part.6.refs_15_ = f32[4,128,256]{2,1,0:T(8,128)S(1)} custom-call(s32[1]{0:T(128)} %bitcast.odd_ref, bf16[4,256,128]{2,1,0:T(8,128)(2,1)S(1)} %collective-permute-done.1.refs_4_.refs_2_.refs_0_, bf16[4,256,128]{2,1,0:T(8,128)(2,1)S(1)} %collective-permute-done.5.refs_3_.refs_1_.refs_0_, bf16[4,256,128]{2,1,0:T(8,128)(2,1)S(1)} %collective-permute-done.10.refs_2_.refs_1_, ...), custom_call_target="tpu_custom_call" | custom-call | bytes 1000000 | tf_op jit(solution)/shard_map/far_part/pallas_call | solution.py:105
  44.9 3.4 %near_part.3 = (bf16[1,24,128,128]{3,2,1,0:T(8,128)(2,1)}, bf16[1,24,128,128]{3,2,1,0:T(8,128)(2,1)}) custom-call(s32[1]{0:T(128)} %bitcast.odd_ref, bf16[4,256,128]{2,1,0:T(8,128)(2,1)S(1)} %collective-permute-done.14.refs_0_.refs_7_, bf16[4,256,128]{2,1,0:T(8,128)(2,1)S(1)} %collective-permute-done.11.refs_1_.refs_6_, ...), custom_call_target="tpu_custom_call" | custom-call | bytes 1000000 | tf_op jit(solution)/shard_map/near_part/pallas_call | solution.py:166
  49.1 4.0 %far_part.7 = (f32[4,128,256]{2,1,0:T(8,128)S(1)}, f32[4,128,256]{2,1,0:T(8,128)S(1)}, f32[4,128,256]{2,1,0:T(8,128)S(1)}) custom-call(s32[1]{0:T(128)} %bitcast.odd_ref, bf16[4,256,128]{2,1,0:T(8,128)(2,1)S(1)} %collective-permute-done.5.refs_3_.refs_1_.refs_0_, bf16[4,256,128]{2,1,0:T(8,128)(2,1)S(1)} %collective-permute-done.10.refs_2_.refs_1_, ...), custom_call_target="tpu_custom_call" | custom-call | bytes 1000000 | tf_op jit(solution)/shard_map/far_part/pallas_call | solution.py:105
  53.1 3.4 %near_part.4 = (bf16[1,24,128,128]{3,2,1,0:T(8,128)(2,1)}, bf16[1,24,128,128]{3,2,1,0:T(8,128)(2,1)}) custom-call(s32[1]{0:T(128)} %bitcast.odd_ref, bf16[4,256,128]{2,1,0:T(8,128)(2,1)S(1)} %collective-permute-done.8.refs_2_.refs_0_.refs_5_, ...), custom_call_target="tpu_custom_call", output_to_operand_aliasing={{0}: (9, {}), {1}: (10, {})} | custom-call | bytes 1000000 | tf_op jit(solution)/shard_map/near_part/pallas_call | solution.py:166
  56.5 2.1 %collective-permute-done.15.refs_3_ = bf16[4,256,128]{2,1,0:T(8,128)(2,1)S(1)} collective-permute-done((bf16[4,256,128]{2,1,0:T(8,128)(2,1)S(1)}, bf16[4,256,128]{2,1,0:T(8,128)(2,1)S(1)}, u32[]{:S(2)}, u32[]{:S(2)}) %collective-permute-start.15) | collective-permute-done | bytes 262176 | tf_op jit(solution)/shard_map/ppermute | solution.py:253
  58.6 8.8 %near_part.5 = (bf16[1,24,128,128]{3,2,1,0:T(8,128)(2,1)}, bf16[1,24,128,128]{3,2,1,0:T(8,128)(2,1)}) custom-call(s32[1]{0:T(128)} %bitcast.odd_ref, bf16[4,256,128]{2,1,0:T(8,128)(2,1)S(1)} %collective-permute-done.4.refs_4_.refs_2_.refs_0_, ...), custom_call_target="tpu_custom_call", output_to_operand_aliasing={{0}: (20, {}), {1}: (21, {})} | custom-call | bytes 1000000 | tf_op jit(solution)/shard_map/near_part/pallas_call | solution.py:166
  (62 shorter events, 9.3 us)
Async XLA Ops:
  0.6 3.3 %copy-start.8 = (bf16[1,24,128,128]{3,2,1,0:T(8,128)(2,1)S(1)}, bf16[1,24,128,128]{3,2,1,0:T(8,128)(2,1)}, u32[]{:S(2)}) copy-start(bf16[1,24,128,128]{3,2,1,0:T(8,128)(2,1)} %param.5) | copy-start | bytes 2359300
  1.9 2.8 %copy-start.9 = (bf16[1,24,128,128]{3,2,1,0:T(8,128)(2,1)S(1)}, bf16[1,24,128,128]{3,2,1,0:T(8,128)(2,1)}, u32[]{:S(2)}) copy-start(bf16[1,24,128,128]{3,2,1,0:T(8,128)(2,1)} %param.6) | copy-start | bytes 2359300
  2.0 13.1 %collective-permute-start = (bf16[4,256,128]{2,1,0:T(8,128)(2,1)S(1)}, bf16[4,256,128]{2,1,0:T(8,128)(2,1)S(1)}, u32[]{:S(2)}, u32[]{:S(2)}) collective-permute-start(bf16[4,256,128]{2,1,0:T(8,128)(2,1)S(1)} %maximum_select_fusion.refs_6_.refs_11_), channel_id=1, source_target_pairs={{0,32},{16,48},{32,64},{48,80},{64,96},{80,112},{96,128},{112,144}... | collective-permute-start | bytes 786440 | tf_op jit(solution)/shard_map/ppermute | solution.py:212
  6.2 14.6 %collective-permute-start.2 = (bf16[4,256,128]{2,1,0:T(8,128)(2,1)}, bf16[4,256,128]{2,1,0:T(8,128)(2,1)S(1)}, u32[]{:S(2)}, u32[]{:S(2)}) collective-permute-start(bf16[4,256,128]{2,1,0:T(8,128)(2,1)} %maximum_select_fusion.1.refs_5_.refs_12_), channel_id=1, source_target_pairs={{0,32},{16,48},{32,64},{48,80},{64,96},{80,112},{96,128},{112,144}... | collective-permute-start | bytes 786440 | tf_op jit(solution)/shard_map/ppermute | solution.py:219
  9.6 1.3 %copy-start.14 = (bf16[4,128,128]{2,1,0:T(8,128)(2,1)S(1)}, bf16[4,128,128]{2,1,0:T(8,128)(2,1)}, u32[]{:S(2)}) copy-start(bf16[4,128,128]{2,1,0:T(8,128)(2,1)} %get-tuple-element.73) | copy-start | bytes 393220
  15.0 10.4 %collective-permute-start.1 = (bf16[4,256,128]{2,1,0:T(8,128)(2,1)}, bf16[4,256,128]{2,1,0:T(8,128)(2,1)S(1)}, u32[]{:S(2)}, u32[]{:S(2)}) collective-permute-start(bf16[4,256,128]{2,1,0:T(8,128)(2,1)} %pad_maximum_fusion.refs_4_), channel_id=1, source_target_pairs={{0,32},{16,48},{32,64},{48,80},{64,96},{80,112},{96,128},{112,144}... | collective-permute-start | bytes 786440 | tf_op jit(solution)/shard_map/ppermute | solution.py:219
  15.0 1.9 %copy-start.10 = (bf16[4,128,128]{2,1,0:T(8,128)(2,1)S(1)}, bf16[4,128,128]{2,1,0:T(8,128)(2,1)}, u32[]{:S(2)}) copy-start(bf16[4,128,128]{2,1,0:T(8,128)(2,1)} %get-tuple-element.68) | copy-start | bytes 393220
  15.0 1.9 %copy-start.11 = (bf16[4,128,128]{2,1,0:T(8,128)(2,1)S(1)}, bf16[4,128,128]{2,1,0:T(8,128)(2,1)}, u32[]{:S(2)}) copy-start(bf16[4,128,128]{2,1,0:T(8,128)(2,1)} %get-tuple-element.74) | copy-start | bytes 393220
  15.8 10.9 %collective-permute-start.3 = (bf16[4,256,128]{2,1,0:T(8,128)(2,1)}, bf16[4,256,128]{2,1,0:T(8,128)(2,1)S(1)}, u32[]{:S(2)}, u32[]{:S(2)}) collective-permute-start(bf16[4,256,128]{2,1,0:T(8,128)(2,1)} %broadcast_select_fusion.6), channel_id=1, source_target_pairs={{0,16},{16,0},{32,48},{48,32},{64,80},{80,64},{96,112},{112,96},{1... | collective-permute-start | bytes 786440 | tf_op jit(solution)/shard_map/ppermute | solution.py:253
  17.7 8.9 %copy-start.1 = (bf16[4,256,128]{2,1,0:T(8,128)(2,1)S(1)}, bf16[4,256,128]{2,1,0:T(8,128)(2,1)}, u32[]{:S(2)}) copy-start(bf16[4,256,128]{2,1,0:T(8,128)(2,1)} %pad_maximum_fusion.2.refs_9_) | copy-start | bytes 786436
  17.7 14.9 %collective-permute-start.7 = (bf16[4,256,128]{2,1,0:T(8,128)(2,1)S(1)}, bf16[4,256,128]{2,1,0:T(8,128)(2,1)S(1)}, u32[]{:S(2)}, u32[]{:S(2)}) collective-permute-start(bf16[4,256,128]{2,1,0:T(8,128)(2,1)S(1)} %collective-permute-done.refs_3_.refs_1_), channel_id=1, source_target_pairs={{1,2},{2,1},{3,4},{4,3},{5,6},{6,5},{7,8},{8,7},{9,10},{10,9},{11,... | collective-permute-start | bytes 786440 | tf_op jit(solution)/shard_map/ppermute | solution.py:252
  20.8 15.3 %collective-permute-start.5 = (bf16[4,256,128]{2,1,0:T(8,128)(2,1)}, bf16[4,256,128]{2,1,0:T(8,128)(2,1)S(1)}, u32[]{:S(2)}, u32[]{:S(2)}) collective-permute-start(bf16[4,256,128]{2,1,0:T(8,128)(2,1)} %pad_maximum_fusion.1.refs_8_), channel_id=1, source_target_pairs={{0,32},{16,48},{32,64},{48,80},{64,96},{80,112},{96,128},{112,144}... | collective-permute-start | bytes 786440 | tf_op jit(solution)/shard_map/ppermute | solution.py:219
  24.0 4.6 %collective-permute-start.6 = (bf16[4,256,128]{2,1,0:T(8,128)(2,1)S(1)}, bf16[4,256,128]{2,1,0:T(8,128)(2,1)S(1)}, u32[]{:S(2)}, u32[]{:S(2)}) collective-permute-start(bf16[4,256,128]{2,1,0:T(8,128)(2,1)S(1)} %collective-permute-done.2.refs_2_.refs_0_.refs_4_), channel_id=1, source_target_pairs={{0,1},{1,0},{2,3},{3,2},{4,5},{5,4},{6,7},{7,6},{8,9},{9,8},{10,11... | collective-permute-start | bytes 786440 | tf_op jit(solution)/shard_map/ppermute | solution.py:255
  25.4 10.6 %collective-permute-start.8 = (bf16[4,256,128]{2,1,0:T(8,128)(2,1)S(1)}, bf16[4,256,128]{2,1,0:T(8,128)(2,1)S(1)}, u32[]{:S(2)}, u32[]{:S(2)}) collective-permute-start(bf16[4,256,128]{2,1,0:T(8,128)(2,1)S(1)} %broadcast_select_fusion.5), channel_id=1, source_target_pairs={{0,16},{16,0},{32,48},{48,32},{64,80},{80,64},{96,112},{112,96},{1... | collective-permute-start | bytes 786440 | tf_op jit(solution)/shard_map/ppermute | solution.py:253
  26.6 13.0 %collective-permute-start.10 = (bf16[4,256,128]{2,1,0:T(8,128)(2,1)S(1)}, bf16[4,256,128]{2,1,0:T(8,128)(2,1)S(1)}, u32[]{:S(2)}, u32[]{:S(2)}) collective-permute-start(bf16[4,256,128]{2,1,0:T(8,128)(2,1)S(1)} %copy-done.1), channel_id=1, source_target_pairs={{0,32},{16,48},{32,64},{48,80},{64,96},{80,112},{96,128},{112,144}... | collective-permute-start | bytes 786440 | tf_op jit(solution)/shard_map/ppermute | solution.py:219
  28.6 12.6 %collective-permute-start.11 = (bf16[4,256,128]{2,1,0:T(8,128)(2,1)S(1)}, bf16[4,256,128]{2,1,0:T(8,128)(2,1)S(1)}, u32[]{:S(2)}, u32[]{:S(2)}) collective-permute-start(bf16[4,256,128]{2,1,0:T(8,128)(2,1)S(1)} %broadcast_select_fusion), channel_id=1, source_target_pairs={{1,2},{2,1},{3,4},{4,3},{5,6},{6,5},{7,24},{8,23},{9,10},{10,9},{1... | collective-permute-start | bytes 786440 | tf_op jit(solution)/shard_map/ppermute | solution.py:258
  32.6 8.6 %collective-permute-start.4 = (bf16[4,256,128]{2,1,0:T(8,128)(2,1)S(1)}, bf16[4,256,128]{2,1,0:T(8,128)(2,1)S(1)}, u32[]{:S(2)}, u32[]{:S(2)}) collective-permute-start(bf16[4,256,128]{2,1,0:T(8,128)(2,1)S(1)} %broadcast_select_fusion.4), channel_id=1, source_target_pairs={{0,16},{16,0},{32,48},{48,32},{64,80},{80,64},{96,112},{112,96},{1... | collective-permute-start | bytes 786440 | tf_op jit(solution)/shard_map/ppermute | solution.py:253
  34.6 1.5 %copy-start.2 = (bf16[4,256,128]{2,1,0:T(8,128)(2,1)S(1)}, bf16[4,256,128]{2,1,0:T(8,128)(2,1)}, u32[]{:S(2)}) copy-start(bf16[4,256,128]{2,1,0:T(8,128)(2,1)} %pad_maximum_fusion.1.refs_8_) | copy-start | bytes 786436
  36.1 8.8 %collective-permute-start.14 = (bf16[4,256,128]{2,1,0:T(8,128)(2,1)S(1)}, bf16[4,256,128]{2,1,0:T(8,128)(2,1)S(1)}, u32[]{:S(2)}, u32[]{:S(2)}) collective-permute-start(bf16[4,256,128]{2,1,0:T(8,128)(2,1)S(1)} %collective-permute-done.8.refs_2_.refs_0_.refs_5_), channel_id=1, source_target_pairs={{0,1},{1,0},{2,3},{3,2},{4,5},{5,4},{6,7},{7,6},{8,9},{9,8},{10,11... | collective-permute-start | bytes 786440 | tf_op jit(solution)/shard_map/ppermute | solution.py:262
  37.0 11.3 %collective-permute-start.13 = (bf16[4,256,128]{2,1,0:T(8,128)(2,1)S(1)}, bf16[4,256,128]{2,1,0:T(8,128)(2,1)S(1)}, u32[]{:S(2)}, u32[]{:S(2)}) collective-permute-start(bf16[4,256,128]{2,1,0:T(8,128)(2,1)S(1)} %copy-done), channel_id=1, source_target_pairs={{0,32},{16,48},{32,64},{48,80},{64,96},{80,112},{96,128},{112,144}... | collective-permute-start | bytes 786440 | tf_op jit(solution)/shard_map/ppermute | solution.py:219
  39.7 9.2 %collective-permute-start.9 = (bf16[4,256,128]{2,1,0:T(8,128)(2,1)S(1)}, bf16[4,256,128]{2,1,0:T(8,128)(2,1)S(1)}, u32[]{:S(2)}, u32[]{:S(2)}) collective-permute-start(bf16[4,256,128]{2,1,0:T(8,128)(2,1)S(1)} %broadcast_select_fusion.3), channel_id=1, source_target_pairs={{0,16},{16,0},{32,48},{48,32},{64,80},{80,64},{96,112},{112,96},{1... | collective-permute-start | bytes 786440 | tf_op jit(solution)/shard_map/ppermute | solution.py:253
  41.3 3.7 %copy-start.4 = (bf16[128,512]{1,0:T(8,128)(2,1)S(1)}, bf16[128,512]{1,0:T(8,128)(2,1)}, u32[]{:S(2)}) copy-start(bf16[128,512]{1,0:T(8,128)(2,1)} %copy-done.3) | copy-start | bytes 393220
  41.3 15.2 %collective-permute-start.12 = (bf16[4,256,128]{2,1,0:T(8,128)(2,1)S(1)}, bf16[4,256,128]{2,1,0:T(8,128)(2,1)S(1)}, u32[]{:S(2)}, u32[]{:S(2)}) collective-permute-start(bf16[4,256,128]{2,1,0:T(8,128)(2,1)S(1)} %broadcast_select_fusion.2), channel_id=1, source_target_pairs={{0,16},{16,0},{32,48},{48,32},{64,80},{80,64},{96,112},{112,96},{1... | collective-permute-start | bytes 786440 | tf_op jit(solution)/shard_map/ppermute | solution.py:253
  49.0 9.6 %collective-permute-start.15 = (bf16[4,256,128]{2,1,0:T(8,128)(2,1)S(1)}, bf16[4,256,128]{2,1,0:T(8,128)(2,1)S(1)}, u32[]{:S(2)}, u32[]{:S(2)}) collective-permute-start(bf16[4,256,128]{2,1,0:T(8,128)(2,1)S(1)} %broadcast_select_fusion.1), channel_id=1, source_target_pairs={{0,16},{16,0},{32,48},{48,32},{64,80},{80,64},{96,112},{112,96},{1... | collective-permute-start | bytes 786440 | tf_op jit(solution)/shard_map/ppermute | solution.py:253
  (7 other events, 6.5 us)

commit v3 on v2

--- a/solution.py
+++ b/solution.py
@@ -229,8 +229,8 @@
     out, done = None, (far_side[0],)
     parts, halos, source = {}, {}, []
     far_work = {2: [0], 3: [1], 4: [2], 5: [3, 4, 5]}
-    near_work = {4: [0], 5: [1]}
-    rest = [2, 3, 4, 5]
+    near_work = {4: [[0]], 5: [[1, 2]]}
+    rest = [3, 4, 5]
 
     def grouped(sent, side, group):
         sent = sent + [sent[-1]] * (chunks - len(sent))
@@ -268,11 +268,11 @@
             for n, c in enumerate(group):
                 parts[c] = part[n]
             done = (part[-1],)
-        for c in near_work.get(i, []):
-            owns = arranged(own, own[0], own[0])[c + 1 : c + 2]
-            tiles = grouped(near, "near", [c])
+        for group in near_work.get(i, []):
+            owns = arranged(own, own[0], own[0])[group[0] + 1 : group[-1] + 2]
+            tiles = grouped(near, "near", group)
             tiles[2] = tied(tiles[2], *done)
-            out = near_part(odd, tiles, *near_side, owns, [parts[c]], c, shape, out)
+            out = near_part(odd, tiles, *near_side, owns, [parts[c] for c in group], group[0], shape, out)
             done = (out[0],)
     owns = arranged(own, own[0], own[0])[rest[0] + 1 : rest[-1] + 2]
     out = near_part(

time: 67.8 us -> 66.2 us (0.976)
  other arithmetic: 7.5 us -> 5.86 us
  Pallas kernels: 25.1 us -> 26 us
    pallas_call x4, Pallas kernels: 8.24 us -> 11.1 us  [far_part(): pl.pallas_call(functools.partial(far_kernel, layout), out_shape=[jax.Shap...]
    ppermute x6, waiting for transfers between devices: 2.65 us -> 0.13 us  [shards(): near.append(lax.ppermute(source[i], 'kz', swap))]
    pallas_call x3, Pallas kernels: 15.6 us -> 13.6 us  [near_part(): pl.pallas_call(functools.partial(near_kernel, (layout, own_layout)), grid...]
    ppermute x5, waiting for transfers between devices: 0.46 us -> 2.03 us  [shards(): far.append(lax.ppermute(own[i], 'kz', two_on))]
    select_n x6, other arithmetic: 2.81 us -> 1.85 us  [shards(): source.append(jnp.where(even, own[i], far[i]))]
    select_n x2, other arithmetic: 0.83 us -> 0.14 us  [by_lane(): return jnp.where(odd_lane, odd, other)]
    unnamed x30 -> x32, local copies, waits for them, and re-layouts: 1.83 us -> 1.89 us
  transfers between devices with their start and end apart: 16 -> 16, of which waited for: 4 -> 3; matrix products, arithmetic and copies ran while one was open for 13% -> 11% of each run, Pallas kernels for 24% -> 30%
where the time goes in v3:
time: 66.2 us; the launch traced here: 65.8 us
  Pallas kernels  26 us (39%)
  starting transfers between devices  23.2 us (35%)
  other arithmetic  5.86 us (9%)
  waiting for transfers between devices  5.12 us (8%)
  local copies, waits for them, and re-layouts  4.62 us (7%)
  between operations  0.92 us (1%)
    pallas_call x3, Pallas kernels, near_part(): pl.pallas_call(functools.partial(near_kernel, (layout, own_layout)), grid...  13.6 us
    pallas_call x4, Pallas kernels, far_part(): pl.pallas_call(functools.partial(far_kernel, layout), out_shape=[jax.Shap...  11.1 us
    ppermute x6, starting transfers between devices, shards(): near.append(lax.ppermute(source[i], 'kz', swap))  7.53 us
    ppermute x5, starting transfers between devices, shards(): far.append(lax.ppermute(own[i], 'kz', two_on))  7.24 us
    ppermute x1, starting transfers between devices, shards(): halos['near', 'outer'] = lax.ppermute(edge, both, outer_turned)  3.3 us
    ppermute x1, starting transfers between devices, shards(): halos['far', 'outer'] = lax.ppermute(far[0], 'en', outer)  3.06 us
    ppermute x1, waiting for transfers between devices, shards(): far, near = ([lax.ppermute(own[0], 'kz', two_on)], [])  2.95 us
    concatenate x4, other arithmetic, cut(): return jnp.concatenate([real[0, energies], imag[0, energies]], axis=1)  2.87 us
  transfers between devices with their start and end apart: 16, of which 3 were waited for; matrix products, arithmetic and copies ran while one was open for 11% of the time, Pallas kernels for 30%

profile of v3, /device:TPU:4, one launch (start us, length us, event | category | flops | bytes accessed | tf_op | source)
XLA Modules:
  0.0 65.8 jit_solution(5271367434572337227)
XLA Ops:
  0.7 1.2 %slice_bitcast_fusion.12 = (bf16[4,128,128]{2,1,0:T(8,128)(2,1)S(1)}, bf16[4,128,128]{2,1,0:T(8,128)(2,1)S(1)}, bf16[4,128,128]{2,1,0:T(8,128)(2,1)S(1)}, bf16[4,128,128]{2,1,0:T(8,128)(2,1)S(1)}) fusion(bf16[1,24,128,128]{3,2,1,0:T(8,128)(2,1)} %param.6, bf16[1,24,128,128]{3,2,1,0:T(8,128)(2,1)} %param.5), kind=kLoop, calls=%fused_computation.25 | loop fusion | bytes 1048576 | tf_op jit(solution)/shard_map/squeeze | solution.py:208
  2.0 2.0 %collective-permute-start.2 = (bf16[4,256,128]{2,1,0:T(8,128)(2,1)S(1)}, bf16[4,256,128]{2,1,0:T(8,128)(2,1)S(1)}, u32[]{:S(2)}, u32[]{:S(2)}) collective-permute-start(bf16[4,256,128]{2,1,0:T(8,128)(2,1)S(1)} %maximum_select_fusion.refs_6_.refs_9_), channel_id=1, source_target_pairs={{0,32},{16,48},{32,64},{48,80},{64,96},{80,112},{96,128},{112,144}... | collective-permute-start | bytes 786440 | tf_op jit(solution)/shard_map/ppermute | solution.py:212
  5.6 2.0 %collective-permute-start = (bf16[4,256,128]{2,1,0:T(8,128)(2,1)S(1)}, bf16[4,256,128]{2,1,0:T(8,128)(2,1)S(1)}, u32[]{:S(2)}, u32[]{:S(2)}) collective-permute-start(bf16[4,256,128]{2,1,0:T(8,128)(2,1)S(1)} %maximum_select_fusion.1.refs_5_.refs_10_), channel_id=1, source_target_pairs={{0,32},{16,48},{32,64},{48,80},{64,96},{80,112},{96,128},{112,144}... | collective-permute-start | bytes 786440 | tf_op jit(solution)/shard_map/ppermute | solution.py:219
  9.0 1.2 %prepare.1 = (bf16[1024,512]{1,0:T(8,128)(2,1)S(1)}, bf16[128,512]{1,0:T(8,128)(2,1)S(1)}, bf16[1024,512]{1,0:T(8,128)(2,1)S(1)}, bf16[128,512]{1,0:T(8,128)(2,1)S(1)}) custom-call(s32[2,8]{1,0:T(2,128)S(1)} %copy-done.7, f32[2,4,8]{2,1,0:T(4,128)S(1)} %copy-done.6, bf16[2,4,1,128,128]{4,3,2,1,0:T(8,128)(2,1)S(1)} %copy-done.5), custom_call_target="tpu_custom_call" | custom-call | bytes 1000000 | tf_op jit(solution)/shard_map/prepare/pallas_call | solution.py:43
  12.1 2.9 %collective-permute-done.2.refs_3_.refs_1_ = bf16[4,256,128]{2,1,0:T(8,128)(2,1)S(1)} collective-permute-done((bf16[4,256,128]{2,1,0:T(8,128)(2,1)S(1)}, bf16[4,256,128]{2,1,0:T(8,128)(2,1)S(1)}, u32[]{:S(2)}, u32[]{:S(2)}) %collective-permute-start.2) | collective-permute-done | bytes 262176 | tf_op jit(solution)/shard_map/ppermute | solution.py:212
  15.8 1.2 %collective-permute-start.6 = (bf16[4,256,128]{2,1,0:T(8,128)(2,1)}, bf16[4,256,128]{2,1,0:T(8,128)(2,1)S(1)}, u32[]{:S(2)}, u32[]{:S(2)}) collective-permute-start(bf16[4,256,128]{2,1,0:T(8,128)(2,1)} %broadcast_select_fusion.6), channel_id=1, source_target_pairs={{0,16},{16,0},{32,48},{48,32},{64,80},{80,64},{96,112},{112,96},{1... | collective-permute-start | bytes 786440 | tf_op jit(solution)/shard_map/ppermute | solution.py:253
  17.7 3.1 %collective-permute-start.4 = (bf16[4,256,128]{2,1,0:T(8,128)(2,1)S(1)}, bf16[4,256,128]{2,1,0:T(8,128)(2,1)S(1)}, u32[]{:S(2)}, u32[]{:S(2)}) collective-permute-start(bf16[4,256,128]{2,1,0:T(8,128)(2,1)S(1)} %collective-permute-done.2.refs_3_.refs_1_), channel_id=1, source_target_pairs={{1,2},{2,1},{3,4},{4,3},{5,6},{6,5},{7,8},{8,7},{9,10},{10,9},{11,... | collective-permute-start | bytes 786440 | tf_op jit(solution)/shard_map/ppermute | solution.py:252
  20.8 2.7 %collective-permute-start.1 = (bf16[4,256,128]{2,1,0:T(8,128)(2,1)}, bf16[4,256,128]{2,1,0:T(8,128)(2,1)S(1)}, u32[]{:S(2)}, u32[]{:S(2)}) collective-permute-start(bf16[4,256,128]{2,1,0:T(8,128)(2,1)} %pad_maximum_fusion.refs_6_), channel_id=1, source_target_pairs={{0,32},{16,48},{32,64},{48,80},{64,96},{80,112},{96,128},{112,144}... | collective-permute-start | bytes 786440 | tf_op jit(solution)/shard_map/ppermute | solution.py:219
  23.5 2.0 %collective-permute-done.5.refs_4_.refs_2_.refs_0_ = bf16[4,256,128]{2,1,0:T(8,128)(2,1)} collective-permute-done((bf16[4,256,128]{2,1,0:T(8,128)(2,1)}, bf16[4,256,128]{2,1,0:T(8,128)(2,1)}, u32[]{:S(2)}, u32[]{:S(2)}) %collective-permute-start.5) | collective-permute-done | bytes 262176 | tf_op jit(solution)/shard_map/ppermute | solution.py:219
  25.5 1.2 %collective-permute-start.7 = (bf16[4,256,128]{2,1,0:T(8,128)(2,1)S(1)}, bf16[4,256,128]{2,1,0:T(8,128)(2,1)S(1)}, u32[]{:S(2)}, u32[]{:S(2)}) collective-permute-start(bf16[4,256,128]{2,1,0:T(8,128)(2,1)S(1)} %broadcast_select_fusion.5), channel_id=1, source_target_pairs={{0,16},{16,0},{32,48},{48,32},{64,80},{80,64},{96,112},{112,96},{1... | collective-permute-start | bytes 786440 | tf_op jit(solution)/shard_map/ppermute | solution.py:253
  26.7 1.0 %broadcast_select_fusion.4 = bf16[4,256,128]{2,1,0:T(8,128)(2,1)S(1)} fusion(bf16[4,256,128]{2,1,0:T(8,128)(2,1)} %pad_maximum_fusion.1.refs_5_, bf16[4,256,128]{2,1,0:T(8,128)(2,1)} %collective-permute-done.5.refs_4_.refs_2_.refs_0_, pred[]{:T(512)S(6)} %eq.16), kind=kLoop, calls=%fused_computation.10 | loop fusion | flops 131072 | bytes 786433 | tf_op jit(solution)/shard_map/jit(_where)/select_n | solution.py:249
  28.7 3.3 %collective-permute-start.11 = (bf16[4,256,128]{2,1,0:T(8,128)(2,1)S(1)}, bf16[4,256,128]{2,1,0:T(8,128)(2,1)S(1)}, u32[]{:S(2)}, u32[]{:S(2)}) collective-permute-start(bf16[4,256,128]{2,1,0:T(8,128)(2,1)S(1)} %broadcast_select_fusion), channel_id=1, source_target_pairs={{1,2},{2,1},{3,4},{4,3},{5,6},{6,5},{7,24},{8,23},{9,10},{10,9},{1... | collective-permute-start | bytes 786440 | tf_op jit(solution)/shard_map/ppermute | solution.py:258
  32.1 1.7 %collective-permute-start.10 = (bf16[4,256,128]{2,1,0:T(8,128)(2,1)S(1)}, bf16[4,256,128]{2,1,0:T(8,128)(2,1)S(1)}, u32[]{:S(2)}, u32[]{:S(2)}) collective-permute-start(bf16[4,256,128]{2,1,0:T(8,128)(2,1)S(1)} %broadcast_select_fusion.4), channel_id=1, source_target_pairs={{0,16},{16,0},{32,48},{48,32},{64,80},{80,64},{96,112},{112,96},{1... | collective-permute-start | bytes 786440 | tf_op jit(solution)/shard_map/ppermute | solution.py:253
  33.8 2.4 %far_part.4.refs_9_ = f32[4,128,256]{2,1,0:T(8,128)S(1)} custom-call(s32[1]{0:T(128)} %bitcast.odd_ref, bf16[4,256,128]{2,1,0:T(8,128)(2,1)S(1)} %collective-permute-done.3.refs_0_.refs_6_, bf16[4,256,128]{2,1,0:T(8,128)(2,1)S(1)} %collective-permute-done.4.refs_1_.refs_5_, bf16[4,256,128]{2,1,0:T(8,128)(2,1)S(1)} %collective-permute-done.refs_2_.refs_0_.refs_4_, ...), custom_call_target="tpu_custom_call" | custom-call | bytes 1000000 | tf_op jit(solution)/shard_map/far_part/pallas_call | solution.py:105
  37.2 2.5 %collective-permute-start.13 = (bf16[4,256,128]{2,1,0:T(8,128)(2,1)S(1)}, bf16[4,256,128]{2,1,0:T(8,128)(2,1)S(1)}, u32[]{:S(2)}, u32[]{:S(2)}) collective-permute-start(bf16[4,256,128]{2,1,0:T(8,128)(2,1)S(1)} %copy-done), channel_id=1, source_target_pairs={{0,32},{16,48},{32,64},{48,80},{64,96},{80,112},{96,128},{112,144}... | collective-permute-start | bytes 786440 | tf_op jit(solution)/shard_map/ppermute | solution.py:219
  39.7 1.0 %collective-permute-start.8 = (bf16[4,256,128]{2,1,0:T(8,128)(2,1)S(1)}, bf16[4,256,128]{2,1,0:T(8,128)(2,1)S(1)}, u32[]{:S(2)}, u32[]{:S(2)}) collective-permute-start(bf16[4,256,128]{2,1,0:T(8,128)(2,1)S(1)} %broadcast_select_fusion.3), channel_id=1, source_target_pairs={{0,16},{16,0},{32,48},{48,32},{64,80},{80,64},{96,112},{112,96},{1... | collective-permute-start | bytes 786440 | tf_op jit(solution)/shard_map/ppermute | solution.py:253
  40.8 2.4 %far_part.5.refs_9_ = f32[4,128,256]{2,1,0:T(8,128)S(1)} custom-call(s32[1]{0:T(128)} %bitcast.odd_ref, bf16[4,256,128]{2,1,0:T(8,128)(2,1)S(1)} %collective-permute-done.refs_2_.refs_0_.refs_4_, bf16[4,256,128]{2,1,0:T(8,128)(2,1)S(1)} %collective-permute-done.2.refs_3_.refs_1_, bf16[4,256,128]{2,1,0:T(8,128)(2,1)} %collective-permute-done.5.refs_4_.refs_2_.refs_0_, ...), custom_call_target="tpu_custom_call" | custom-call | bytes 1000000 | tf_op jit(solution)/shard_map/far_part/pallas_call | solution.py:105
  43.2 1.3 %collective-permute-start.12 = (bf16[4,256,128]{2,1,0:T(8,128)(2,1)S(1)}, bf16[4,256,128]{2,1,0:T(8,128)(2,1)S(1)}, u32[]{:S(2)}, u32[]{:S(2)}) collective-permute-start(bf16[4,256,128]{2,1,0:T(8,128)(2,1)S(1)} %broadcast_select_fusion.2), channel_id=1, source_target_pairs={{0,16},{16,0},{32,48},{48,32},{64,80},{80,64},{96,112},{112,96},{1... | collective-permute-start | bytes 786440 | tf_op jit(solution)/shard_map/ppermute | solution.py:253
  44.5 2.4 %far_part.6.refs_10_ = f32[4,128,256]{2,1,0:T(8,128)S(1)} custom-call(s32[1]{0:T(128)} %bitcast.odd_ref, bf16[4,256,128]{2,1,0:T(8,128)(2,1)} %collective-permute-done.5.refs_4_.refs_2_.refs_0_, bf16[4,256,128]{2,1,0:T(8,128)(2,1)S(1)} %collective-permute-done.1.refs_3_.refs_1_.refs_0_, bf16[4,256,128]{2,1,0:T(8,128)(2,1)S(1)} %collective-permute-done.9.refs_2_.refs_1_, ...), custom_call_target="tpu_custom_call" | custom-call | bytes 1000000 | tf_op jit(solution)/shard_map/far_part/pallas_call | solution.py:105
  46.9 2.5 %near_part.3 = (bf16[1,24,128,128]{3,2,1,0:T(8,128)(2,1)}, bf16[1,24,128,128]{3,2,1,0:T(8,128)(2,1)}) custom-call(s32[1]{0:T(128)} %bitcast.odd_ref, bf16[4,256,128]{2,1,0:T(8,128)(2,1)S(1)} %collective-permute-done.14.refs_0_.refs_6_, bf16[4,256,128]{2,1,0:T(8,128)(2,1)S(1)} %collective-permute-done.11.refs_1_.refs_5_, ...), custom_call_target="tpu_custom_call" | custom-call | bytes 1000000 | tf_op jit(solution)/shard_map/near_part/pallas_call | solution.py:166
  49.4 1.1 %collective-permute-start.15 = (bf16[4,256,128]{2,1,0:T(8,128)(2,1)S(1)}, bf16[4,256,128]{2,1,0:T(8,128)(2,1)S(1)}, u32[]{:S(2)}, u32[]{:S(2)}) collective-permute-start(bf16[4,256,128]{2,1,0:T(8,128)(2,1)S(1)} %broadcast_select_fusion.1), channel_id=1, source_target_pairs={{0,16},{16,0},{32,48},{48,32},{64,80},{80,64},{96,112},{112,96},{1... | collective-permute-start | bytes 786440 | tf_op jit(solution)/shard_map/ppermute | solution.py:253
  50.5 4.0 %far_part.7 = (f32[4,128,256]{2,1,0:T(8,128)S(1)}, f32[4,128,256]{2,1,0:T(8,128)S(1)}, f32[4,128,256]{2,1,0:T(8,128)S(1)}) custom-call(s32[1]{0:T(128)} %bitcast.odd_ref, bf16[4,256,128]{2,1,0:T(8,128)(2,1)S(1)} %collective-permute-done.1.refs_3_.refs_1_.refs_0_, bf16[4,256,128]{2,1,0:T(8,128)(2,1)S(1)} %collective-permute-done.9.refs_2_.refs_1_, ...), custom_call_target="tpu_custom_call" | custom-call | bytes 1000000 | tf_op jit(solution)/shard_map/far_part/pallas_call | solution.py:105
  54.6 5.2 %near_part.4 = (bf16[1,24,128,128]{3,2,1,0:T(8,128)(2,1)}, bf16[1,24,128,128]{3,2,1,0:T(8,128)(2,1)}) custom-call(s32[1]{0:T(128)} %bitcast.odd_ref, bf16[4,256,128]{2,1,0:T(8,128)(2,1)S(1)} %collective-permute-done.7.refs_2_.refs_0_.refs_4_, ...), custom_call_target="tpu_custom_call", output_to_operand_aliasing={{0}: (12, {}), {1}: (13, {})} | custom-call | bytes 1000000 | tf_op jit(solution)/shard_map/near_part/pallas_call | solution.py:166
  59.7 6.0 %near_part.5 = (bf16[1,24,128,128]{3,2,1,0:T(8,128)(2,1)}, bf16[1,24,128,128]{3,2,1,0:T(8,128)(2,1)}) custom-call(s32[1]{0:T(128)} %bitcast.odd_ref, bf16[4,256,128]{2,1,0:T(8,128)(2,1)S(1)} %collective-permute-done.8.refs_3_.refs_0_, ...), custom_call_target="tpu_custom_call", output_to_operand_aliasing={{0}: (17, {}), {1}: (18, {})} | custom-call | bytes 1000000 | tf_op jit(solution)/shard_map/near_part/pallas_call | solution.py:166
  (64 shorter events, 8.5 us)
Async XLA Ops:
  0.6 3.3 %copy-start.8 = (bf16[1,24,128,128]{3,2,1,0:T(8,128)(2,1)S(1)}, bf16[1,24,128,128]{3,2,1,0:T(8,128)(2,1)}, u32[]{:S(2)}) copy-start(bf16[1,24,128,128]{3,2,1,0:T(8,128)(2,1)} %param.5) | copy-start | bytes 2359300
  1.9 2.8 %copy-start.9 = (bf16[1,24,128,128]{3,2,1,0:T(8,128)(2,1)S(1)}, bf16[1,24,128,128]{3,2,1,0:T(8,128)(2,1)}, u32[]{:S(2)}) copy-start(bf16[1,24,128,128]{3,2,1,0:T(8,128)(2,1)} %param.6) | copy-start | bytes 2359300
  2.0 13.1 %collective-permute-start.2 = (bf16[4,256,128]{2,1,0:T(8,128)(2,1)S(1)}, bf16[4,256,128]{2,1,0:T(8,128)(2,1)S(1)}, u32[]{:S(2)}, u32[]{:S(2)}) collective-permute-start(bf16[4,256,128]{2,1,0:T(8,128)(2,1)S(1)} %maximum_select_fusion.refs_6_.refs_9_), channel_id=1, source_target_pairs={{0,32},{16,48},{32,64},{48,80},{64,96},{80,112},{96,128},{112,144}... | collective-permute-start | bytes 786440 | tf_op jit(solution)/shard_map/ppermute | solution.py:212
  5.6 15.2 %collective-permute-start = (bf16[4,256,128]{2,1,0:T(8,128)(2,1)S(1)}, bf16[4,256,128]{2,1,0:T(8,128)(2,1)S(1)}, u32[]{:S(2)}, u32[]{:S(2)}) collective-permute-start(bf16[4,256,128]{2,1,0:T(8,128)(2,1)S(1)} %maximum_select_fusion.1.refs_5_.refs_10_), channel_id=1, source_target_pairs={{0,32},{16,48},{32,64},{48,80},{64,96},{80,112},{96,128},{112,144}... | collective-permute-start | bytes 786440 | tf_op jit(solution)/shard_map/ppermute | solution.py:219
  9.0 1.3 %copy-start.15 = (bf16[4,128,128]{2,1,0:T(8,128)(2,1)S(1)}, bf16[4,128,128]{2,1,0:T(8,128)(2,1)}, u32[]{:S(2)}) copy-start(bf16[4,128,128]{2,1,0:T(8,128)(2,1)} %get-tuple-element.73) | copy-start | bytes 393220
  15.0 10.5 %collective-permute-start.5 = (bf16[4,256,128]{2,1,0:T(8,128)(2,1)}, bf16[4,256,128]{2,1,0:T(8,128)(2,1)}, u32[]{:S(2)}, u32[]{:S(2)}) collective-permute-start(bf16[4,256,128]{2,1,0:T(8,128)(2,1)} %pad_maximum_fusion.1.refs_5_), channel_id=1, source_target_pairs={{0,32},{16,48},{32,64},{48,80},{64,96},{80,112},{96,128},{112,144}... | collective-permute-start | bytes 786440 | tf_op jit(solution)/shard_map/ppermute | solution.py:219
  15.0 1.9 %copy-start.10 = (bf16[4,128,128]{2,1,0:T(8,128)(2,1)S(1)}, bf16[4,128,128]{2,1,0:T(8,128)(2,1)}, u32[]{:S(2)}) copy-start(bf16[4,128,128]{2,1,0:T(8,128)(2,1)} %get-tuple-element.71) | copy-start | bytes 393220
  15.0 1.9 %copy-start.11 = (bf16[4,128,128]{2,1,0:T(8,128)(2,1)S(1)}, bf16[4,128,128]{2,1,0:T(8,128)(2,1)}, u32[]{:S(2)}) copy-start(bf16[4,128,128]{2,1,0:T(8,128)(2,1)} %get-tuple-element.77) | copy-start | bytes 393220
  15.8 11.0 %collective-permute-start.6 = (bf16[4,256,128]{2,1,0:T(8,128)(2,1)}, bf16[4,256,128]{2,1,0:T(8,128)(2,1)S(1)}, u32[]{:S(2)}, u32[]{:S(2)}) collective-permute-start(bf16[4,256,128]{2,1,0:T(8,128)(2,1)} %broadcast_select_fusion.6), channel_id=1, source_target_pairs={{0,16},{16,0},{32,48},{48,32},{64,80},{80,64},{96,112},{112,96},{1... | collective-permute-start | bytes 786440 | tf_op jit(solution)/shard_map/ppermute | solution.py:253
  17.7 9.1 %copy-start.1 = (bf16[4,256,128]{2,1,0:T(8,128)(2,1)S(1)}, bf16[4,256,128]{2,1,0:T(8,128)(2,1)}, u32[]{:S(2)}) copy-start(bf16[4,256,128]{2,1,0:T(8,128)(2,1)} %pad_maximum_fusion.2.refs_7_) | copy-start | bytes 786436
  17.7 14.4 %collective-permute-start.4 = (bf16[4,256,128]{2,1,0:T(8,128)(2,1)S(1)}, bf16[4,256,128]{2,1,0:T(8,128)(2,1)S(1)}, u32[]{:S(2)}, u32[]{:S(2)}) collective-permute-start(bf16[4,256,128]{2,1,0:T(8,128)(2,1)S(1)} %collective-permute-done.2.refs_3_.refs_1_), channel_id=1, source_target_pairs={{1,2},{2,1},{3,4},{4,3},{5,6},{6,5},{7,8},{8,7},{9,10},{10,9},{11,... | collective-permute-start | bytes 786440 | tf_op jit(solution)/shard_map/ppermute | solution.py:252
  20.8 15.5 %collective-permute-start.1 = (bf16[4,256,128]{2,1,0:T(8,128)(2,1)}, bf16[4,256,128]{2,1,0:T(8,128)(2,1)S(1)}, u32[]{:S(2)}, u32[]{:S(2)}) collective-permute-start(bf16[4,256,128]{2,1,0:T(8,128)(2,1)} %pad_maximum_fusion.refs_6_), channel_id=1, source_target_pairs={{0,32},{16,48},{32,64},{48,80},{64,96},{80,112},{96,128},{112,144}... | collective-permute-start | bytes 786440 | tf_op jit(solution)/shard_map/ppermute | solution.py:219
  23.5 5.3 %collective-permute-start.3 = (bf16[4,256,128]{2,1,0:T(8,128)(2,1)S(1)}, bf16[4,256,128]{2,1,0:T(8,128)(2,1)S(1)}, u32[]{:S(2)}, u32[]{:S(2)}) collective-permute-start(bf16[4,256,128]{2,1,0:T(8,128)(2,1)S(1)} %collective-permute-done.refs_2_.refs_0_.refs_4_), channel_id=1, source_target_pairs={{0,1},{1,0},{2,3},{3,2},{4,5},{5,4},{6,7},{7,6},{8,9},{9,8},{10,11... | collective-permute-start | bytes 786440 | tf_op jit(solution)/shard_map/ppermute | solution.py:255
  25.5 10.7 %collective-permute-start.7 = (bf16[4,256,128]{2,1,0:T(8,128)(2,1)S(1)}, bf16[4,256,128]{2,1,0:T(8,128)(2,1)S(1)}, u32[]{:S(2)}, u32[]{:S(2)}) collective-permute-start(bf16[4,256,128]{2,1,0:T(8,128)(2,1)S(1)} %broadcast_select_fusion.5), channel_id=1, source_target_pairs={{0,16},{16,0},{32,48},{48,32},{64,80},{80,64},{96,112},{112,96},{1... | collective-permute-start | bytes 786440 | tf_op jit(solution)/shard_map/ppermute | solution.py:253
  26.7 13.0 %collective-permute-start.9 = (bf16[4,256,128]{2,1,0:T(8,128)(2,1)S(1)}, bf16[4,256,128]{2,1,0:T(8,128)(2,1)S(1)}, u32[]{:S(2)}, u32[]{:S(2)}) collective-permute-start(bf16[4,256,128]{2,1,0:T(8,128)(2,1)S(1)} %copy-done.1), channel_id=1, source_target_pairs={{0,32},{16,48},{32,64},{48,80},{64,96},{80,112},{96,128},{112,144}... | collective-permute-start | bytes 786440 | tf_op jit(solution)/shard_map/ppermute | solution.py:219
  28.7 14.4 %collective-permute-start.11 = (bf16[4,256,128]{2,1,0:T(8,128)(2,1)S(1)}, bf16[4,256,128]{2,1,0:T(8,128)(2,1)S(1)}, u32[]{:S(2)}, u32[]{:S(2)}) collective-permute-start(bf16[4,256,128]{2,1,0:T(8,128)(2,1)S(1)} %broadcast_select_fusion), channel_id=1, source_target_pairs={{1,2},{2,1},{3,4},{4,3},{5,6},{6,5},{7,24},{8,23},{9,10},{10,9},{1... | collective-permute-start | bytes 786440 | tf_op jit(solution)/shard_map/ppermute | solution.py:258
  32.1 11.1 %collective-permute-start.10 = (bf16[4,256,128]{2,1,0:T(8,128)(2,1)S(1)}, bf16[4,256,128]{2,1,0:T(8,128)(2,1)S(1)}, u32[]{:S(2)}, u32[]{:S(2)}) collective-permute-start(bf16[4,256,128]{2,1,0:T(8,128)(2,1)S(1)} %broadcast_select_fusion.4), channel_id=1, source_target_pairs={{0,16},{16,0},{32,48},{48,32},{64,80},{80,64},{96,112},{112,96},{1... | collective-permute-start | bytes 786440 | tf_op jit(solution)/shard_map/ppermute | solution.py:253
  33.8 2.5 %copy-start.2 = (bf16[4,256,128]{2,1,0:T(8,128)(2,1)S(1)}, bf16[4,256,128]{2,1,0:T(8,128)(2,1)}, u32[]{:S(2)}) copy-start(bf16[4,256,128]{2,1,0:T(8,128)(2,1)} %pad_maximum_fusion.refs_6_) | copy-start | bytes 786436
  36.3 10.6 %collective-permute-start.14 = (bf16[4,256,128]{2,1,0:T(8,128)(2,1)S(1)}, bf16[4,256,128]{2,1,0:T(8,128)(2,1)S(1)}, u32[]{:S(2)}, u32[]{:S(2)}) collective-permute-start(bf16[4,256,128]{2,1,0:T(8,128)(2,1)S(1)} %collective-permute-done.7.refs_2_.refs_0_.refs_4_), channel_id=1, source_target_pairs={{0,1},{1,0},{2,3},{3,2},{4,5},{5,4},{6,7},{7,6},{8,9},{9,8},{10,11... | collective-permute-start | bytes 786440 | tf_op jit(solution)/shard_map/ppermute | solution.py:262
  37.2 12.2 %collective-permute-start.13 = (bf16[4,256,128]{2,1,0:T(8,128)(2,1)S(1)}, bf16[4,256,128]{2,1,0:T(8,128)(2,1)S(1)}, u32[]{:S(2)}, u32[]{:S(2)}) collective-permute-start(bf16[4,256,128]{2,1,0:T(8,128)(2,1)S(1)} %copy-done), channel_id=1, source_target_pairs={{0,32},{16,48},{32,64},{48,80},{64,96},{80,112},{96,128},{112,144}... | collective-permute-start | bytes 786440 | tf_op jit(solution)/shard_map/ppermute | solution.py:219
  39.7 9.6 %collective-permute-start.8 = (bf16[4,256,128]{2,1,0:T(8,128)(2,1)S(1)}, bf16[4,256,128]{2,1,0:T(8,128)(2,1)S(1)}, u32[]{:S(2)}, u32[]{:S(2)}) collective-permute-start(bf16[4,256,128]{2,1,0:T(8,128)(2,1)S(1)} %broadcast_select_fusion.3), channel_id=1, source_target_pairs={{0,16},{16,0},{32,48},{48,32},{64,80},{80,64},{96,112},{112,96},{1... | collective-permute-start | bytes 786440 | tf_op jit(solution)/shard_map/ppermute | solution.py:253
  43.2 3.7 %copy-start.4 = (bf16[128,512]{1,0:T(8,128)(2,1)S(1)}, bf16[128,512]{1,0:T(8,128)(2,1)}, u32[]{:S(2)}) copy-start(bf16[128,512]{1,0:T(8,128)(2,1)} %copy-done.3) | copy-start | bytes 393220
  43.2 11.4 %collective-permute-start.12 = (bf16[4,256,128]{2,1,0:T(8,128)(2,1)S(1)}, bf16[4,256,128]{2,1,0:T(8,128)(2,1)S(1)}, u32[]{:S(2)}, u32[]{:S(2)}) collective-permute-start(bf16[4,256,128]{2,1,0:T(8,128)(2,1)S(1)} %broadcast_select_fusion.2), channel_id=1, source_target_pairs={{0,16},{16,0},{32,48},{48,32},{64,80},{80,64},{96,112},{112,96},{1... | collective-permute-start | bytes 786440 | tf_op jit(solution)/shard_map/ppermute | solution.py:253
  49.4 10.4 %collective-permute-start.15 = (bf16[4,256,128]{2,1,0:T(8,128)(2,1)S(1)}, bf16[4,256,128]{2,1,0:T(8,128)(2,1)S(1)}, u32[]{:S(2)}, u32[]{:S(2)}) collective-permute-start(bf16[4,256,128]{2,1,0:T(8,128)(2,1)S(1)} %broadcast_select_fusion.1), channel_id=1, source_target_pairs={{0,16},{16,0},{32,48},{48,32},{64,80},{80,64},{96,112},{112,96},{1... | collective-permute-start | bytes 786440 | tf_op jit(solution)/shard_map/ppermute | solution.py:253
  (8 other events, 7.6 us)

commit v4 on v3

--- a/solution.py
+++ b/solution.py
@@ -23,37 +23,33 @@
 FREE = pl.CostEstimate(flops=0, bytes_accessed=10**6, transcendentals=0)
 
 
-def prepare_kernel(offsets_ref, strengths_ref, coupling_ref, *outs):
+def prepare_kernel(s, offsets_ref, strengths_ref, coupling_ref, weights_ref, joined_ref):
     no = coupling_ref.shape[-1]
-    for s in range(HOPS):
-        weights_ref, joined_ref = outs[2 * s : 2 * s + 2]
-        for n in range(BRANCHES):
-            matrix = coupling_ref[s, n, 0]
-            joined_ref[:, n * no : (n + 1) * no] = matrix
-            turned = matrix.astype(F32).T
-            for i in range(WINDOW):
-                w = offsets_ref[s, i]
-                j = jnp.where(w > 0, REACH - w, REACH - 1 - w)
-                rows = pl.ds(pl.multiple_of(j * no, no), no)
-                weights_ref[rows, n * no : (n + 1) * no] = (strengths_ref[s, n, i] * turned).astype(BF16)
-
-
-def prepare(coupling, strengths, offsets):
+    for n in range(BRANCHES):
+        matrix = coupling_ref[s, n, 0]
+        joined_ref[:, n * no : (n + 1) * no] = matrix
+        turned = matrix.astype(F32).T
+        for i in range(WINDOW):
+            w = offsets_ref[s, i]
+            j = jnp.where(w > 0, REACH - w, REACH - 1 - w)
+            rows = pl.ds(pl.multiple_of(j * no, no), no)
+            weights_ref[rows, n * no : (n + 1) * no] = (strengths_ref[s, n, i] * turned).astype(BF16)
+
+
+def prepare(s, coupling, strengths, offsets):
     no = coupling.shape[-1]
-    outs = pl.pallas_call(
-        prepare_kernel,
+    return pl.pallas_call(
+        functools.partial(prepare_kernel, s),
         out_shape=[
             jax.ShapeDtypeStruct((WINDOW * no, BRANCHES * no), BF16),
             jax.ShapeDtypeStruct((no, BRANCHES * no), BF16),
-        ]
-        * HOPS,
+        ],
         in_specs=[SCALARS, SCALARS, WHOLE],
-        out_specs=[WHOLE] * (2 * HOPS),
+        out_specs=[WHOLE] * 2,
         compiler_params=pltpu.CompilerParams(vmem_limit_bytes=VMEM_LIMIT),
         cost_estimate=FREE,
         name="prepare",
     )(offsets, strengths, coupling)
-    return outs[:2], outs[2:]
 
 
 def hop_terms(odd_ref, tiles, first, weights_ref, joined_ref):
@@ -217,7 +213,7 @@
         if i >= AHEAD:
             own[i] = tied(own[i], far[i - AHEAD])
         far.append(lax.ppermute(own[i], "kz", two_on))
-    near_side, far_side = prepare(coupling, strengths, offsets)
+    near_side = prepare(0, coupling, strengths, offsets)
 
     def arranged(sent, outer_halo, inner_halo):
         below, first = (inner_halo, outer_halo), (sent[1], sent[0])
@@ -226,7 +222,7 @@
 
     shape = green_real.shape
     odd = odd_lane.astype(jnp.int32).reshape(1)
-    out, done = None, (far_side[0],)
+    out, done = None, (near_side[0],)
     parts, halos, source = {}, {}, []
     far_work = {2: [0], 3: [1], 4: [2], 5: [3, 4, 5]}
     near_work = {4: [[0]], 5: [[1, 2]]}
@@ -249,6 +245,8 @@
         source.append(jnp.where(even, own[i], far[i]))
         gate = [source[i]]
         if i == 0:
+            far_side = prepare(1, tied(coupling, source[0]), strengths, offsets)
+            gate.append(far_side[0])
             halos["far", "outer"] = lax.ppermute(far[0], "en", outer)
         near.append(lax.ppermute(source[i], "kz", swap))
         if i == 1:

time: 66.2 us -> 64.8 us (0.979)
  waiting for transfers between devices: 5.12 us -> 11.5 us
  Pallas kernels: 26 us -> 22.8 us
  other arithmetic: 5.86 us -> 2.8 us
  starting transfers between devices: 23.2 us -> 22 us
    pallas_call x4, Pallas kernels: 11.1 us -> 8.26 us  [far_part(): pl.pallas_call(functools.partial(far_kernel, layout), out_shape=[jax.Shap...]
    ppermute x1, waiting for transfers between devices: 2.95 us -> 5.61 us  [shards(): far, near = ([lax.ppermute(own[0], 'kz', two_on)], [])]
    ppermute x6, waiting for transfers between devices: 0.13 us -> 2.58 us  [shards(): near.append(lax.ppermute(source[i], 'kz', swap))]
    concatenate x4, other arithmetic: 2.87 us -> 0.78 us  [cut(): return jnp.concatenate([real[0, energies], imag[0, energies]], axis=1)]
    ppermute x5, starting transfers between devices: 7.24 us -> 5.89 us  [shards(): far.append(lax.ppermute(own[i], 'kz', two_on))]
    ppermute x1, waiting for transfers between devices: 0.01 us -> 1.25 us  [shards(): halos['far', 'outer'] = lax.ppermute(far[0], 'en', outer)]
    pallas_call x3, Pallas kernels: 13.6 us -> 12.7 us  [near_part(): pl.pallas_call(functools.partial(near_kernel, (layout, own_layout)), grid...]
    select_n x6, other arithmetic: 1.85 us -> 0.89 us  [shards(): source.append(jnp.where(even, own[i], far[i]))]
  transfers between devices with their start and end apart: 16 -> 16, of which waited for: 3 -> 6; matrix products, arithmetic and copies ran while one was open for 11% -> 6% of each run, Pallas kernels for 30% -> 26%
where the time goes in v4:
time: 64.8 us; the launch traced here: 64.5 us
  Pallas kernels  22.8 us (35%)
  starting transfers between devices  22 us (34%)
  waiting for transfers between devices  11.5 us (18%)
  local copies, waits for them, and re-layouts  4.51 us (7%)
  other arithmetic  2.8 us (4%)
  between operations  0.89 us (1%)
    pallas_call x3, Pallas kernels, near_part(): pl.pallas_call(functools.partial(near_kernel, (layout, own_layout)), grid...  12.7 us
    pallas_call x4, Pallas kernels, far_part(): pl.pallas_call(functools.partial(far_kernel, layout), out_shape=[jax.Shap...  8.26 us
    ppermute x6, starting transfers between devices, shards(): near.append(lax.ppermute(source[i], 'kz', swap))  6.95 us
    ppermute x5, starting transfers between devices, shards(): far.append(lax.ppermute(own[i], 'kz', two_on))  5.89 us
    ppermute x1, waiting for transfers between devices, shards(): far, near = ([lax.ppermute(own[0], 'kz', two_on)], [])  5.61 us
    ppermute x1, starting transfers between devices, shards(): halos['near', 'outer'] = lax.ppermute(edge, both, outer_turned)  3.46 us
    ppermute x1, starting transfers between devices, shards(): halos['far', 'outer'] = lax.ppermute(far[0], 'en', outer)  2.93 us
    squeeze x3, local copies, waits for them, and re-layouts, cut(): return jnp.concatenate([real[0, energies], imag[0, energies]], axis=1)  2.64 us
  transfers between devices with their start and end apart: 16, of which 6 were waited for; matrix products, arithmetic and copies ran while one was open for 6% of the time, Pallas kernels for 26%

profile of v4, /device:TPU:4, one launch (start us, length us, event | category | flops | bytes accessed | tf_op | source)
XLA Modules:
  0.0 64.5 jit_solution(11893273495862807933)
XLA Ops:
  0.7 1.2 %slice_bitcast_fusion.12 = (bf16[4,128,128]{2,1,0:T(8,128)(2,1)S(1)}, bf16[4,128,128]{2,1,0:T(8,128)(2,1)S(1)}, bf16[4,128,128]{2,1,0:T(8,128)(2,1)S(1)}, bf16[4,128,128]{2,1,0:T(8,128)(2,1)S(1)}) fusion(bf16[1,24,128,128]{3,2,1,0:T(8,128)(2,1)} %param.6, bf16[1,24,128,128]{3,2,1,0:T(8,128)(2,1)} %param.5), kind=kLoop, calls=%fused_computation.25 | loop fusion | bytes 1048576 | tf_op jit(solution)/shard_map/squeeze | solution.py:204
  2.0 2.0 %collective-permute-start.2 = (bf16[4,256,128]{2,1,0:T(8,128)(2,1)S(1)}, bf16[4,256,128]{2,1,0:T(8,128)(2,1)S(1)}, u32[]{:S(2)}, u32[]{:S(2)}) collective-permute-start(bf16[4,256,128]{2,1,0:T(8,128)(2,1)S(1)} %maximum_select_fusion.refs_6_.refs_9_), channel_id=1, source_target_pairs={{0,32},{16,48},{32,64},{48,80},{64,96},{80,112},{96,128},{112,144}... | collective-permute-start | bytes 786440 | tf_op jit(solution)/shard_map/ppermute | solution.py:208
  5.5 2.0 %collective-permute-start = (bf16[4,256,128]{2,1,0:T(8,128)(2,1)S(1)}, bf16[4,256,128]{2,1,0:T(8,128)(2,1)S(1)}, u32[]{:S(2)}, u32[]{:S(2)}) collective-permute-start(bf16[4,256,128]{2,1,0:T(8,128)(2,1)S(1)} %maximum_select_fusion.1.refs_5_.refs_10_), channel_id=1, source_target_pairs={{0,32},{16,48},{32,64},{48,80},{64,96},{80,112},{96,128},{112,144}... | collective-permute-start | bytes 786440 | tf_op jit(solution)/shard_map/ppermute | solution.py:215
  9.4 5.6 %collective-permute-done.2.refs_3_.refs_1_ = bf16[4,256,128]{2,1,0:T(8,128)(2,1)S(1)} collective-permute-done((bf16[4,256,128]{2,1,0:T(8,128)(2,1)S(1)}, bf16[4,256,128]{2,1,0:T(8,128)(2,1)S(1)}, u32[]{:S(2)}, u32[]{:S(2)}) %collective-permute-start.2) | collective-permute-done | bytes 262176 | tf_op jit(solution)/shard_map/ppermute | solution.py:208
  15.8 1.2 %collective-permute-start.6 = (bf16[4,256,128]{2,1,0:T(8,128)(2,1)}, bf16[4,256,128]{2,1,0:T(8,128)(2,1)S(1)}, u32[]{:S(2)}, u32[]{:S(2)}) collective-permute-start(bf16[4,256,128]{2,1,0:T(8,128)(2,1)} %broadcast_select_fusion.6), channel_id=1, source_target_pairs={{0,16},{16,0},{32,48},{48,32},{64,80},{80,64},{96,112},{112,96},{1... | collective-permute-start | bytes 786440 | tf_op jit(solution)/shard_map/ppermute | solution.py:251
  17.7 2.9 %collective-permute-start.4 = (bf16[4,256,128]{2,1,0:T(8,128)(2,1)S(1)}, bf16[4,256,128]{2,1,0:T(8,128)(2,1)S(1)}, u32[]{:S(2)}, u32[]{:S(2)}) collective-permute-start(bf16[4,256,128]{2,1,0:T(8,128)(2,1)S(1)} %collective-permute-done.2.refs_3_.refs_1_), channel_id=1, source_target_pairs={{1,2},{2,1},{3,4},{4,3},{5,6},{6,5},{7,8},{8,7},{9,10},{10,9},{11,... | collective-permute-start | bytes 786440 | tf_op jit(solution)/shard_map/ppermute | solution.py:250
  23.4 2.0 %collective-permute-done.5.refs_4_.refs_2_.refs_0_ = bf16[4,256,128]{2,1,0:T(8,128)(2,1)S(1)} collective-permute-done((bf16[4,256,128]{2,1,0:T(8,128)(2,1)S(1)}, bf16[4,256,128]{2,1,0:T(8,128)(2,1)S(1)}, u32[]{:S(2)}, u32[]{:S(2)}) %collective-permute-start.5) | collective-permute-done | bytes 262176 | tf_op jit(solution)/shard_map/ppermute | solution.py:215
  25.4 1.3 %collective-permute-start.7 = (bf16[4,256,128]{2,1,0:T(8,128)(2,1)S(1)}, bf16[4,256,128]{2,1,0:T(8,128)(2,1)S(1)}, u32[]{:S(2)}, u32[]{:S(2)}) collective-permute-start(bf16[4,256,128]{2,1,0:T(8,128)(2,1)S(1)} %broadcast_select_fusion.5), channel_id=1, source_target_pairs={{0,16},{16,0},{32,48},{48,32},{64,80},{80,64},{96,112},{112,96},{1... | collective-permute-start | bytes 786440 | tf_op jit(solution)/shard_map/ppermute | solution.py:251
  26.7 1.0 %broadcast_select_fusion = bf16[4,256,128]{2,1,0:T(8,128)(2,1)S(1)} fusion(bf16[4,256,128]{2,1,0:T(8,128)(2,1)} %broadcast_select_fusion.6, bf16[4,256,128]{2,1,0:T(8,128)(2,1)S(1)} %collective-permute-done.6.refs_3_.refs_1_, pred[]{:T(512)S(6)} %or.3), kind=kLoop, calls=%fused_computation.6 | loop fusion | flops 131072 | bytes 786433 | tf_op jit(solution)/shard_map/jit(_where)/select_n | solution.py:255
  27.7 1.3 %collective-permute-done.4.refs_1_.refs_5_ = bf16[4,256,128]{2,1,0:T(8,128)(2,1)S(1)} collective-permute-done((bf16[4,256,128]{2,1,0:T(8,128)(2,1)S(1)}, bf16[4,256,128]{2,1,0:T(8,128)(2,1)S(1)}, u32[]{:S(2)}, u32[]{:S(2)}) %collective-permute-start.4) | collective-permute-done | bytes 262176 | tf_op jit(solution)/shard_map/ppermute | solution.py:250
  29.0 3.5 %collective-permute-start.11 = (bf16[4,256,128]{2,1,0:T(8,128)(2,1)S(1)}, bf16[4,256,128]{2,1,0:T(8,128)(2,1)S(1)}, u32[]{:S(2)}, u32[]{:S(2)}) collective-permute-start(bf16[4,256,128]{2,1,0:T(8,128)(2,1)S(1)} %broadcast_select_fusion), channel_id=1, source_target_pairs={{1,2},{2,1},{3,4},{4,3},{5,6},{6,5},{7,24},{8,23},{9,10},{10,9},{1... | collective-permute-start | bytes 786440 | tf_op jit(solution)/shard_map/ppermute | solution.py:256
  32.5 1.1 %collective-permute-start.10 = (bf16[4,256,128]{2,1,0:T(8,128)(2,1)S(1)}, bf16[4,256,128]{2,1,0:T(8,128)(2,1)S(1)}, u32[]{:S(2)}, u32[]{:S(2)}) collective-permute-start(bf16[4,256,128]{2,1,0:T(8,128)(2,1)S(1)} %broadcast_select_fusion.4), channel_id=1, source_target_pairs={{0,16},{16,0},{32,48},{48,32},{64,80},{80,64},{96,112},{112,96},{1... | collective-permute-start | bytes 786440 | tf_op jit(solution)/shard_map/ppermute | solution.py:251
  33.5 1.4 %far_part.4.refs_9_ = f32[4,128,256]{2,1,0:T(8,128)S(1)} custom-call(s32[1]{0:T(128)} %bitcast.odd_ref, bf16[4,256,128]{2,1,0:T(8,128)(2,1)S(1)} %collective-permute-done.3.refs_0_.refs_6_, bf16[4,256,128]{2,1,0:T(8,128)(2,1)S(1)} %collective-permute-done.4.refs_1_.refs_5_, bf16[4,256,128]{2,1,0:T(8,128)(2,1)S(1)} %collective-permute-done.refs_2_.refs_0_.refs_4_, ...), custom_call_target="tpu_custom_call" | custom-call | bytes 1000000 | tf_op jit(solution)/shard_map/far_part/pallas_call | solution.py:101
  35.2 3.8 %collective-permute-start.13 = (bf16[4,256,128]{2,1,0:T(8,128)(2,1)S(1)}, bf16[4,256,128]{2,1,0:T(8,128)(2,1)S(1)}, u32[]{:S(2)}, u32[]{:S(2)}) collective-permute-start(bf16[4,256,128]{2,1,0:T(8,128)(2,1)S(1)} %pad_maximum_fusion.3.refs_8_), channel_id=1, source_target_pairs={{0,32},{16,48},{32,64},{48,80},{64,96},{80,112},{96,128},{112,144}... | collective-permute-start | bytes 786440 | tf_op jit(solution)/shard_map/ppermute | solution.py:215
  38.9 1.0 %collective-permute-start.8 = (bf16[4,256,128]{2,1,0:T(8,128)(2,1)S(1)}, bf16[4,256,128]{2,1,0:T(8,128)(2,1)S(1)}, u32[]{:S(2)}, u32[]{:S(2)}) collective-permute-start(bf16[4,256,128]{2,1,0:T(8,128)(2,1)S(1)} %broadcast_select_fusion.3), channel_id=1, source_target_pairs={{0,16},{16,0},{32,48},{48,32},{64,80},{80,64},{96,112},{112,96},{1... | collective-permute-start | bytes 786440 | tf_op jit(solution)/shard_map/ppermute | solution.py:251
  40.0 1.4 %far_part.5.refs_9_ = f32[4,128,256]{2,1,0:T(8,128)S(1)} custom-call(s32[1]{0:T(128)} %bitcast.odd_ref, bf16[4,256,128]{2,1,0:T(8,128)(2,1)S(1)} %collective-permute-done.refs_2_.refs_0_.refs_4_, bf16[4,256,128]{2,1,0:T(8,128)(2,1)S(1)} %collective-permute-done.2.refs_3_.refs_1_, bf16[4,256,128]{2,1,0:T(8,128)(2,1)S(1)} %collective-permute-done.5.refs_4_.refs_2_.refs_0_, ...), custom_call_target="tpu_custom_call" | custom-call | bytes 1000000 | tf_op jit(solution)/shard_map/far_part/pallas_call | solution.py:101
  41.5 1.2 %collective-permute-start.12 = (bf16[4,256,128]{2,1,0:T(8,128)(2,1)S(1)}, bf16[4,256,128]{2,1,0:T(8,128)(2,1)S(1)}, u32[]{:S(2)}, u32[]{:S(2)}) collective-permute-start(bf16[4,256,128]{2,1,0:T(8,128)(2,1)S(1)} %broadcast_select_fusion.2), channel_id=1, source_target_pairs={{0,16},{16,0},{32,48},{48,32},{64,80},{80,64},{96,112},{112,96},{1... | collective-permute-start | bytes 786440 | tf_op jit(solution)/shard_map/ppermute | solution.py:251
  42.7 1.4 %far_part.6.refs_10_ = f32[4,128,256]{2,1,0:T(8,128)S(1)} custom-call(s32[1]{0:T(128)} %bitcast.odd_ref, bf16[4,256,128]{2,1,0:T(8,128)(2,1)S(1)} %collective-permute-done.5.refs_4_.refs_2_.refs_0_, bf16[4,256,128]{2,1,0:T(8,128)(2,1)S(1)} %collective-permute-done.1.refs_3_.refs_1_.refs_0_, bf16[4,256,128]{2,1,0:T(8,128)(2,1)S(1)} %collective-permute-done.9.refs_2_.refs_1_, ...), custom_call_target="tpu_custom_call" | custom-call | bytes 1000000 | tf_op jit(solution)/shard_map/far_part/pallas_call | solution.py:101
  44.2 2.5 %near_part.3 = (bf16[1,24,128,128]{3,2,1,0:T(8,128)(2,1)}, bf16[1,24,128,128]{3,2,1,0:T(8,128)(2,1)}) custom-call(s32[1]{0:T(128)} %bitcast.odd_ref, bf16[4,256,128]{2,1,0:T(8,128)(2,1)S(1)} %collective-permute-done.14.refs_0_.refs_6_, bf16[4,256,128]{2,1,0:T(8,128)(2,1)S(1)} %collective-permute-done.11.refs_1_.refs_5_, ...), custom_call_target="tpu_custom_call" | custom-call | bytes 1000000 | tf_op jit(solution)/shard_map/near_part/pallas_call | solution.py:162
  46.6 1.4 %collective-permute-done.8.refs_3_.refs_0_ = bf16[4,256,128]{2,1,0:T(8,128)(2,1)S(1)} collective-permute-done((bf16[4,256,128]{2,1,0:T(8,128)(2,1)S(1)}, bf16[4,256,128]{2,1,0:T(8,128)(2,1)S(1)}, u32[]{:S(2)}, u32[]{:S(2)}) %collective-permute-start.8) | collective-permute-done | bytes 262176 | tf_op jit(solution)/shard_map/ppermute | solution.py:251
  48.1 1.1 %collective-permute-start.15 = (bf16[4,256,128]{2,1,0:T(8,128)(2,1)S(1)}, bf16[4,256,128]{2,1,0:T(8,128)(2,1)S(1)}, u32[]{:S(2)}, u32[]{:S(2)}) collective-permute-start(bf16[4,256,128]{2,1,0:T(8,128)(2,1)S(1)} %broadcast_select_fusion.1), channel_id=1, source_target_pairs={{0,16},{16,0},{32,48},{48,32},{64,80},{80,64},{96,112},{112,96},{1... | collective-permute-start | bytes 786440 | tf_op jit(solution)/shard_map/ppermute | solution.py:251
  49.2 3.9 %far_part.7 = (f32[4,128,256]{2,1,0:T(8,128)S(1)}, f32[4,128,256]{2,1,0:T(8,128)S(1)}, f32[4,128,256]{2,1,0:T(8,128)S(1)}) custom-call(s32[1]{0:T(128)} %bitcast.odd_ref, bf16[4,256,128]{2,1,0:T(8,128)(2,1)S(1)} %collective-permute-done.1.refs_3_.refs_1_.refs_0_, bf16[4,256,128]{2,1,0:T(8,128)(2,1)S(1)} %collective-permute-done.9.refs_2_.refs_1_, ...), custom_call_target="tpu_custom_call" | custom-call | bytes 1000000 | tf_op jit(solution)/shard_map/far_part/pallas_call | solution.py:101
  53.7 4.2 %near_part.4 = (bf16[1,24,128,128]{3,2,1,0:T(8,128)(2,1)}, bf16[1,24,128,128]{3,2,1,0:T(8,128)(2,1)}) custom-call(s32[1]{0:T(128)} %bitcast.odd_ref, bf16[4,256,128]{2,1,0:T(8,128)(2,1)S(1)} %collective-permute-done.7.refs_2_.refs_0_.refs_4_, ...), custom_call_target="tpu_custom_call", output_to_operand_aliasing={{0}: (12, {}), {1}: (13, {})} | custom-call | bytes 1000000 | tf_op jit(solution)/shard_map/near_part/pallas_call | solution.py:162
  58.5 6.0 %near_part.5 = (bf16[1,24,128,128]{3,2,1,0:T(8,128)(2,1)}, bf16[1,24,128,128]{3,2,1,0:T(8,128)(2,1)}) custom-call(s32[1]{0:T(128)} %bitcast.odd_ref, bf16[4,256,128]{2,1,0:T(8,128)(2,1)S(1)} %collective-permute-done.8.refs_3_.refs_0_, ...), custom_call_target="tpu_custom_call", output_to_operand_aliasing={{0}: (17, {}), {1}: (18, {})} | custom-call | bytes 1000000 | tf_op jit(solution)/shard_map/near_part/pallas_call | solution.py:162
  (51 shorter events, 9.1 us)
Async XLA Ops:
  0.6 3.3 %copy-start.5 = (bf16[1,24,128,128]{3,2,1,0:T(8,128)(2,1)S(1)}, bf16[1,24,128,128]{3,2,1,0:T(8,128)(2,1)}, u32[]{:S(2)}) copy-start(bf16[1,24,128,128]{3,2,1,0:T(8,128)(2,1)} %param.5) | copy-start | bytes 2359300
  1.9 2.7 %copy-start.6 = (bf16[1,24,128,128]{3,2,1,0:T(8,128)(2,1)S(1)}, bf16[1,24,128,128]{3,2,1,0:T(8,128)(2,1)}, u32[]{:S(2)}) copy-start(bf16[1,24,128,128]{3,2,1,0:T(8,128)(2,1)} %param.6) | copy-start | bytes 2359300
  2.0 13.1 %collective-permute-start.2 = (bf16[4,256,128]{2,1,0:T(8,128)(2,1)S(1)}, bf16[4,256,128]{2,1,0:T(8,128)(2,1)S(1)}, u32[]{:S(2)}, u32[]{:S(2)}) collective-permute-start(bf16[4,256,128]{2,1,0:T(8,128)(2,1)S(1)} %maximum_select_fusion.refs_6_.refs_9_), channel_id=1, source_target_pairs={{0,32},{16,48},{32,64},{48,80},{64,96},{80,112},{96,128},{112,144}... | collective-permute-start | bytes 786440 | tf_op jit(solution)/shard_map/ppermute | solution.py:208
  5.5 15.2 %collective-permute-start = (bf16[4,256,128]{2,1,0:T(8,128)(2,1)S(1)}, bf16[4,256,128]{2,1,0:T(8,128)(2,1)S(1)}, u32[]{:S(2)}, u32[]{:S(2)}) collective-permute-start(bf16[4,256,128]{2,1,0:T(8,128)(2,1)S(1)} %maximum_select_fusion.1.refs_5_.refs_10_), channel_id=1, source_target_pairs={{0,32},{16,48},{32,64},{48,80},{64,96},{80,112},{96,128},{112,144}... | collective-permute-start | bytes 786440 | tf_op jit(solution)/shard_map/ppermute | solution.py:215
  7.5 0.9 %copy-start.1 = (bf16[2,4,1,128,128]{4,3,2,1,0:T(8,128)(2,1)S(1)}, bf16[2,4,1,128,128]{4,3,2,1,0:T(8,128)(2,1)}, u32[]{:S(2)}) copy-start(bf16[2,4,1,128,128]{4,3,2,1,0:T(8,128)(2,1)} %coupling_ref.2) | copy-start | bytes 786436
  7.5 0.9 %copy-start.3 = (f32[2,4,8]{2,1,0:T(4,128)S(1)}, f32[2,4,8]{2,1,0:T(4,128)}, u32[]{:S(2)}) copy-start(f32[2,4,8]{2,1,0:T(4,128)} %strengths_ref.3) | copy-start | bytes 772
  15.0 10.4 %collective-permute-start.5 = (bf16[4,256,128]{2,1,0:T(8,128)(2,1)S(1)}, bf16[4,256,128]{2,1,0:T(8,128)(2,1)S(1)}, u32[]{:S(2)}, u32[]{:S(2)}) collective-permute-start(bf16[4,256,128]{2,1,0:T(8,128)(2,1)S(1)} %pad_maximum_fusion.1.refs_5_), channel_id=1, source_target_pairs={{0,32},{16,48},{32,64},{48,80},{64,96},{80,112},{96,128},{112,144}... | collective-permute-start | bytes 786440 | tf_op jit(solution)/shard_map/ppermute | solution.py:215
  15.0 1.9 %copy-start.7 = (bf16[4,128,128]{2,1,0:T(8,128)(2,1)S(1)}, bf16[4,128,128]{2,1,0:T(8,128)(2,1)}, u32[]{:S(2)}) copy-start(bf16[4,128,128]{2,1,0:T(8,128)(2,1)} %get-tuple-element.73) | copy-start | bytes 393220
  15.0 1.9 %copy-start.8 = (bf16[4,128,128]{2,1,0:T(8,128)(2,1)S(1)}, bf16[4,128,128]{2,1,0:T(8,128)(2,1)}, u32[]{:S(2)}) copy-start(bf16[4,128,128]{2,1,0:T(8,128)(2,1)} %get-tuple-element.79) | copy-start | bytes 393220
  15.8 10.9 %collective-permute-start.6 = (bf16[4,256,128]{2,1,0:T(8,128)(2,1)}, bf16[4,256,128]{2,1,0:T(8,128)(2,1)S(1)}, u32[]{:S(2)}, u32[]{:S(2)}) collective-permute-start(bf16[4,256,128]{2,1,0:T(8,128)(2,1)} %broadcast_select_fusion.6), channel_id=1, source_target_pairs={{0,16},{16,0},{32,48},{48,32},{64,80},{80,64},{96,112},{112,96},{1... | collective-permute-start | bytes 786440 | tf_op jit(solution)/shard_map/ppermute | solution.py:251
  17.7 11.3 %collective-permute-start.4 = (bf16[4,256,128]{2,1,0:T(8,128)(2,1)S(1)}, bf16[4,256,128]{2,1,0:T(8,128)(2,1)S(1)}, u32[]{:S(2)}, u32[]{:S(2)}) collective-permute-start(bf16[4,256,128]{2,1,0:T(8,128)(2,1)S(1)} %collective-permute-done.2.refs_3_.refs_1_), channel_id=1, source_target_pairs={{1,2},{2,1},{3,4},{4,3},{5,6},{6,5},{7,8},{8,7},{9,10},{10,9},{11,... | collective-permute-start | bytes 786440 | tf_op jit(solution)/shard_map/ppermute | solution.py:250
  20.6 14.3 %collective-permute-start.1 = (bf16[4,256,128]{2,1,0:T(8,128)(2,1)}, bf16[4,256,128]{2,1,0:T(8,128)(2,1)S(1)}, u32[]{:S(2)}, u32[]{:S(2)}) collective-permute-start(bf16[4,256,128]{2,1,0:T(8,128)(2,1)} %pad_maximum_fusion.refs_6_), channel_id=1, source_target_pairs={{0,32},{16,48},{32,64},{48,80},{64,96},{80,112},{96,128},{112,144}... | collective-permute-start | bytes 786440 | tf_op jit(solution)/shard_map/ppermute | solution.py:215
  20.8 0.9 %copy-start.2 = (bf16[2,4,1,128,128]{4,3,2,1,0:T(8,128)(2,1)S(1)}, bf16[2,4,1,128,128]{4,3,2,1,0:T(8,128)(2,1)}, u32[]{:S(2)}) copy-start(bf16[2,4,1,128,128]{4,3,2,1,0:T(8,128)(2,1)} %coupling_ref.2) | copy-start | bytes 786436
  22.7 9.8 %collective-permute-start.3 = (bf16[4,256,128]{2,1,0:T(8,128)(2,1)S(1)}, bf16[4,256,128]{2,1,0:T(8,128)(2,1)S(1)}, u32[]{:S(2)}, u32[]{:S(2)}) collective-permute-start(bf16[4,256,128]{2,1,0:T(8,128)(2,1)S(1)} %collective-permute-done.refs_2_.refs_0_.refs_4_), channel_id=1, source_target_pairs={{0,1},{1,0},{2,3},{3,2},{4,5},{5,4},{6,7},{7,6},{8,9},{9,8},{10,11... | collective-permute-start | bytes 786440 | tf_op jit(solution)/shard_map/ppermute | solution.py:253
  25.4 9.6 %collective-permute-start.7 = (bf16[4,256,128]{2,1,0:T(8,128)(2,1)S(1)}, bf16[4,256,128]{2,1,0:T(8,128)(2,1)S(1)}, u32[]{:S(2)}, u32[]{:S(2)}) collective-permute-start(bf16[4,256,128]{2,1,0:T(8,128)(2,1)S(1)} %broadcast_select_fusion.5), channel_id=1, source_target_pairs={{0,16},{16,0},{32,48},{48,32},{64,80},{80,64},{96,112},{112,96},{1... | collective-permute-start | bytes 786440 | tf_op jit(solution)/shard_map/ppermute | solution.py:251
  26.7 12.2 %collective-permute-start.9 = (bf16[4,256,128]{2,1,0:T(8,128)(2,1)S(1)}, bf16[4,256,128]{2,1,0:T(8,128)(2,1)S(1)}, u32[]{:S(2)}, u32[]{:S(2)}) collective-permute-start(bf16[4,256,128]{2,1,0:T(8,128)(2,1)S(1)} %pad_maximum_fusion.2.refs_7_), channel_id=1, source_target_pairs={{0,32},{16,48},{32,64},{48,80},{64,96},{80,112},{96,128},{112,144}... | collective-permute-start | bytes 786440 | tf_op jit(solution)/shard_map/ppermute | solution.py:215
  29.0 12.4 %collective-permute-start.11 = (bf16[4,256,128]{2,1,0:T(8,128)(2,1)S(1)}, bf16[4,256,128]{2,1,0:T(8,128)(2,1)S(1)}, u32[]{:S(2)}, u32[]{:S(2)}) collective-permute-start(bf16[4,256,128]{2,1,0:T(8,128)(2,1)S(1)} %broadcast_select_fusion), channel_id=1, source_target_pairs={{1,2},{2,1},{3,4},{4,3},{5,6},{6,5},{7,24},{8,23},{9,10},{10,9},{1... | collective-permute-start | bytes 786440 | tf_op jit(solution)/shard_map/ppermute | solution.py:256
  32.5 9.0 %collective-permute-start.10 = (bf16[4,256,128]{2,1,0:T(8,128)(2,1)S(1)}, bf16[4,256,128]{2,1,0:T(8,128)(2,1)S(1)}, u32[]{:S(2)}, u32[]{:S(2)}) collective-permute-start(bf16[4,256,128]{2,1,0:T(8,128)(2,1)S(1)} %broadcast_select_fusion.4), channel_id=1, source_target_pairs={{0,16},{16,0},{32,48},{48,32},{64,80},{80,64},{96,112},{112,96},{1... | collective-permute-start | bytes 786440 | tf_op jit(solution)/shard_map/ppermute | solution.py:251
  33.5 1.5 %copy-start = (bf16[4,256,128]{2,1,0:T(8,128)(2,1)S(1)}, bf16[4,256,128]{2,1,0:T(8,128)(2,1)}, u32[]{:S(2)}) copy-start(bf16[4,256,128]{2,1,0:T(8,128)(2,1)} %pad_maximum_fusion.refs_6_) | copy-start | bytes 786436
  35.1 9.1 %collective-permute-start.14 = (bf16[4,256,128]{2,1,0:T(8,128)(2,1)S(1)}, bf16[4,256,128]{2,1,0:T(8,128)(2,1)S(1)}, u32[]{:S(2)}, u32[]{:S(2)}) collective-permute-start(bf16[4,256,128]{2,1,0:T(8,128)(2,1)S(1)} %collective-permute-done.7.refs_2_.refs_0_.refs_4_), channel_id=1, source_target_pairs={{0,1},{1,0},{2,3},{3,2},{4,5},{5,4},{6,7},{7,6},{8,9},{9,8},{10,11... | collective-permute-start | bytes 786440 | tf_op jit(solution)/shard_map/ppermute | solution.py:260
  35.2 11.5 %collective-permute-start.13 = (bf16[4,256,128]{2,1,0:T(8,128)(2,1)S(1)}, bf16[4,256,128]{2,1,0:T(8,128)(2,1)S(1)}, u32[]{:S(2)}, u32[]{:S(2)}) collective-permute-start(bf16[4,256,128]{2,1,0:T(8,128)(2,1)S(1)} %pad_maximum_fusion.3.refs_8_), channel_id=1, source_target_pairs={{0,32},{16,48},{32,64},{48,80},{64,96},{80,112},{96,128},{112,144}... | collective-permute-start | bytes 786440 | tf_op jit(solution)/shard_map/ppermute | solution.py:215
  38.9 9.2 %collective-permute-start.8 = (bf16[4,256,128]{2,1,0:T(8,128)(2,1)S(1)}, bf16[4,256,128]{2,1,0:T(8,128)(2,1)S(1)}, u32[]{:S(2)}, u32[]{:S(2)}) collective-permute-start(bf16[4,256,128]{2,1,0:T(8,128)(2,1)S(1)} %broadcast_select_fusion.3), channel_id=1, source_target_pairs={{0,16},{16,0},{32,48},{48,32},{64,80},{80,64},{96,112},{112,96},{1... | collective-permute-start | bytes 786440 | tf_op jit(solution)/shard_map/ppermute | solution.py:251
  41.5 12.2 %collective-permute-start.12 = (bf16[4,256,128]{2,1,0:T(8,128)(2,1)S(1)}, bf16[4,256,128]{2,1,0:T(8,128)(2,1)S(1)}, u32[]{:S(2)}, u32[]{:S(2)}) collective-permute-start(bf16[4,256,128]{2,1,0:T(8,128)(2,1)S(1)} %broadcast_select_fusion.2), channel_id=1, source_target_pairs={{0,16},{16,0},{32,48},{48,32},{64,80},{80,64},{96,112},{112,96},{1... | collective-permute-start | bytes 786440 | tf_op jit(solution)/shard_map/ppermute | solution.py:251
  48.1 10.4 %collective-permute-start.15 = (bf16[4,256,128]{2,1,0:T(8,128)(2,1)S(1)}, bf16[4,256,128]{2,1,0:T(8,128)(2,1)S(1)}, u32[]{:S(2)}, u32[]{:S(2)}) collective-permute-start(bf16[4,256,128]{2,1,0:T(8,128)(2,1)S(1)} %broadcast_select_fusion.1), channel_id=1, source_target_pairs={{0,16},{16,0},{32,48},{48,32},{64,80},{80,64},{96,112},{112,96},{1... | collective-permute-start | bytes 786440 | tf_op jit(solution)/shard_map/ppermute | solution.py:251
  (1 other events, 0.9 us)

commit v5 on v4

--- a/solution.py
+++ b/solution.py
@@ -224,8 +224,8 @@
     odd = odd_lane.astype(jnp.int32).reshape(1)
     out, done = None, (near_side[0],)
     parts, halos, source = {}, {}, []
-    far_work = {2: [0], 3: [1], 4: [2], 5: [3, 4, 5]}
-    near_work = {4: [[0]], 5: [[1, 2]]}
+    far_work = {3: [1], 4: [0], 5: [2, 3, 4, 5]}
+    near_work = {4: [[0, 1]], 5: [[2]]}
     rest = [3, 4, 5]
 
     def grouped(sent, side, group):

time: 64.8 us -> 78.5 us (1.21)
  the two profiles are of different devices: /device:TPU:4 before, /device:TPU:38 now
where the time goes in v5:
time: 78.5 us; the launch traced here: 78 us
  starting transfers between devices  31 us (39%)
  Pallas kernels  28.5 us (36%)
  local copies, waits for them, and re-layouts  8.59 us (11%)
  other arithmetic  6.6 us (8%)
  waiting for transfers between devices  2.44 us (3%)
  between operations  0.93 us (1%)
    pallas_call x3, Pallas kernels, near_part(): pl.pallas_call(functools.partial(near_kernel, (layout, own_layout)), grid...  16.4 us
    ppermute x5, starting transfers between devices, shards(): far.append(lax.ppermute(own[i], 'kz', two_on))  13 us
    pallas_call x3, Pallas kernels, far_part(): pl.pallas_call(functools.partial(far_kernel, layout), out_shape=[jax.Shap...  10.2 us
    ppermute x6, starting transfers between devices, shards(): near.append(lax.ppermute(source[i], 'kz', swap))  7.37 us
    ppermute x1, starting transfers between devices, shards(): halos['far', 'outer'] = lax.ppermute(far[0], 'en', outer)  6.03 us
    unnamed x42, local copies, waits for them, and re-layouts  5.96 us
    concatenate x4, other arithmetic, cut(): return jnp.concatenate([real[0, energies], imag[0, energies]], axis=1)  2.9 us
    squeeze x3, local copies, waits for them, and re-layouts, cut(): return jnp.concatenate([real[0, energies], imag[0, energies]], axis=1)  2.62 us
  transfers between devices with their start and end apart: 16, of which 4 were waited for; matrix products, arithmetic and copies ran while one was open for 10% of the time, Pallas kernels for 27%

profile of v5, /device:TPU:38, one launch (start us, length us, event | category | flops | bytes accessed | tf_op | source)
XLA Modules:
  0.0 78.0 jit_solution(12185973976947225465)
XLA Ops:
  0.7 1.2 %slice_bitcast_fusion.12 = (bf16[4,128,128]{2,1,0:T(8,128)(2,1)S(1)}, bf16[4,128,128]{2,1,0:T(8,128)(2,1)S(1)}, bf16[4,128,128]{2,1,0:T(8,128)(2,1)S(1)}, bf16[4,128,128]{2,1,0:T(8,128)(2,1)S(1)}) fusion(bf16[1,24,128,128]{3,2,1,0:T(8,128)(2,1)} %param.6, bf16[1,24,128,128]{3,2,1,0:T(8,128)(2,1)} %param.5), kind=kLoop, calls=%fused_computation.25 | loop fusion | bytes 1048576 | tf_op jit(solution)/shard_map/squeeze | solution.py:204
  2.0 2.0 %collective-permute-start.2 = (bf16[4,256,128]{2,1,0:T(8,128)(2,1)S(1)}, bf16[4,256,128]{2,1,0:T(8,128)(2,1)S(1)}, u32[]{:S(2)}, u32[]{:S(2)}) collective-permute-start(bf16[4,256,128]{2,1,0:T(8,128)(2,1)S(1)} %maximum_select_fusion.refs_7_.refs_9_), channel_id=1, source_target_pairs={{0,32},{16,48},{32,64},{48,80},{64,96},{80,112},{96,128},{112,144}... | collective-permute-start | bytes 786440 | tf_op jit(solution)/shard_map/ppermute | solution.py:208
  5.5 2.0 %collective-permute-start = (bf16[4,256,128]{2,1,0:T(8,128)(2,1)S(1)}, bf16[4,256,128]{2,1,0:T(8,128)(2,1)S(1)}, u32[]{:S(2)}, u32[]{:S(2)}) collective-permute-start(bf16[4,256,128]{2,1,0:T(8,128)(2,1)S(1)} %maximum_select_fusion.1.refs_6_.refs_10_), channel_id=1, source_target_pairs={{0,32},{16,48},{32,64},{48,80},{64,96},{80,112},{96,128},{112,144}... | collective-permute-start | bytes 786440 | tf_op jit(solution)/shard_map/ppermute | solution.py:215
  8.1 0.9 %prepare.2 = (bf16[1024,512]{1,0:T(8,128)(2,1)S(1)}, bf16[128,512]{1,0:T(8,128)(2,1)S(1)}) custom-call(s32[2,8]{1,0:T(2,128)S(1)} %copy-done.16, f32[2,4,8]{2,1,0:T(4,128)S(1)} %copy-done.15, bf16[2,4,1,128,128]{4,3,2,1,0:T(8,128)(2,1)S(1)} %copy-done.11), custom_call_target="tpu_custom_call" | custom-call | bytes 1000000 | tf_op jit(solution)/shard_map/prepare/pallas_call | solution.py:41
  11.2 2.4 %collective-permute-start.3 = (bf16[4,256,128]{2,1,0:T(8,128)(2,1)}, bf16[4,256,128]{2,1,0:T(8,128)(2,1)S(1)}, u32[]{:S(2)}, u32[]{:S(2)}) collective-permute-start(bf16[4,256,128]{2,1,0:T(8,128)(2,1)} %pad_maximum_fusion.1.refs_8_), channel_id=1, source_target_pairs={{0,32},{16,48},{32,64},{48,80},{64,96},{80,112},{96,128},{112,144}... | collective-permute-start | bytes 786440 | tf_op jit(solution)/shard_map/ppermute | solution.py:215
  16.7 2.1 %collective-permute-start.1 = (bf16[4,256,128]{2,1,0:T(8,128)(2,1)}, bf16[4,256,128]{2,1,0:T(8,128)(2,1)S(1)}, u32[]{:S(2)}, u32[]{:S(2)}) collective-permute-start(bf16[4,256,128]{2,1,0:T(8,128)(2,1)} %pad_maximum_fusion.refs_3_), channel_id=1, source_target_pairs={{0,32},{16,48},{32,64},{48,80},{64,96},{80,112},{96,128},{112,144}... | collective-permute-start | bytes 786440 | tf_op jit(solution)/shard_map/ppermute | solution.py:215
  18.8 0.9 %copy-done.12 = bf16[2,4,1,128,128]{4,3,2,1,0:T(8,128)(2,1)S(1)} copy-done((bf16[2,4,1,128,128]{4,3,2,1,0:T(8,128)(2,1)S(1)}, bf16[2,4,1,128,128]{4,3,2,1,0:T(8,128)(2,1)}, u32[]{:S(2)}) %copy-start.12) | copy-done | bytes 262168
  19.7 0.9 %prepare.3 = (bf16[1024,512]{1,0:T(8,128)(2,1)S(1)}, bf16[128,512]{1,0:T(8,128)(2,1)S(1)}) custom-call(s32[2,8]{1,0:T(2,128)S(1)} %copy-done.16, f32[2,4,8]{2,1,0:T(4,128)S(1)} %copy-done.15, bf16[2,4,1,128,128]{4,3,2,1,0:T(8,128)(2,1)S(1)} %copy-done.12), custom_call_target="tpu_custom_call" | custom-call | bytes 1000000 | tf_op jit(solution)/shard_map/prepare/pallas_call | solution.py:41
  22.3 3.1 %collective-permute-start.7 = (bf16[4,256,128]{2,1,0:T(8,128)(2,1)S(1)}, bf16[4,256,128]{2,1,0:T(8,128)(2,1)S(1)}, u32[]{:S(2)}, u32[]{:S(2)}) collective-permute-start(bf16[4,256,128]{2,1,0:T(8,128)(2,1)S(1)} %copy-done), channel_id=1, source_target_pairs={{0,32},{16,48},{32,64},{48,80},{64,96},{80,112},{96,128},{112,144}... | collective-permute-start | bytes 786440 | tf_op jit(solution)/shard_map/ppermute | solution.py:215
  25.5 1.9 %collective-permute-start.8 = (bf16[4,256,128]{2,1,0:T(8,128)(2,1)S(1)}, bf16[4,256,128]{2,1,0:T(8,128)(2,1)S(1)}, u32[]{:S(2)}, u32[]{:S(2)}) collective-permute-start(bf16[4,256,128]{2,1,0:T(8,128)(2,1)S(1)} %broadcast_select_fusion.4), channel_id=1, source_target_pairs={{0,16},{16,0},{32,48},{48,32},{64,80},{80,64},{96,112},{112,96},{1... | collective-permute-start | bytes 786440 | tf_op jit(solution)/shard_map/ppermute | solution.py:251
  27.4 1.0 %broadcast_select_fusion = bf16[4,256,128]{2,1,0:T(8,128)(2,1)S(1)} fusion(bf16[4,256,128]{2,1,0:T(8,128)(2,1)} %broadcast_select_fusion.6, bf16[4,256,128]{2,1,0:T(8,128)(2,1)} %collective-permute-done.4.refs_3_, pred[]{:T(512)S(6)} %or.3), kind=kLoop, calls=%fused_computation.6 | loop fusion | flops 131072 | bytes 786433 | tf_op jit(solution)/shard_map/jit(_where)/select_n | solution.py:255
  28.4 1.9 %collective-permute-start.9 = (bf16[4,256,128]{2,1,0:T(8,128)(2,1)S(1)}, bf16[4,256,128]{2,1,0:T(8,128)(2,1)S(1)}, u32[]{:S(2)}, u32[]{:S(2)}) collective-permute-start(bf16[4,256,128]{2,1,0:T(8,128)(2,1)S(1)} %broadcast_select_fusion), channel_id=1, source_target_pairs={{1,2},{2,1},{3,4},{4,3},{5,6},{6,5},{7,24},{8,23},{9,10},{10,9},{1... | collective-permute-start | bytes 786440 | tf_op jit(solution)/shard_map/ppermute | solution.py:256
  31.0 6.0 %collective-permute-start.14 = (bf16[4,256,128]{2,1,0:T(8,128)(2,1)S(1)}, bf16[4,256,128]{2,1,0:T(8,128)(2,1)}, u32[]{:S(2)}, u32[]{:S(2)}) collective-permute-start(bf16[4,256,128]{2,1,0:T(8,128)(2,1)S(1)} %collective-permute-done.2.refs_1_.refs_3_.refs_4_), channel_id=1, source_target_pairs={{1,2},{2,1},{3,4},{4,3},{5,6},{6,5},{7,8},{8,7},{9,10},{10,9},{11,... | collective-permute-start | bytes 786440 | tf_op jit(solution)/shard_map/ppermute | solution.py:250
  40.1 1.9 %collective-permute-start.6 = (bf16[4,256,128]{2,1,0:T(8,128)(2,1)}, bf16[4,256,128]{2,1,0:T(8,128)(2,1)}, u32[]{:S(2)}, u32[]{:S(2)}) collective-permute-start(bf16[4,256,128]{2,1,0:T(8,128)(2,1)} %broadcast_select_fusion.3), channel_id=1, source_target_pairs={{0,16},{16,0},{32,48},{48,32},{64,80},{80,64},{96,112},{112,96},{1... | collective-permute-start | bytes 786440 | tf_op jit(solution)/shard_map/ppermute | solution.py:251
  42.7 3.3 %collective-permute-start.11 = (bf16[4,256,128]{2,1,0:T(8,128)(2,1)}, bf16[4,256,128]{2,1,0:T(8,128)(2,1)}, u32[]{:S(2)}, u32[]{:S(2)}) collective-permute-start(bf16[4,256,128]{2,1,0:T(8,128)(2,1)} %pad_maximum_fusion.3.refs_8_), channel_id=1, source_target_pairs={{0,32},{16,48},{32,64},{48,80},{64,96},{80,112},{96,128},{112,144}... | collective-permute-start | bytes 786440 | tf_op jit(solution)/shard_map/ppermute | solution.py:215
  46.0 0.9 %copy-done.3 = bf16[4,256,128]{2,1,0:T(8,128)(2,1)S(1)} copy-done((bf16[4,256,128]{2,1,0:T(8,128)(2,1)S(1)}, bf16[4,256,128]{2,1,0:T(8,128)(2,1)}, u32[]{:S(2)}) %copy-start.3) | copy-done | bytes 262168
  47.8 1.4 %far_part.3.refs_12_ = f32[4,128,256]{2,1,0:T(8,128)S(1)} custom-call(s32[1]{0:T(128)} %bitcast.odd_ref, bf16[4,256,128]{2,1,0:T(8,128)(2,1)S(1)} %collective-permute-done.refs_0_.refs_2_.refs_5_, bf16[4,256,128]{2,1,0:T(8,128)(2,1)S(1)} %collective-permute-done.2.refs_1_.refs_3_.refs_4_, ...), custom_call_target="tpu_custom_call" | custom-call | bytes 1000000 | tf_op jit(solution)/shard_map/far_part/pallas_call | solution.py:101
  50.2 2.5 %far_part.4.refs_11_ = f32[4,128,256]{2,1,0:T(8,128)S(1)} custom-call(s32[1]{0:T(128)} %bitcast.odd_ref, bf16[4,256,128]{2,1,0:T(8,128)(2,1)} %collective-permute-done.13.refs_0_.refs_7_, bf16[4,256,128]{2,1,0:T(8,128)(2,1)} %collective-permute-done.14.refs_1_.refs_6_, bf16[4,256,128]{2,1,0:T(8,128)(2,1)S(1)} %collective-permute-done.refs_0_.refs_2_.refs_5_, ...), custom_call_target="tpu_custom_call" | custom-call | bytes 1000000 | tf_op jit(solution)/shard_map/far_part/pallas_call | solution.py:101
  52.7 5.6 %near_part.3 = (bf16[1,24,128,128]{3,2,1,0:T(8,128)(2,1)}, bf16[1,24,128,128]{3,2,1,0:T(8,128)(2,1)}) custom-call(s32[1]{0:T(128)} %bitcast.odd_ref, bf16[4,256,128]{2,1,0:T(8,128)(2,1)} %collective-permute-done.12.refs_0_.refs_6_, bf16[4,256,128]{2,1,0:T(8,128)(2,1)S(1)} %copy-done.8, bf16[4,256,128]{2,1,0:T(8,128)(2,1)} %collective-permute-done.5.refs_2_.refs_4_, ...), custom_call_target="tpu_custom_call" | custom-call | bytes 1000000 | tf_op jit(solution)/shard_map/near_part/pallas_call | solution.py:162
  58.3 1.0 %broadcast_select_fusion.1 = bf16[4,256,128]{2,1,0:T(8,128)(2,1)S(1)} fusion(bf16[4,256,128]{2,1,0:T(8,128)(2,1)} %pad_maximum_fusion.3.refs_8_, bf16[4,256,128]{2,1,0:T(8,128)(2,1)} %collective-permute-done.11.refs_3_, pred[]{:T(512)S(6)} %eq.16), kind=kLoop, calls=%fused_computation.7 | loop fusion | flops 131072 | bytes 786433 | tf_op jit(solution)/shard_map/jit(_where)/select_n | solution.py:245
  59.3 1.6 %collective-permute-start.15 = (bf16[4,256,128]{2,1,0:T(8,128)(2,1)S(1)}, bf16[4,256,128]{2,1,0:T(8,128)(2,1)S(1)}, u32[]{:S(2)}, u32[]{:S(2)}) collective-permute-start(bf16[4,256,128]{2,1,0:T(8,128)(2,1)S(1)} %broadcast_select_fusion.1), channel_id=1, source_target_pairs={{0,16},{16,0},{32,48},{48,32},{64,80},{80,64},{96,112},{112,96},{1... | collective-permute-start | bytes 786440 | tf_op jit(solution)/shard_map/ppermute | solution.py:251
  60.9 6.3 %far_part.5 = (f32[4,128,256]{2,1,0:T(8,128)S(1)}, f32[4,128,256]{2,1,0:T(8,128)S(1)}, f32[4,128,256]{2,1,0:T(8,128)S(1)}, f32[4,128,256]{2,1,0:T(8,128)S(1)}) custom-call(s32[1]{0:T(128)} %bitcast.odd_ref, bf16[4,256,128]{2,1,0:T(8,128)(2,1)S(1)} %collective-permute-done.3.refs_2_.refs_4_.refs_0_, bf16[4,256,128]{2,1,0:T(8,128)(2,1)S(1)} %copy-done.3, ...), custom_call_target="tpu_custom_call" | custom-call | bytes 1000000 | tf_op jit(solution)/shard_map/far_part/pallas_call | solution.py:101
  67.2 3.5 %near_part.4 = (bf16[1,24,128,128]{3,2,1,0:T(8,128)(2,1)}, bf16[1,24,128,128]{3,2,1,0:T(8,128)(2,1)}) custom-call(s32[1]{0:T(128)} %bitcast.odd_ref, bf16[4,256,128]{2,1,0:T(8,128)(2,1)S(1)} %copy-done.10, bf16[4,256,128]{2,1,0:T(8,128)(2,1)} %collective-permute-done.6.refs_5_.refs_1_.refs_0_, ...), custom_call_target="tpu_custom_call", output_to_operand_aliasing={{0}: (8, {}), {1}: (9, {})} | custom-call | bytes 1000000 | tf_op jit(solution)/shard_map/near_part/pallas_call | solution.py:162
  70.7 7.3 %near_part.5 = (bf16[1,24,128,128]{3,2,1,0:T(8,128)(2,1)}, bf16[1,24,128,128]{3,2,1,0:T(8,128)(2,1)}) custom-call(s32[1]{0:T(128)} %bitcast.odd_ref, bf16[4,256,128]{2,1,0:T(8,128)(2,1)} %collective-permute-done.6.refs_5_.refs_1_.refs_0_, ...), custom_call_target="tpu_custom_call", output_to_operand_aliasing={{0}: (17, {}), {1}: (18, {})} | custom-call | bytes 1000000 | tf_op jit(solution)/shard_map/near_part/pallas_call | solution.py:162
  (74 shorter events, 15.3 us)
Async XLA Ops:
  0.6 3.3 %copy-start.17 = (bf16[1,24,128,128]{3,2,1,0:T(8,128)(2,1)S(1)}, bf16[1,24,128,128]{3,2,1,0:T(8,128)(2,1)}, u32[]{:S(2)}) copy-start(bf16[1,24,128,128]{3,2,1,0:T(8,128)(2,1)} %param.5) | copy-start | bytes 2359300
  1.9 2.7 %copy-start.18 = (bf16[1,24,128,128]{3,2,1,0:T(8,128)(2,1)S(1)}, bf16[1,24,128,128]{3,2,1,0:T(8,128)(2,1)}, u32[]{:S(2)}) copy-start(bf16[1,24,128,128]{3,2,1,0:T(8,128)(2,1)} %param.6) | copy-start | bytes 2359300
  2.0 9.3 %collective-permute-start.2 = (bf16[4,256,128]{2,1,0:T(8,128)(2,1)S(1)}, bf16[4,256,128]{2,1,0:T(8,128)(2,1)S(1)}, u32[]{:S(2)}, u32[]{:S(2)}) collective-permute-start(bf16[4,256,128]{2,1,0:T(8,128)(2,1)S(1)} %maximum_select_fusion.refs_7_.refs_9_), channel_id=1, source_target_pairs={{0,32},{16,48},{32,64},{48,80},{64,96},{80,112},{96,128},{112,144}... | collective-permute-start | bytes 786440 | tf_op jit(solution)/shard_map/ppermute | solution.py:208
  5.5 11.2 %collective-permute-start = (bf16[4,256,128]{2,1,0:T(8,128)(2,1)S(1)}, bf16[4,256,128]{2,1,0:T(8,128)(2,1)S(1)}, u32[]{:S(2)}, u32[]{:S(2)}) collective-permute-start(bf16[4,256,128]{2,1,0:T(8,128)(2,1)S(1)} %maximum_select_fusion.1.refs_6_.refs_10_), channel_id=1, source_target_pairs={{0,32},{16,48},{32,64},{48,80},{64,96},{80,112},{96,128},{112,144}... | collective-permute-start | bytes 786440 | tf_op jit(solution)/shard_map/ppermute | solution.py:215
  11.2 11.1 %collective-permute-start.3 = (bf16[4,256,128]{2,1,0:T(8,128)(2,1)}, bf16[4,256,128]{2,1,0:T(8,128)(2,1)S(1)}, u32[]{:S(2)}, u32[]{:S(2)}) collective-permute-start(bf16[4,256,128]{2,1,0:T(8,128)(2,1)} %pad_maximum_fusion.1.refs_8_), channel_id=1, source_target_pairs={{0,32},{16,48},{32,64},{48,80},{64,96},{80,112},{96,128},{112,144}... | collective-permute-start | bytes 786440 | tf_op jit(solution)/shard_map/ppermute | solution.py:215
  14.4 11.0 %collective-permute-start.4 = (bf16[4,256,128]{2,1,0:T(8,128)(2,1)}, bf16[4,256,128]{2,1,0:T(8,128)(2,1)}, u32[]{:S(2)}, u32[]{:S(2)}) collective-permute-start(bf16[4,256,128]{2,1,0:T(8,128)(2,1)} %broadcast_select_fusion.6), channel_id=1, source_target_pairs={{0,16},{16,0},{32,48},{48,32},{64,80},{80,64},{96,112},{112,96},{1... | collective-permute-start | bytes 786440 | tf_op jit(solution)/shard_map/ppermute | solution.py:251
  16.7 14.3 %collective-permute-start.1 = (bf16[4,256,128]{2,1,0:T(8,128)(2,1)}, bf16[4,256,128]{2,1,0:T(8,128)(2,1)S(1)}, u32[]{:S(2)}, u32[]{:S(2)}) collective-permute-start(bf16[4,256,128]{2,1,0:T(8,128)(2,1)} %pad_maximum_fusion.refs_3_), channel_id=1, source_target_pairs={{0,32},{16,48},{32,64},{48,80},{64,96},{80,112},{96,128},{112,144}... | collective-permute-start | bytes 786440 | tf_op jit(solution)/shard_map/ppermute | solution.py:215
  21.3 15.8 %collective-permute-start.5 = (bf16[4,256,128]{2,1,0:T(8,128)(2,1)S(1)}, bf16[4,256,128]{2,1,0:T(8,128)(2,1)}, u32[]{:S(2)}, u32[]{:S(2)}) collective-permute-start(bf16[4,256,128]{2,1,0:T(8,128)(2,1)S(1)} %broadcast_select_fusion.5), channel_id=1, source_target_pairs={{0,16},{16,0},{32,48},{48,32},{64,80},{80,64},{96,112},{112,96},{1... | collective-permute-start | bytes 786440 | tf_op jit(solution)/shard_map/ppermute | solution.py:251
  22.3 15.6 %collective-permute-start.7 = (bf16[4,256,128]{2,1,0:T(8,128)(2,1)S(1)}, bf16[4,256,128]{2,1,0:T(8,128)(2,1)S(1)}, u32[]{:S(2)}, u32[]{:S(2)}) collective-permute-start(bf16[4,256,128]{2,1,0:T(8,128)(2,1)S(1)} %copy-done), channel_id=1, source_target_pairs={{0,32},{16,48},{32,64},{48,80},{64,96},{80,112},{96,128},{112,144}... | collective-permute-start | bytes 786440 | tf_op jit(solution)/shard_map/ppermute | solution.py:215
  25.5 4.8 %copy-start.19 = (bf16[4,128,128]{2,1,0:T(8,128)(2,1)S(1)}, bf16[4,128,128]{2,1,0:T(8,128)(2,1)}, u32[]{:S(2)}) copy-start(bf16[4,128,128]{2,1,0:T(8,128)(2,1)} %get-tuple-element.68) | copy-start | bytes 393220
  25.5 4.8 %copy-start.20 = (bf16[4,128,128]{2,1,0:T(8,128)(2,1)S(1)}, bf16[4,128,128]{2,1,0:T(8,128)(2,1)}, u32[]{:S(2)}) copy-start(bf16[4,128,128]{2,1,0:T(8,128)(2,1)} %get-tuple-element.74) | copy-start | bytes 393220
  25.5 16.5 %collective-permute-start.8 = (bf16[4,256,128]{2,1,0:T(8,128)(2,1)S(1)}, bf16[4,256,128]{2,1,0:T(8,128)(2,1)S(1)}, u32[]{:S(2)}, u32[]{:S(2)}) collective-permute-start(bf16[4,256,128]{2,1,0:T(8,128)(2,1)S(1)} %broadcast_select_fusion.4), channel_id=1, source_target_pairs={{0,16},{16,0},{32,48},{48,32},{64,80},{80,64},{96,112},{112,96},{1... | collective-permute-start | bytes 786440 | tf_op jit(solution)/shard_map/ppermute | solution.py:251
  28.4 11.0 %collective-permute-start.9 = (bf16[4,256,128]{2,1,0:T(8,128)(2,1)S(1)}, bf16[4,256,128]{2,1,0:T(8,128)(2,1)S(1)}, u32[]{:S(2)}, u32[]{:S(2)}) collective-permute-start(bf16[4,256,128]{2,1,0:T(8,128)(2,1)S(1)} %broadcast_select_fusion), channel_id=1, source_target_pairs={{1,2},{2,1},{3,4},{4,3},{5,6},{6,5},{7,24},{8,23},{9,10},{10,9},{1... | collective-permute-start | bytes 786440 | tf_op jit(solution)/shard_map/ppermute | solution.py:256
  31.0 6.9 %copy-start.2 = (bf16[4,256,128]{2,1,0:T(8,128)(2,1)}, bf16[4,256,128]{2,1,0:T(8,128)(2,1)S(1)}, u32[]{:S(2)}) copy-start(bf16[4,256,128]{2,1,0:T(8,128)(2,1)S(1)} %collective-permute-done.1.refs_3_.refs_1_) | copy-start | bytes 786436
  31.0 18.4 %collective-permute-start.14 = (bf16[4,256,128]{2,1,0:T(8,128)(2,1)S(1)}, bf16[4,256,128]{2,1,0:T(8,128)(2,1)}, u32[]{:S(2)}, u32[]{:S(2)}) collective-permute-start(bf16[4,256,128]{2,1,0:T(8,128)(2,1)S(1)} %collective-permute-done.2.refs_1_.refs_3_.refs_4_), channel_id=1, source_target_pairs={{1,2},{2,1},{3,4},{4,3},{5,6},{6,5},{7,8},{8,7},{9,10},{10,9},{11,... | collective-permute-start | bytes 786440 | tf_op jit(solution)/shard_map/ppermute | solution.py:250
  37.1 12.7 %collective-permute-start.13 = (bf16[4,256,128]{2,1,0:T(8,128)(2,1)S(1)}, bf16[4,256,128]{2,1,0:T(8,128)(2,1)}, u32[]{:S(2)}, u32[]{:S(2)}) collective-permute-start(bf16[4,256,128]{2,1,0:T(8,128)(2,1)S(1)} %collective-permute-done.refs_0_.refs_2_.refs_5_), channel_id=1, source_target_pairs={{0,1},{1,0},{2,3},{3,2},{4,5},{5,4},{6,7},{7,6},{8,9},{9,8},{10,11... | collective-permute-start | bytes 786440 | tf_op jit(solution)/shard_map/ppermute | solution.py:253
  37.9 4.0 %copy-start.13 = (bf16[4,256,128]{2,1,0:T(8,128)(2,1)}, bf16[4,256,128]{2,1,0:T(8,128)(2,1)S(1)}, u32[]{:S(2)}) copy-start(bf16[4,256,128]{2,1,0:T(8,128)(2,1)S(1)} %collective-permute-done.7.refs_2_) | copy-start | bytes 786436
  37.9 14.7 %collective-permute-start.12 = (bf16[4,256,128]{2,1,0:T(8,128)(2,1)}, bf16[4,256,128]{2,1,0:T(8,128)(2,1)}, u32[]{:S(2)}, u32[]{:S(2)}) collective-permute-start(bf16[4,256,128]{2,1,0:T(8,128)(2,1)} %collective-permute-done.5.refs_2_.refs_4_), channel_id=1, source_target_pairs={{0,1},{1,0},{2,3},{3,2},{4,5},{5,4},{6,7},{7,6},{8,9},{9,8},{10,11... | collective-permute-start | bytes 786440 | tf_op jit(solution)/shard_map/ppermute | solution.py:260
  40.1 12.6 %collective-permute-start.6 = (bf16[4,256,128]{2,1,0:T(8,128)(2,1)}, bf16[4,256,128]{2,1,0:T(8,128)(2,1)}, u32[]{:S(2)}, u32[]{:S(2)}) collective-permute-start(bf16[4,256,128]{2,1,0:T(8,128)(2,1)} %broadcast_select_fusion.3), channel_id=1, source_target_pairs={{0,16},{16,0},{32,48},{48,32},{64,80},{80,64},{96,112},{112,96},{1... | collective-permute-start | bytes 786440 | tf_op jit(solution)/shard_map/ppermute | solution.py:251
  42.7 15.6 %collective-permute-start.11 = (bf16[4,256,128]{2,1,0:T(8,128)(2,1)}, bf16[4,256,128]{2,1,0:T(8,128)(2,1)}, u32[]{:S(2)}, u32[]{:S(2)}) collective-permute-start(bf16[4,256,128]{2,1,0:T(8,128)(2,1)} %pad_maximum_fusion.3.refs_8_), channel_id=1, source_target_pairs={{0,32},{16,48},{32,64},{48,80},{64,96},{80,112},{96,128},{112,144}... | collective-permute-start | bytes 786440 | tf_op jit(solution)/shard_map/ppermute | solution.py:215
  49.4 3.4 %copy-start.8 = (bf16[4,256,128]{2,1,0:T(8,128)(2,1)S(1)}, bf16[4,256,128]{2,1,0:T(8,128)(2,1)}, u32[]{:S(2)}) copy-start(bf16[4,256,128]{2,1,0:T(8,128)(2,1)} %copy-done.7) | copy-start | bytes 786436
  49.4 3.4 %copy-start.10 = (bf16[4,256,128]{2,1,0:T(8,128)(2,1)S(1)}, bf16[4,256,128]{2,1,0:T(8,128)(2,1)}, u32[]{:S(2)}) copy-start(bf16[4,256,128]{2,1,0:T(8,128)(2,1)} %copy-done.9) | copy-start | bytes 786436
  49.4 17.8 %collective-permute-start.10 = (bf16[4,256,128]{2,1,0:T(8,128)(2,1)S(1)}, bf16[4,256,128]{2,1,0:T(8,128)(2,1)S(1)}, u32[]{:S(2)}, u32[]{:S(2)}) collective-permute-start(bf16[4,256,128]{2,1,0:T(8,128)(2,1)S(1)} %broadcast_select_fusion.2), channel_id=1, source_target_pairs={{0,16},{16,0},{32,48},{48,32},{64,80},{80,64},{96,112},{112,96},{1... | collective-permute-start | bytes 786440 | tf_op jit(solution)/shard_map/ppermute | solution.py:251
  59.3 11.4 %collective-permute-start.15 = (bf16[4,256,128]{2,1,0:T(8,128)(2,1)S(1)}, bf16[4,256,128]{2,1,0:T(8,128)(2,1)S(1)}, u32[]{:S(2)}, u32[]{:S(2)}) collective-permute-start(bf16[4,256,128]{2,1,0:T(8,128)(2,1)S(1)} %broadcast_select_fusion.1), channel_id=1, source_target_pairs={{0,16},{16,0},{32,48},{48,32},{64,80},{80,64},{96,112},{112,96},{1... | collective-permute-start | bytes 786440 | tf_op jit(solution)/shard_map/ppermute | solution.py:251
  (13 other events, 13.8 us)
